TPU v7x, 32 devices: a whole 2x2x4 slice. The times are simulated.
32 devices in a mesh: loop: 4 (over y, x), dp: 8 (over z, core).
Axes of the slice: x: 2, y: 2, z: 4, core: 2. Of those that a mesh axis runs over, the one named last changes fastest.
Arguments:
- tokens: bfloat16 [1792, 8192], P('dp', 'loop'), may hold values from -8 to 8
- weight: bfloat16 [8192, 14336], P('loop', 'dp'), as said below
- rounding: float32 [8192, 14336], P('loop', 'dp'), may hold values from -6 to 6
- floor_codes: int32 [8192, 14336], P('loop', 'dp'), may hold values from -1 to 15
- scale_codes: int32 [14336], P('dp'), may hold values from 12 to 15
- zero_codes: int32 [14336], P('dp'), may hold values from 0 to 15
- block_mask: int32 [128, 224], P('loop', 'dp'), may hold values from 0 to 1, as said below
Outputs:
- refined: float32 [8192, 14336], P('loop', 'dp')
Inputs may be any that keep to these rules, and one draw needn't show every extreme that they name: weight equals scales times (floor_codes - zero_point + a fraction in [0, 1)), then is rounded to bfloat16. `block_mask`: the share of surviving blocks differs between column blocks.
All inputs are finite; a program needn't handle non-finite values.
Results may differ from a plain program's by a relative error of at most 0.019.
Values may be sent and summed in bfloat16 or wider, within the bound.
No kernel may reach another device: no remote copies, remote signals or barrier semaphores. Data moves between devices by JAX's collectives and lax.ppermute only.
A program may use at most 192 MiB of HBM per device.

v0:
```python
import jax
import jax.numpy as jnp
from jax import lax
from jax.sharding import PartitionSpec as P

BLOCK = 64
ITERS = 2


step_rate = 20.0
reg_weight = 0.05
base_scale = 0.02


def expand(block_mask):
    row_blocks, col_blocks = block_mask.shape
    spread = jnp.broadcast_to(block_mask[:, None, :, None], (row_blocks, BLOCK, col_blocks, BLOCK))
    return spread.reshape(row_blocks * BLOCK, col_blocks * BLOCK).astype(jnp.float32)


def token_product(token_rows, scaled_err):
    return lax.dot_general(
        token_rows, scaled_err, (((0,), (0,)), ((), ())), preferred_element_type=jnp.float32
    )


def per_device(tokens, weight, rounding, floor_codes, scale_codes, zero_codes, block_mask):
    gathered = lax.all_gather(tokens, "dp", axis=0, tiled=True)
    token_count = gathered.shape[0]
    scales = base_scale * jnp.exp2(scale_codes.astype(jnp.float32) * 0.25)
    zero_point = zero_codes.astype(jnp.float32)
    kept_mask = expand(block_mask)
    floors = floor_codes.astype(jnp.float32)
    in_range = ((floor_codes >= 0) & (floor_codes <= 14)).astype(jnp.float32)
    target = weight.astype(jnp.float32)
    for iteration in range(ITERS):
        relaxed = jax.nn.sigmoid(rounding)
        levels = jnp.clip(floors + relaxed, 0.0, 15.0)
        w_delta = (kept_mask * (scales[None, :] * (levels - zero_point[None, :]) - target)).astype(
            jnp.bfloat16
        )
        partial_sum = jnp.dot(gathered, w_delta, preferred_element_type=jnp.float32)
        residual = lax.psum(partial_sum.astype(jnp.bfloat16), "loop").astype(jnp.float32)
        scaled_err = (2.0 / token_count * residual).astype(jnp.bfloat16)
        gradient = token_product(gathered, scaled_err)
        centered = 2.0 * relaxed - 1.0
        descent = gradient * scales[None, :] * in_range - reg_weight * 8.0 * centered**3
        rounding = rounding - step_rate * kept_mask * descent * relaxed * (1.0 - relaxed)
    return rounding


def solution(mesh):
    placed = (
        P("dp", "loop"),
        P("loop", "dp"),
        P("loop", "dp"),
        P("loop", "dp"),
        P("dp"),
        P("dp"),
        P("loop", "dp"),
    )
    return jax.shard_map(
        per_device, mesh=mesh, in_specs=placed, out_specs=P("loop", "dp"), check_vma=False
    )
```

profile of v0, /device:TPU:0, one launch (start us, length us, event | category | flops | bytes accessed | tf_op | source)
XLA Modules:
  0.0 513.9 jit_solution(12518929168036352402)
XLA Ops:
  6.5 0.0 all-gather.2.cloned.1.call-start
  6.5 0.7 all-gather.2.cloned.1.call-update
  7.3 0.0 all-reduce.3.cloned.1.call-start
  7.3 0.7 convert_element_type.50
  8.0 0.1 copy.8
  8.1 14.7 %broadcast_in_dim.2 = f32[32,64,28,64]{1,0,3,2:T(8,128)} broadcast(f32[32,28]{0,1:T(8,128)S(1)} %copy.8), dimensions={0,2} | broadcast | bytes 14683648 | tf_op jit(solution)/shard_map/broadcast_in_dim | solution.py:17
  22.9 25.5 %convert_element_type.51 = f32[2048,1792]{0,1:T(8,128)} reshape(f32[32,64,28,64]{1,0,3,2:T(8,128)} %broadcast_in_dim.2) | data formatting | bytes 29360128 | tf_op jit(solution)/shard_map/convert_element_type | solution.py:18
  48.4 15.2 %copy.9 = s32[2048,1792]{0,1:T(8,128)} copy(s32[2048,1792]{1,0:T(8,128)} %param.10) | data formatting | bytes 29360128 | tf_op args[3]
  63.6 15.2 %copy.14 = f32[2048,1792]{0,1:T(8,128)} copy(f32[2048,1792]{1,0:T(8,128)} %param.9) | data formatting | bytes 29360128 | tf_op args[2]
  78.8 0.0 copy-start
  78.8 0.0 copy-start.1
  78.8 10.6 %copy.13 = bf16[2048,1792]{0,1:T(8,128)(2,1)} copy(bf16[2048,1792]{1,0:T(8,128)(2,1)} %param.8) | data formatting | bytes 14680064 | tf_op args[1]
  89.4 0.0 copy-done
  89.4 0.0 copy-done.1
  89.4 0.0 all-gather.2.cloned.1.call-done
  89.4 29.0 %fusion.18 = bf16[1792,1792]{0,1:T(8,128)(2,1)} fusion(bf16[1792,2048]{1,0:T(8,128)(2,1)} %all-gather.2.cloned.1.call-done, f32[2048,1792]{0,1:T(8,128)} %convert_element_type.51, bf16[2048,1792]{0,1:T(8,128)(2,1)} %copy.13, s32[2048,1792]{0,1:T(8,128)} %copy.9, f32[2048,1792]{0,1:T(8,128)} %copy.14, f32[1792]{0:T(1024)S(1)} %convert_element_type.54, ...), kind=kOutput, calls=%fused_computation.29 | convolution fusion | flops 13200588800 | bytes 65157120 | tf_op jit(solution)/shard_map/dot_general | solution.py:42
  118.5 0.0 all-reduce.3.cloned.1.call-update
  118.5 0.2 all-reduce.5.cloned.1.call-start
  118.7 8.3 %compare_and_fusion = pred[2048,1792]{0,1:T(32,128)(4,1)} fusion(s32[2048,1792]{0,1:T(8,128)} %copy.9), kind=kLoop, calls=%fused_computation.24 | loop fusion | flops 11010048 | bytes 18350080 | tf_op jit(solution)/shard_map/and | solution.py:34
  127.1 134.8 %all-reduce.3.cloned.1.call-done = bf16[1792,1792]{0,1:T(8,128)(2,1)} async-done(((bf16[1792,1792]{0,1:T(8,128)(2,1)}), bf16[1792,1792]{0,1:T(8,128)(2,1)}) %all-reduce.3.cloned.1.call-update) | async-done | bytes 6422544 | tf_op jit(solution)/shard_map/psum | solution.py:43
  261.9 30.7 %fusion.9 = f32[2048,1792]{0,1:T(8,128)} fusion(f32[2048,1792]{0,1:T(8,128)} %copy.14, pred[2048,1792]{0,1:T(32,128)(4,1)} %compare_and_fusion, f32[2048,1792]{0,1:T(8,128)} %convert_element_type.51, bf16[1792,2048]{1,0:T(8,128)(2,1)} %all-gather.2.cloned.1.call-done, f32[1792]{0:T(1024)S(1)} %exponential_multiply_fusion, ...), kind=kOutput, calls=%fused_computation.13 | convolution fusion | flops 13225361408 | bytes 61479936 | tf_op jit(solution)/shard_map/dot_general | solution.py:22
  292.5 29.1 %fusion.21 = bf16[1792,1792]{0,1:T(8,128)(2,1)} fusion(bf16[1792,2048]{1,0:T(8,128)(2,1)} %all-gather.2.cloned.1.call-done, f32[2048,1792]{0,1:T(8,128)} %convert_element_type.51, bf16[2048,1792]{0,1:T(8,128)(2,1)} %copy.13, s32[2048,1792]{0,1:T(8,128)} %copy.9, f32[2048,1792]{0,1:T(8,128)} %fusion.9, f32[1792]{0:T(1024)S(1)} %convert_element_type.54, ...), kind=kOutput, calls=%fused_computation.30 | convolution fusion | flops 13200588800 | bytes 65157120 | tf_op jit(solution)/shard_map/dot_general | solution.py:42
  321.6 0.0 all-reduce.5.cloned.1.call-update
  321.6 140.8 %all-reduce.5.cloned.1.call-done = bf16[1792,1792]{0,1:T(8,128)(2,1)} async-done(((bf16[1792,1792]{0,1:T(8,128)(2,1)}), bf16[1792,1792]{0,1:T(8,128)(2,1)}) %all-reduce.5.cloned.1.call-update) | async-done | bytes 6422544 | tf_op jit(solution)/shard_map/psum | solution.py:43
  462.4 30.7 %fusion.15 = f32[2048,1792]{0,1:T(8,128)} fusion(f32[2048,1792]{0,1:T(8,128)} %fusion.9, pred[2048,1792]{0,1:T(32,128)(4,1)} %compare_and_fusion, f32[2048,1792]{0,1:T(8,128)} %convert_element_type.51, bf16[1792,2048]{1,0:T(8,128)(2,1)} %all-gather.2.cloned.1.call-done, f32[1792]{0:T(1024)S(1)} %exponential_multiply_fusion, ...), kind=kOutput, calls=%fused_computation.19 | convolution fusion | flops 13225361408 | bytes 61479936 | tf_op jit(solution)/shard_map/dot_general | solution.py:22
  493.1 14.3 %copy.15 = f32[2048,1792]{1,0:T(8,128)} copy(f32[2048,1792]{0,1:T(8,128)} %fusion.15) | data formatting | bytes 29360128 | tf_op jit(solution)/shard_map/sub | solution.py:48
  (2 shorter events, 0.0 us)
Async XLA Ops:
  6.5 82.9 %all-gather.2.cloned.1.call-start = ((), (), s32[]{:S(2)}) async-start(), calls=%async_computation | async-start | bytes 8257536 | tf_op jit(solution)/shard_map/all_gather | solution.py:28
  7.3 254.6 %all-reduce.3.cloned.1.call-start = ((), (), s32[]{:S(2)}) async-start(), calls=%async_computation.1 | async-start | bytes 12845056 | tf_op jit(solution)/shard_map/psum | solution.py:43
  78.8 10.6 %copy-start = (s32[1792]{0:T(1024)S(1)}, s32[1792]{0:T(1024)}, u32[]{:S(2)}) copy-start(s32[1792]{0:T(1024)} %param.12) | copy-start | bytes 21508
  78.8 10.6 %copy-start.1 = (s32[1792]{0:T(1024)S(1)}, s32[1792]{0:T(1024)}, u32[]{:S(2)}) copy-start(s32[1792]{0:T(1024)} %param.11) | copy-start | bytes 21508
  118.5 343.9 %all-reduce.5.cloned.1.call-start = ((), (), s32[]{:S(2)}) async-start(), calls=%async_computation.2 | async-start | bytes 12845056 | tf_op jit(solution)/shard_map/psum | solution.py:43
Sparse Core Ops, SparseCore 0:
  9.0 76.0 all-gather.1
  118.6 143.1 all-reduce.2
  321.7 140.5 all-reduce.4
where the time goes:
time: 516 us; the launch traced here: 514 us
  waiting for transfers between devices  276 us (53%)
  matrix products  120 us (23%)
  local copies, waits for them, and re-layouts  95.6 us (19%)
  between operations  13.1 us (3%)
  other arithmetic  9.05 us (2%)
    psum x2, waiting for transfers between devices, per_device(): lax.psum(partial_sum.astype(jnp.bfloat16), 'loop').astype(jnp.float32)  276 us
    dot_general x2, matrix products, token_product(): lax.dot_general(token_rows, scaled_err, (((0,), (0,)), ((), ())), preferr...  61.4 us
    dot_general x2, matrix products, per_device(): partial_sum = jnp.dot(gathered, w_delta, preferred_element_type=jnp.float32)  58.1 us
    unnamed x7, local copies, waits for them, and re-layouts  41 us
    convert_element_type x2, local copies, waits for them, and re-layouts, expand(): spread.reshape(row_blocks * BLOCK, col_blocks * BLOCK).astype(jnp.float32)  25.6 us
    broadcast_in_dim x1, local copies, waits for them, and re-layouts, expand(): jnp.broadcast_to(block_mask[:, None, :, None], (row_blocks, BLOCK, col_bl...  14.7 us
    sub x1, local copies, waits for them, and re-layouts, per_device(): rounding - step_rate * kept_mask * descent * relaxed * (1.0 - relaxed)  14.3 us
  transfers between devices with their start and end apart: 3, of which 2 were waited for; matrix products, arithmetic and copies ran while one was open for 18% of the time, Pallas kernels for 0%

commit v1 on v0

--- a/solution.py
+++ b/solution.py
@@ -1,15 +1,24 @@
 import jax
 import jax.numpy as jnp
 from jax import lax
+from jax.experimental import pallas as pl
+from jax.experimental.pallas import tpu as pltpu
 from jax.sharding import PartitionSpec as P
 
 BLOCK = 64
 ITERS = 2
+TILE = 256
+STRIP = 16
+ROWS = 512
+VMEM_LIMIT = 24 * 1024 * 1024
 
 
 step_rate = 20.0
 reg_weight = 0.05
 base_scale = 0.02
+
+f32 = jnp.float32
+bf16 = jnp.bfloat16
 
 
 def expand(block_mask):
@@ -24,7 +33,7 @@
     )
 
 
-def per_device(tokens, weight, rounding, floor_codes, scale_codes, zero_codes, block_mask):
+def plain(tokens, weight, rounding, floor_codes, scale_codes, zero_codes, block_mask):
     gathered = lax.all_gather(tokens, "dp", axis=0, tiled=True)
     token_count = gathered.shape[0]
     scales = base_scale * jnp.exp2(scale_codes.astype(jnp.float32) * 0.25)
@@ -49,6 +58,407 @@
     return rounding
 
 
+KERNEL_FLOPS = 40_000_000_000
+VMEM = pl.BlockSpec(memory_space=pltpu.VMEM)
+ANY = pl.BlockSpec(memory_space=pl.ANY)
+HBM = pl.BlockSpec(memory_space=pltpu.HBM)
+SMEM = pl.BlockSpec(memory_space=pltpu.SMEM)
+
+
+class Chain:
+    def __init__(self):
+        self.last = None
+
+    def call(self, kernel, name, operands, in_specs, out_specs, out_shape, flops, moved, grid=(), scratch=(), aliases=None, late_hbm=False):
+        count = len(operands)
+        late = [] if self.last is None or late_hbm else [self.last]
+
+        def wrapped(*refs):
+            return kernel(*refs[:count], *refs[count + len(late):])
+
+        out = pl.pallas_call(
+            wrapped,
+            grid=grid,
+            in_specs=list(in_specs) + [ANY] * len(late),
+            out_specs=out_specs,
+            out_shape=out_shape,
+            scratch_shapes=list(scratch),
+            input_output_aliases=aliases or {},
+            compiler_params=pltpu.CompilerParams(vmem_limit_bytes=VMEM_LIMIT),
+            cost_estimate=pl.CostEstimate(flops=KERNEL_FLOPS, bytes_accessed=1024, transcendentals=0),
+            name=name,
+        )(*operands, *late)
+        self.last = pltpu.with_memory_space_constraint(out[0], pltpu.HBM) if late_hbm else out[-1]
+        return out
+
+
+def delta_rows(half_tanh, floors, weight, scales, zeros, kept):
+    levels = jnp.clip(floors + (0.5 + 0.5 * half_tanh), 0.0, 15.0)
+    return (kept * (scales * (levels - zeros) - weight)).astype(bf16)
+
+
+def update_rows(grad, t, v, code, scales, kept):
+    square = t * t
+    pull = jnp.where((code >= 0) & (code <= 14), grad * scales, 0.0)
+    descent = pull - (8.0 * reg_weight) * (t * square)
+    return v - ((0.25 * step_rate) * kept) * (1.0 - square) * descent
+
+
+def by_rows(rows, body):
+    def block(i, carry):
+        for j in range(BLOCK // STRIP):
+            body(pl.multiple_of(i * BLOCK + j * STRIP, STRIP), i)
+        return carry
+
+    lax.fori_loop(0, rows // BLOCK, block, 0)
+
+
+def steps_of(codes):
+    return base_scale * jnp.exp2(codes.astype(f32) * 0.25)
+
+
+def first_delta(chain, col, cols, weight, rounding, floors, scale_codes, zeros, kept):
+    d = weight.shape[0]
+    wide = 512 if cols % 512 == 0 and col % 512 == 0 else TILE
+    rows = min(d, 512 * 512 // wide)
+    first = col // wide
+
+    def kernel(s_ref, zp_ref, m, v, fl, w, out):
+        def tile(v_t, fl_t, w_t):
+            j, i = pl.program_id(0), pl.program_id(1)
+            lanes = pl.ds(pl.multiple_of(j * wide, wide), wide)
+            there = pl.ds(pl.multiple_of((first + j) * wide, wide), wide)
+            s, zp = steps_of(s_ref[:, there]), zp_ref[:, there].astype(f32)
+
+            def strip(start, b):
+                at = pl.ds(start, STRIP)
+                t = jnp.tanh(0.5 * v_t[at, :])
+                mask = m[i * (rows // BLOCK) + b, :, there]
+                out[pl.ds(pl.multiple_of(i * rows + start, STRIP), STRIP), lanes] = delta_rows(
+                    t, fl_t[at, :].astype(f32), w_t[at, :].astype(f32), s, zp, mask)
+
+            by_rows(rows, strip)
+
+        spec = pl.BlockSpec((rows, wide), lambda j, i: (i, j + first))
+        pltpu.emit_pipeline(tile, grid=(cols // wide, d // rows), in_specs=[spec] * 3)(v, fl, w)
+
+    return chain.call(
+        kernel, "delta", [scale_codes, zeros, kept, rounding, floors, weight],
+        [VMEM] * 3 + [HBM] * 3, [VMEM], [jax.ShapeDtypeStruct((d, cols), bf16)], 20 * d * cols, 12 * d * cols,
+    )[0]
+
+
+def split_rows(part, bit, send, keep, at, cols):
+    half = part.shape[0] // 2
+    low, high = part[:half, :], part[half:, :]
+    first = bit == 0
+    keep[pl.ds(at, half), cols] = jnp.where(first, low, high).astype(bf16)
+    send[pl.ds(at, half), cols] = jnp.where(first, high, low).astype(bf16)
+
+
+def column_tiles(cols):
+    return [(at, min(512, cols - at)) for at in range(0, cols, 512)]
+
+
+def forward(chain, place, x, first, chunks, rows, deltas):
+    d = x.shape[1]
+    total = sum(a.shape[1] for a in deltas)
+
+    def kernel(place_ref, x_ref, *refs):
+        ws, (send, keep) = refs[:-2], refs[-2:]
+        base = 0
+        for w in ws:
+            for at, cols in column_tiles(w.shape[1]):
+                for i in range(chunks):
+                    part = jnp.dot(x_ref[first + i * rows:first + (i + 1) * rows, :], w[:, at:at + cols], preferred_element_type=f32)
+                    split_rows(part, place_ref[0], send, keep, i * (rows // 2), pl.ds(base + at, cols))
+            base += w.shape[1]
+
+    shape = jax.ShapeDtypeStruct((chunks * rows // 2, total), bf16)
+    return chain.call(
+        kernel, "forward", [place, x, *deltas], [SMEM] + [VMEM] * (1 + len(deltas)), [VMEM] * 2, [shape] * 2,
+        2 * chunks * rows * d * total, 2 * d * (chunks * rows + total) // 4,
+    )
+
+
+def add(chain, a, b, scale=None):
+    rows, cols = a.shape
+    step = 32
+
+    def kernel(a_ref, b_ref, out):
+        def strip(i, carry):
+            at = pl.ds(pl.multiple_of(i * step, step), step)
+            total = a_ref[at, :].astype(f32) + b_ref[at, :].astype(f32)
+            out[at, :] = (total if scale is None else scale * total).astype(bf16)
+            return carry
+
+        lax.fori_loop(0, rows // step, strip, 0)
+
+    return chain.call(
+        kernel, "pair" if scale is None else "err", [a, b], [VMEM] * 2, [VMEM],
+        [jax.ShapeDtypeStruct(a.shape, bf16)], rows * cols, 6 * rows * cols,
+    )[0]
+
+
+def gate(chain, a):
+    return chain.call(
+        lambda a_ref, out: None, "gate", [a], [ANY], [ANY], [jax.ShapeDtypeStruct(a.shape, a.dtype)], 1, 1, aliases={0: 0}
+    )[0]
+
+
+def choose(chain, place, pieces, candidates, choices, name):
+    arrays = pieces + candidates
+    rows = [a.shape[0] for a in pieces] + [candidates[0].shape[0]] * len(choices) if candidates else [a.shape[0] for a in pieces]
+    starts = [sum(rows[:i]) for i in range(len(rows))]
+    width = arrays[0].shape[1]
+
+    def kernel(place_ref, *refs):
+        ins, (out, sems) = refs[:len(arrays)], refs[len(arrays):]
+
+        def copy(ref, i):
+            return pltpu.make_async_copy(ref, out.at[pl.ds(starts[i], rows[i]), :], sems.at[i])
+
+        for i in range(len(pieces)):
+            copy(ins[i], i).start()
+        for z in range(4 if choices else 0):
+            for core in range(2):
+                @pl.when((place_ref[1] == z) & (place_ref[2] == core))
+                def _(z=z, core=core):
+                    picked = [copy(ins[len(pieces) + choice(z, core)], len(pieces) + i) for i, choice in enumerate(choices)]
+                    for one in picked:
+                        one.start()
+                    for one in picked:
+                        one.wait()
+        for i in range(len(pieces)):
+            copy(ins[i], i).wait()
+
+    return chain.call(
+        kernel, name, [place, *arrays], [SMEM] + [VMEM] * len(pieces) + [ANY] * len(candidates), [VMEM], [jax.ShapeDtypeStruct((sum(rows), width), bf16)],
+        1, 4 * sum(rows) * width, scratch=[pltpu.SemaphoreType.DMA((len(rows),))],
+    )[0]
+
+
+def join(chain, place, mine, got, rows):
+    half = rows // 2
+    count = mine.shape[0] // half
+    cols = mine.shape[1]
+
+    def kernel(place_ref, mine_ref, got_ref, out):
+        bit = place_ref[0]
+        for i in range(count):
+            def strip(k, carry):
+                at = i * half + k * 32
+                to = i * rows + k * 32
+                out[pl.ds(pl.multiple_of(to + bit * half, 32), 32), :] = mine_ref[pl.ds(pl.multiple_of(at, 32), 32), :]
+                out[pl.ds(pl.multiple_of(to + (1 - bit) * half, 32), 32), :] = got_ref[pl.ds(pl.multiple_of(at, 32), 32), :]
+                return carry
+
+            lax.fori_loop(0, half // 32, strip, 0)
+
+    return chain.call(
+        kernel, "join", [place, mine, got], [SMEM, VMEM, VMEM], [VMEM],
+        [jax.ShapeDtypeStruct((count * rows, cols), bf16)], rows * cols, 6 * rows * cols,
+    )[0]
+
+
+def backward(chain, place, errs, starts, x_full, weight, rounding, v_col, floors, scales, zeros, kept, col, cols, out_prev, last):
+    tokens, d = x_full.shape
+    rows = tokens // 4
+    n_err = len(errs)
+    here = col // cols
+    lanes = pl.ds(col, cols)
+
+    def kernel(place_ref, *refs):
+        e_refs, rest = refs[:n_err], list(refs[n_err:])
+        x, s, zp, m, v, fl = rest[:6]
+        rest = rest[6:]
+        if last:
+            if out_prev is not None:
+                rest = rest[1:]
+            out, err, grad = rest
+            streams = [v, fl]
+        else:
+            w, out, send, keep, err, grad, delta = rest
+            streams = [v, fl, w]
+        if len(errs) == 1:
+            (err,) = e_refs
+        else:
+            base = 0
+            for ref, at in zip(e_refs, starts):
+                err[base:base + ref.shape[0], :] = ref[:, at:at + cols]
+                base += ref.shape[0]
+
+        def tile(*tiles):
+            v_t, fl_t, out_t = tiles[0], tiles[1], tiles[-1]
+            g = pl.program_id(0)
+            features = pl.ds(pl.multiple_of(g * ROWS, ROWS), ROWS)
+            scales, zero = steps_of(s[:, lanes]), None if last else zp[:, lanes].astype(f32)
+            grad[...] = lax.dot_general(x[:, features], err[...], (((0,), (0,)), ((), ())), preferred_element_type=f32)
+
+            def strip(start, i):
+                at = pl.ds(start, STRIP)
+                code = fl_t[at, :]
+                old = v_t[at, :]
+                mask = m[g * (ROWS // BLOCK) + i, :, lanes]
+                new = update_rows(grad[at, :], jnp.tanh(0.5 * old), old, code, scales, mask)
+                out_t[at, :] = new
+                if not last:
+                    to = pl.ds(pl.multiple_of(g * ROWS + start, STRIP), STRIP)
+                    delta[to, :] = delta_rows(jnp.tanh(0.5 * new), code.astype(f32), tiles[2][at, :].astype(f32), scales, zero, mask)
+
+            by_rows(ROWS, strip)
+
+        def spec(c):
+            return pl.BlockSpec((ROWS, cols), lambda g: (g, c))
+
+        pltpu.emit_pipeline(
+            tile, grid=(d // ROWS,),
+            in_specs=[spec(v_col // cols)] + [spec(here)] * (len(streams) - 1),
+            out_specs=[spec(here if last else 0)],
+        )(*streams, out)
+
+        if not last:
+            def two(c, carry):
+                part = jnp.dot(x[pl.ds(pl.multiple_of(c * 2 * rows, 16), 2 * rows), :], delta[...], preferred_element_type=f32)
+                at = pl.multiple_of(c * rows, 16)
+                split_rows(part[:rows, :], place_ref[0], send, keep, at, slice(None))
+                split_rows(part[rows:, :], place_ref[0], send, keep, at + rows // 2, slice(None))
+                return carry
+
+            lax.fori_loop(0, 2, two, 0)
+
+    operands = [place, *errs, x_full, scales, zeros, kept, rounding, floors]
+    in_specs = [SMEM] + [VMEM] * (n_err + 4) + [HBM] * 2
+    scratch = [pltpu.VMEM((tokens, cols), bf16), pltpu.VMEM((ROWS, cols), f32)]
+    aliases = {}
+    if last:
+        if out_prev is not None:
+            aliases = {len(operands): 0}
+            operands.append(out_prev)
+            in_specs.append(HBM)
+        out_specs = [HBM]
+        out_shape = [pltpu.HBM(floors.shape, f32)]
+    else:
+        operands.append(weight)
+        in_specs.append(HBM)
+        out_specs = [HBM, VMEM, VMEM]
+        out_shape = [pltpu.HBM((d, cols), f32)] + [jax.ShapeDtypeStruct((tokens // 2, cols), bf16)] * 2
+        scratch.append(pltpu.VMEM((d, cols), bf16))
+    return chain.call(
+        kernel, "backward_last" if last else "backward_forward", operands, in_specs, out_specs, out_shape,
+        (2 if last else 4) * tokens * d * cols, 16 * d * cols, scratch=scratch, aliases=aliases, late_hbm=last,
+    )
+
+
+def swap_loop(a, core0, core1, n):
+    pairs = [(i * n + j, (i ^ (core1 if j % 2 else core0)) * n + j) for i in range(4) for j in range(n)]
+    return lax.ppermute(a, ("loop", "dp"), pairs)
+
+
+def swap_core(a, n):
+    return lax.ppermute(a, "dp", [(i, i ^ 1) for i in range(n)])
+
+
+def spread(a, step, n):
+    pairs = []
+    for z in range(n // 2):
+        if z - step >= 0 and z + 1 < n // 2:
+            pairs.append((2 * z, 2 * z + 2))
+        if z + step < n // 2 and z - 1 >= 0:
+            pairs.append((2 * z + 1, 2 * z - 1))
+    return lax.ppermute(a, "dp", pairs)
+
+
+ORDER = [
+    "D0", "D1", "K0", "Fo0", "Fo1", "D2", "Po0", "Po1", "Fo2", "Eo0", "G1", "Eo1", "Po2", "Ro0", "K1", "Fn",
+    "Ro1", "Eo2", "G2", "Pn", "Ro2", "K2", "Fm", "En", "G3", "Pm", "K3", "Ff0", "Rn", "Ff1", "Ff2", "Em",
+    "Pf0", "Pf1", "Pf2", "Rm", "Ef0", "Ef1", "Ef2", "Rf0", "B0", "Rf1", "Rf2", "B1", "Ps0", "B2", "Ps1", "B3",
+    "Es0", "Ps2", "Es1", "Ps3", "Rs0", "L0", "Es2", "Rs1", "L1", "Es3", "Rs2", "L2", "Rs3", "L3",
+]
+
+
+def piped(tokens, weight, rounding, floor_codes, scale_codes, zero_codes, block_mask):
+    n = 8
+    rows = 2 * tokens.shape[0]
+    scale = 2.0 / (tokens.shape[0] * n)
+    width = weight.shape[1]
+    loop_at, dp_at = lax.axis_index("loop"), lax.axis_index("dp")
+    core, z = dp_at % 2, dp_at // 2
+    place = jnp.stack([jnp.where(core == 0, loop_at % 2, loop_at // 2), z, core]).astype(jnp.int32)
+    scales, zeros = scale_codes[None, :], zero_codes[None, :]
+    weight, rounding, floor_codes = (pltpu.with_memory_space_constraint(a, pltpu.HBM) for a in (weight, rounding, floor_codes))
+    kept = jnp.repeat(block_mask.astype(f32), BLOCK, axis=1)[:, None, :]
+    chain = Chain()
+
+    blocks = [(0, 512), (512, 512), (1024, width - 1024)]
+    groups = [(0, 512), (512, 512), (1024, 512), (1536, width - 1536)]
+    other = swap_core(tokens, n)
+    came, passed = {}, {}
+    chunk, deltas, sent, kept_part, pairs, errs, second, out = {}, {}, {}, {}, {}, {}, {}, [None]
+
+    def above(step):
+        return lambda core: step - 1 if core == 1 else 3 + step - 1
+
+    def below(step):
+        return lambda core: step - 1 if core == 0 else 3 + step - 1
+
+    near_of = [above(1), above(1), below(1), below(1)]
+    mid_of = [above(2), below(1), above(1), below(2)]
+    far_of = [above(3), above(2), below(2), below(3)]
+
+    def home(col):
+        i = max(i for i, (start, _) in enumerate(blocks) if start <= col)
+        return i, col - blocks[i][0]
+
+    for step in ORDER:
+        kind, arg = step[0], step[1:]
+        if kind == "K":
+            if arg == "0":
+                chunk["o"] = choose(chain, place, [tokens, other], [], [], "own")
+                came[1] = spread(chunk["o"], 0, n)
+            elif arg == "1":
+                near = [lambda z, core: 0 if near_of[z](core) == 0 else 1]
+                chunk["n"] = choose(chain, place, [], [came[1], passed[1]], near, "near")
+            elif arg == "2":
+                chunk["m"] = choose(chain, place, [], [came[1], came[2], passed[1], passed[2]],
+                                    [lambda z, core: {0: 0, 1: 1, 3: 2, 4: 3}[mid_of[z](core)]], "mid")
+            else:
+                chunk["f"] = choose(chain, place, [chunk["o"], chunk["n"], chunk["m"]], [came[2], came[3], passed[2], passed[3]],
+                                    [lambda z, core: {1: 0, 2: 1, 4: 2, 5: 3}[far_of[z](core)]], "all_tokens")
+        elif kind == "G":
+            i = int(arg)
+            came[i] = gate(chain, came[i])
+            passed[i] = swap_core(came[i], n)
+            if i < 3:
+                came[i + 1] = spread(came[i], i, n)
+        elif kind == "D":
+            i = int(arg)
+            deltas[i] = first_delta(chain, *blocks[i], weight, rounding, floor_codes, scales, zeros, kept)
+        elif kind == "F":
+            ws = [deltas[int(arg[1])]] if len(arg) > 1 else [deltas[i] for i in range(len(blocks))]
+            first, count = (3 * rows, 1) if arg[0] == "f" else (0, 1)
+            sent[arg], kept_part[arg] = forward(chain, place, chunk[arg[0]], first, count, rows, ws)
+        elif kind == "P":
+            pairs[arg] = add(chain, kept_part[arg], swap_loop(sent[arg], 1, 2, n))
+        elif kind == "E":
+            mine = add(chain, pairs[arg], swap_loop(pairs[arg], 2, 1, n), scale)
+            errs[arg] = (mine, swap_loop(mine, 1, 2, n))
+        elif kind == "R":
+            errs[arg] = join(chain, place, *errs[arg], rows)
+        elif kind == "B":
+            col, cols = groups[int(arg)]
+            i, inner = home(col)
+            second[arg], sent["s" + arg], kept_part["s" + arg] = backward(
+                chain, place, [errs["o%d" % i], errs["n"], errs["m"], errs["f%d" % i]], [inner, col, col, inner],
+                chunk["f"], weight, rounding, col, floor_codes, scales, zeros, kept, col, cols, None, False)
+        elif kind == "L":
+            col, cols = groups[int(arg)]
+            (out[0],) = backward(
+                chain, place, [errs["s" + arg]], [0],
+                chunk["f"], weight, second[arg], 0, floor_codes, scales, zeros, kept, col, cols, out[0], True)
+    return out[0]
+
+
 def solution(mesh):
     placed = (
         P("dp", "loop"),
@@ -59,6 +469,7 @@
         P("dp"),
         P("loop", "dp"),
     )
+    per_device = piped if (mesh.shape["loop"], mesh.shape["dp"]) == (4, 8) else plain
     return jax.shard_map(
         per_device, mesh=mesh, in_specs=placed, out_specs=P("loop", "dp"), check_vma=False
     )

time: 516 us -> 326 us (0.63)
  waiting for transfers between devices: 276 us -> 92.1 us
  Pallas kernels: 0 us -> 173 us
  matrix products: 120 us -> 0 us
  local copies, waits for them, and re-layouts: 95.6 us -> 14.6 us
  starting transfers between devices: 0.26 us -> 43.6 us
  between operations: 13.1 us -> 0.86 us
  other arithmetic: 9.05 us -> 0.8 us
    psum x2 -> x0, waiting for transfers between devices: 276 us -> none  [per_device(): lax.psum(partial_sum.astype(jnp.bfloat16), 'loop').astype(jnp.float32)]
    pallas_call x0 -> x62, Pallas kernels: none -> 173 us  [call(): pl.pallas_call(wrapped, grid=grid, in_specs=list(in_specs) + [ANY] * len(...]
    dot_general x4 -> x0, matrix products: 120 us -> none  [the longest x2 61.4 us: token_product(): lax.dot_general(token_rows, scaled_err, (((0,), (0,)), ((), ())), preferr...]
    ppermute x0 -> x43, waiting for transfers between devices: none -> 92.1 us  [the longest x36 92 us: swap_loop(): return lax.ppermute(a, ('loop', 'dp'), pairs)]
    ppermute x0 -> x43, starting transfers between devices: none -> 43.6 us  [the longest x36 31 us: swap_loop(): return lax.ppermute(a, ('loop', 'dp'), pairs)]
    unnamed x7 -> x76, local copies, waits for them, and re-layouts: 41 us -> 12.7 us
    convert_element_type x2 -> x0, local copies, waits for them, and re-layouts: 25.6 us -> none  [expand(): spread.reshape(row_blocks * BLOCK, col_blocks * BLOCK).astype(jnp.float32)]
    sub x1 -> x0, local copies, waits for them, and re-layouts: 14.3 us -> none  [per_device(): rounding - step_rate * kept_mask * descent * relaxed * (1.0 - relaxed)]
  transfers between devices with their start and end apart: 3 -> 43, of which waited for: 2 -> 16; matrix products, arithmetic and copies ran while one was open for 18% -> 1% of each run, Pallas kernels for 0% -> 49%
where the time goes in v1:
time: 326 us; the launch traced here: 325 us
  Pallas kernels  173 us (53%)
  waiting for transfers between devices  92.1 us (28%)
  starting transfers between devices  43.6 us (13%)
  local copies, waits for them, and re-layouts  14.6 us (4%)
    pallas_call x62, Pallas kernels, call(): pl.pallas_call(wrapped, grid=grid, in_specs=list(in_specs) + [ANY] * len(...  173 us
    ppermute x36, waiting for transfers between devices, swap_loop(): return lax.ppermute(a, ('loop', 'dp'), pairs)  92 us
    ppermute x36, starting transfers between devices, swap_loop(): return lax.ppermute(a, ('loop', 'dp'), pairs)  31 us
    unnamed x76, local copies, waits for them, and re-layouts  12.7 us
    ppermute x3, starting transfers between devices, spread(): return lax.ppermute(a, 'dp', pairs)  9.49 us
  transfers between devices with their start and end apart: 43, of which 16 were waited for; matrix products, arithmetic and copies ran while one was open for 1% of the time, Pallas kernels for 49%

profile of v1, /device:TPU:0, one launch (start us, length us, event | category | flops | bytes accessed | tf_op | source)
XLA Modules:
  0.0 325.2 jit_solution(16370489001155187825)
XLA Ops:
  3.1 5.5 %delta.3.refs_6_.refs_2_ = bf16[2048,512]{1,0:T(8,128)(2,1)S(1)} custom-call(s32[1,1792]{1,0:T(1,128)S(1)} %broadcast_in_dim.9.refs_0_.refs_6_.refs_3_, s32[1,1792]{1,0:T(1,128)S(1)} %broadcast_in_dim.10.refs_1_.refs_7_.refs_4_, f32[32,1,1792]{2,1,0:T(1,128)S(1)} %broadcast_in_dim_reshape.4.refs_2_.refs_8_.refs_5_, f32[2048,1792]{1,0:T(8,128)} %refs_9_.7, ...), custom_call_target="tpu_custom_call" | custom-call | flops 40000000000 | bytes 1024 | tf_op jit(solution)/shard_map/delta/pallas_call | solution.py:79
  8.6 6.3 %delta.4.refs_3_.refs_2_ = bf16[2048,512]{1,0:T(8,128)(2,1)S(1)} custom-call(s32[1,1792]{1,0:T(1,128)S(1)} %broadcast_in_dim.9.refs_0_.refs_6_.refs_3_, s32[1,1792]{1,0:T(1,128)S(1)} %broadcast_in_dim.10.refs_1_.refs_7_.refs_4_, f32[32,1,1792]{2,1,0:T(1,128)S(1)} %broadcast_in_dim_reshape.4.refs_2_.refs_8_.refs_5_, f32[2048,1792]{1,0:T(8,128)} %refs_9_.7, ...), custom_call_target="tpu_custom_call" | custom-call | flops 40000000000 | bytes 1024 | tf_op jit(solution)/shard_map/delta/pallas_call | solution.py:79
  18.0 2.3 own.1.refs_1_.refs_3_
  20.3 2.8 forward.8
  23.1 5.7 %collective-permute-start.5 = (bf16[448,2048]{1,0:T(8,128)(2,1)}, bf16[448,2048]{1,0:T(8,128)(2,1)}, u32[]{:S(2)}, u32[]{:S(2)}) collective-permute-start(bf16[448,2048]{1,0:T(8,128)(2,1)} %own.1.refs_1_.refs_3_), channel_id=1, source_target_pairs={{0,2},{2,4},{3,1},{4,6},{5,3},{7,5},{8,10},{10,12},{11,9},{12,14},... | collective-permute-start | bytes 5505032 | tf_op jit(solution)/shard_map/ppermute | solution.py:369
  28.8 2.6 forward.9
  33.0 8.4 %delta.5.refs_2_.refs_4_ = bf16[2048,768]{1,0:T(8,128)(2,1)S(1)} custom-call(s32[1,1792]{1,0:T(1,128)S(1)} %broadcast_in_dim.9.refs_0_.refs_6_.refs_3_, s32[1,1792]{1,0:T(1,128)S(1)} %broadcast_in_dim.10.refs_1_.refs_7_.refs_4_, f32[32,1,1792]{2,1,0:T(1,128)S(1)} %broadcast_in_dim_reshape.4.refs_2_.refs_8_.refs_5_, f32[2048,1792]{1,0:T(8,128)} %refs_9_.7, ...), custom_call_target="tpu_custom_call" | custom-call | flops 40000000000 | bytes 1024 | tf_op jit(solution)/shard_map/delta/pallas_call | solution.py:79
  43.6 3.8 %collective-permute-done.1.refs_1_ = bf16[224,512]{1,0:T(8,128)(2,1)S(1)} collective-permute-done((bf16[224,512]{1,0:T(8,128)(2,1)S(1)}, bf16[224,512]{1,0:T(8,128)(2,1)S(1)}, u32[]{:S(2)}, u32[]{:S(2)}) %collective-permute-start.1) | collective-permute-done | bytes 229408 | tf_op jit(solution)/shard_map/ppermute | solution.py:355
  47.5 3.2 forward.10
  56.4 2.5 collective-permute-done.4.refs_1_
  68.1 4.1 %forward.11 = (bf16[224,1792]{1,0:T(8,128)(2,1)S(1)}, bf16[224,1792]{1,0:T(8,128)(2,1)S(1)}) custom-call(s32[3]{0:T(128)S(1)} %copy-done.2, bf16[448,2048]{1,0:T(8,128)(2,1)S(1)} %near.1.refs_1_.refs_5_.refs_2_, bf16[2048,512]{1,0:T(8,128)(2,1)S(1)} %copy-done.25, bf16[2048,512]{1,0:T(8,128)(2,1)S(1)} %copy-done.20, bf16[2048,768]{1,0:T(8,128)(2,1)S(1)} %copy-done.13, ...), custom_call_target="tpu_custom_call" | custom-call | flops 40000000000 | bytes 1024 | tf_op jit(solution)/shard_map/forward/pallas_call | solution.py:79
  76.9 2.6 collective-permute-start.15
  81.3 3.7 %collective-permute-done.12.refs_1_ = bf16[224,1792]{1,0:T(8,128)(2,1)S(1)} collective-permute-done((bf16[224,1792]{1,0:T(8,128)(2,1)S(1)}, bf16[224,1792]{1,0:T(8,128)(2,1)S(1)}, u32[]{:S(2)}, u32[]{:S(2)}) %collective-permute-start.12) | collective-permute-done | bytes 802848 | tf_op jit(solution)/shard_map/ppermute | solution.py:355
  85.4 7.1 %collective-permute-done.11.refs_2_ = bf16[224,768]{1,0:T(8,128)(2,1)S(1)} collective-permute-done((bf16[224,768]{1,0:T(8,128)(2,1)S(1)}, bf16[224,768]{1,0:T(8,128)(2,1)S(1)}, u32[]{:S(2)}, u32[]{:S(2)}) %collective-permute-start.11) | collective-permute-done | bytes 344096 | tf_op jit(solution)/shard_map/ppermute | solution.py:355
  97.1 4.1 %forward.12 = (bf16[224,1792]{1,0:T(8,128)(2,1)S(1)}, bf16[224,1792]{1,0:T(8,128)(2,1)S(1)}) custom-call(s32[3]{0:T(128)S(1)} %copy-done.2, bf16[448,2048]{1,0:T(8,128)(2,1)S(1)} %mid.1.refs_1_.refs_5_.refs_3_, bf16[2048,512]{1,0:T(8,128)(2,1)S(1)} %copy-done.26, bf16[2048,512]{1,0:T(8,128)(2,1)S(1)} %copy-done.21, bf16[2048,768]{1,0:T(8,128)(2,1)S(1)} %copy-done.14, ...), custom_call_target="tpu_custom_call" | custom-call | flops 40000000000 | bytes 1024 | tf_op jit(solution)/shard_map/forward/pallas_call | solution.py:79
  104.7 12.2 %collective-permute-done.19.refs_1_ = bf16[224,1792]{1,0:T(8,128)(2,1)S(1)} collective-permute-done((bf16[224,1792]{1,0:T(8,128)(2,1)S(1)}, bf16[224,1792]{1,0:T(8,128)(2,1)S(1)}, u32[]{:S(2)}, u32[]{:S(2)}) %collective-permute-start.19) | collective-permute-done | bytes 802848 | tf_op jit(solution)/shard_map/ppermute | solution.py:355
  121.9 8.9 %collective-permute-done.16.refs_2_ = bf16[224,1792]{1,0:T(8,128)(2,1)} collective-permute-done((bf16[224,1792]{1,0:T(8,128)(2,1)}, bf16[224,1792]{1,0:T(8,128)(2,1)}, u32[]{:S(2)}, u32[]{:S(2)}) %collective-permute-start.16) | collective-permute-done | bytes 802848 | tf_op jit(solution)/shard_map/ppermute | solution.py:355
  144.8 4.4 %collective-permute-done.23.refs_1_ = bf16[224,512]{1,0:T(8,128)(2,1)S(1)} collective-permute-done((bf16[224,512]{1,0:T(8,128)(2,1)S(1)}, bf16[224,512]{1,0:T(8,128)(2,1)S(1)}, u32[]{:S(2)}, u32[]{:S(2)}) %collective-permute-start.23) | collective-permute-done | bytes 229408 | tf_op jit(solution)/shard_map/ppermute | solution.py:355
  149.4 3.5 %collective-permute-done.22.refs_1_ = bf16[224,768]{1,0:T(8,128)(2,1)S(1)} collective-permute-done((bf16[224,768]{1,0:T(8,128)(2,1)S(1)}, bf16[224,768]{1,0:T(8,128)(2,1)S(1)}, u32[]{:S(2)}, u32[]{:S(2)}) %collective-permute-start.22) | collective-permute-done | bytes 344096 | tf_op jit(solution)/shard_map/ppermute | solution.py:355
  153.1 8.4 %collective-permute-done.21.refs_2_ = bf16[224,1792]{1,0:T(8,128)(2,1)S(1)} collective-permute-done((bf16[224,1792]{1,0:T(8,128)(2,1)S(1)}, bf16[224,1792]{1,0:T(8,128)(2,1)S(1)}, u32[]{:S(2)}, u32[]{:S(2)}) %collective-permute-start.21) | collective-permute-done | bytes 802848 | tf_op jit(solution)/shard_map/ppermute | solution.py:355
  165.7 2.7 collective-permute-done.30.refs_2_
  169.0 16.5 %backward_forward.4 = (f32[2048,512]{1,0:T(8,128)}, bf16[896,512]{1,0:T(8,128)(2,1)S(1)}, bf16[896,512]{1,0:T(8,128)(2,1)S(1)}) custom-call(s32[3]{0:T(128)S(1)} %copy-done.2, bf16[448,512]{1,0:T(8,128)(2,1)S(1)} %copy-done.35, bf16[448,1792]{1,0:T(8,128)(2,1)S(1)} %join.15.refs_3_.refs_2_, bf16[448,1792]{1,0:T(8,128)(2,1)S(1)} %join.16.refs_2_.refs_3_, ...), custom_call_target="tpu_custom_call" | custom-call | flops 40000000000 | bytes 1024 | tf_op jit(solution)/shard_map/backward_forward/pallas_call | solution.py:79
  187.5 16.6 %backward_forward.5 = (f32[2048,512]{1,0:T(8,128)}, bf16[896,512]{1,0:T(8,128)(2,1)S(1)}, bf16[896,512]{1,0:T(8,128)(2,1)S(1)}) custom-call(s32[3]{0:T(128)S(1)} %copy-done.2, bf16[448,512]{1,0:T(8,128)(2,1)S(1)} %copy-done.33, bf16[448,1792]{1,0:T(8,128)(2,1)S(1)} %join.15.refs_3_.refs_2_, bf16[448,1792]{1,0:T(8,128)(2,1)S(1)} %join.16.refs_2_.refs_3_, ...), custom_call_target="tpu_custom_call" | custom-call | flops 40000000000 | bytes 1024 | tf_op jit(solution)/shard_map/backward_forward/pallas_call | solution.py:79
  207.0 16.5 %backward_forward.6 = (f32[2048,512]{1,0:T(8,128)}, bf16[896,512]{1,0:T(8,128)(2,1)S(1)}, bf16[896,512]{1,0:T(8,128)(2,1)S(1)}) custom-call(s32[3]{0:T(128)S(1)} %copy-done.2, bf16[448,768]{1,0:T(8,128)(2,1)S(1)} %copy-done.31, bf16[448,1792]{1,0:T(8,128)(2,1)S(1)} %join.15.refs_3_.refs_2_, bf16[448,1792]{1,0:T(8,128)(2,1)S(1)} %join.16.refs_2_.refs_3_, ...), custom_call_target="tpu_custom_call" | custom-call | flops 40000000000 | bytes 1024 | tf_op jit(solution)/shard_map/backward_forward/pallas_call | solution.py:79
  225.4 10.6 %backward_forward.7 = (f32[2048,256]{1,0:T(8,128)}, bf16[896,256]{1,0:T(8,128)(2,1)S(1)}, bf16[896,256]{1,0:T(8,128)(2,1)S(1)}) custom-call(s32[3]{0:T(128)S(1)} %copy-done.2, bf16[448,768]{1,0:T(8,128)(2,1)S(1)} %copy-done.31, bf16[448,1792]{1,0:T(8,128)(2,1)S(1)} %join.15.refs_3_.refs_2_, bf16[448,1792]{1,0:T(8,128)(2,1)S(1)} %join.16.refs_2_.refs_3_, ...), custom_call_target="tpu_custom_call" | custom-call | flops 40000000000 | bytes 1024 | tf_op jit(solution)/shard_map/backward_forward/pallas_call | solution.py:79
  238.7 8.2 %collective-permute-done.36.refs_1_ = bf16[896,512]{1,0:T(8,128)(2,1)S(1)} collective-permute-done((bf16[896,512]{1,0:T(8,128)(2,1)S(1)}, bf16[896,512]{1,0:T(8,128)(2,1)S(1)}, u32[]{:S(2)}, u32[]{:S(2)}) %collective-permute-start.36) | collective-permute-done | bytes 917536 | tf_op jit(solution)/shard_map/ppermute | solution.py:355
  250.2 15.8 %collective-permute-done.34.refs_1_ = bf16[896,512]{1,0:T(8,128)(2,1)S(1)} collective-permute-done((bf16[896,512]{1,0:T(8,128)(2,1)S(1)}, bf16[896,512]{1,0:T(8,128)(2,1)S(1)}, u32[]{:S(2)}, u32[]{:S(2)}) %collective-permute-start.34) | collective-permute-done | bytes 917536 | tf_op jit(solution)/shard_map/ppermute | solution.py:355
  269.6 6.9 %collective-permute-done.40.refs_2_ = bf16[896,512]{1,0:T(8,128)(2,1)S(1)} collective-permute-done((bf16[896,512]{1,0:T(8,128)(2,1)S(1)}, bf16[896,512]{1,0:T(8,128)(2,1)S(1)}, u32[]{:S(2)}, u32[]{:S(2)}) %collective-permute-start.40) | collective-permute-done | bytes 917536 | tf_op jit(solution)/shard_map/ppermute | solution.py:355
  277.3 10.3 %backward_last.4.refs_2_.refs_8_ = f32[2048,1792]{1,0:T(8,128)} custom-call(s32[3]{0:T(128)S(1)} %copy-done.2, bf16[1792,512]{1,0:T(8,128)(2,1)S(1)} %join.20.refs_1_, bf16[1792,2048]{1,0:T(8,128)(2,1)S(1)} %bitcast.4, s32[1,1792]{1,0:T(1,128)S(1)} %broadcast_in_dim.9.refs_0_.refs_6_.refs_3_, s32[1,1792]{1,0:T(1,128)S(1)} %broadcast_in_dim.10.refs_1_.refs_7_.refs_4_, ...), custom_call_target="tpu_custom_call" | custom-call | flops 40000000000 | bytes 1024 | tf_op jit(solution)/shard_map/backward_last/pallas_call | solution.py:79
  292.6 10.2 %backward_last.5.refs_2_.refs_8_ = f32[2048,1792]{1,0:T(8,128)} custom-call(s32[3]{0:T(128)S(1)} %copy-done.2, bf16[1792,512]{1,0:T(8,128)(2,1)S(1)} %join.21.refs_1_, bf16[1792,2048]{1,0:T(8,128)(2,1)S(1)} %bitcast.4, s32[1,1792]{1,0:T(1,128)S(1)} %broadcast_in_dim.9.refs_0_.refs_6_.refs_3_, ...), custom_call_target="tpu_custom_call", output_to_operand_aliasing={{}: (8, {})} | custom-call | flops 40000000000 | bytes 1024 | tf_op jit(solution)/shard_map/backward_last/pallas_call | solution.py:79
  306.5 10.2 %backward_last.6.refs_3_.refs_8_ = f32[2048,1792]{1,0:T(8,128)} custom-call(s32[3]{0:T(128)S(1)} %copy-done.2, bf16[1792,512]{1,0:T(8,128)(2,1)S(1)} %join.22.refs_1_, bf16[1792,2048]{1,0:T(8,128)(2,1)S(1)} %bitcast.4, s32[1,1792]{1,0:T(1,128)S(1)} %broadcast_in_dim.9.refs_0_.refs_6_.refs_3_, ...), custom_call_target="tpu_custom_call", output_to_operand_aliasing={{}: (8, {})} | custom-call | flops 40000000000 | bytes 1024 | tf_op jit(solution)/shard_map/backward_last/pallas_call | solution.py:79
  318.3 6.9 %backward_last.7 = f32[2048,1792]{1,0:T(8,128)} custom-call(s32[3]{0:T(128)S(1)} %copy-done.2, bf16[1792,256]{1,0:T(8,128)(2,1)S(1)} %join.23.refs_1_, bf16[1792,2048]{1,0:T(8,128)(2,1)S(1)} %bitcast.4, s32[1,1792]{1,0:T(1,128)S(1)} %broadcast_in_dim.9.refs_0_.refs_6_.refs_3_, ...), custom_call_target="tpu_custom_call", output_to_operand_aliasing={{}: (8, {})} | custom-call | flops 40000000000 | bytes 1024 | tf_op jit(solution)/shard_map/backward_last/pallas_call | solution.py:79
  (199 shorter events, 91.1 us)
Async XLA Ops:
  0.0 16.4 %collective-permute-start = (bf16[224,2048]{1,0:T(8,128)(2,1)}, bf16[224,2048]{1,0:T(8,128)(2,1)S(1)}, u32[]{:S(2)}, u32[]{:S(2)}) collective-permute-start(bf16[224,2048]{1,0:T(8,128)(2,1)} %refs_1_.1), channel_id=1, source_target_pairs={{0,1},{1,0},{2,3},{3,2},{4,5},{5,4},{6,7},{7,6},{8,9},{9,8},{10,11... | collective-permute-start | bytes 2752520 | tf_op jit(solution)/shard_map/ppermute | solution.py:359
  23.1 31.4 %collective-permute-start.5 = (bf16[448,2048]{1,0:T(8,128)(2,1)}, bf16[448,2048]{1,0:T(8,128)(2,1)}, u32[]{:S(2)}, u32[]{:S(2)}) collective-permute-start(bf16[448,2048]{1,0:T(8,128)(2,1)} %own.1.refs_1_.refs_3_), channel_id=1, source_target_pairs={{0,2},{2,4},{3,1},{4,6},{5,3},{7,5},{8,10},{10,12},{11,9},{12,14},... | collective-permute-start | bytes 5505032 | tf_op jit(solution)/shard_map/ppermute | solution.py:369
  54.5 22.4 %collective-permute-start.13 = (bf16[448,2048]{1,0:T(8,128)(2,1)}, bf16[448,2048]{1,0:T(8,128)(2,1)}, u32[]{:S(2)}, u32[]{:S(2)}) collective-permute-start(bf16[448,2048]{1,0:T(8,128)(2,1)} %gate.3.refs_2_.refs_1_), channel_id=1, source_target_pairs={{2,4},{3,1},{4,6},{5,3},{10,12},{11,9},{12,14},{13,11},{18,20},{19... | collective-permute-start | bytes 5505032 | tf_op jit(solution)/shard_map/ppermute | solution.py:369
  59.7 13.1 %collective-permute-start.8 = (bf16[224,512]{1,0:T(8,128)(2,1)}, bf16[224,512]{1,0:T(8,128)(2,1)}, u32[]{:S(2)}, u32[]{:S(2)}) collective-permute-start(bf16[224,512]{1,0:T(8,128)(2,1)} %err.13.refs_2_.refs_1_), channel_id=1, source_target_pairs={{0,8},{1,17},{2,10},{3,19},{4,12},{5,21},{6,14},{7,23},{8,0},{9,25... | collective-permute-start | bytes 688136 | tf_op jit(solution)/shard_map/ppermute | solution.py:355
  61.0 12.9 %collective-permute-start.7 = (bf16[224,768]{1,0:T(8,128)(2,1)}, bf16[224,768]{1,0:T(8,128)(2,1)}, u32[]{:S(2)}, u32[]{:S(2)}) collective-permute-start(bf16[224,768]{1,0:T(8,128)(2,1)} %pair.14.refs_3_.refs_0_), channel_id=1, source_target_pairs={{0,16},{1,9},{2,18},{3,11},{4,20},{5,13},{6,22},{7,15},{8,24},{9,1... | collective-permute-start | bytes 1032200 | tf_op jit(solution)/shard_map/ppermute | solution.py:355
  72.2 12.9 %collective-permute-start.12 = (bf16[224,1792]{1,0:T(8,128)(2,1)S(1)}, bf16[224,1792]{1,0:T(8,128)(2,1)S(1)}, u32[]{:S(2)}, u32[]{:S(2)}) collective-permute-start(bf16[224,1792]{1,0:T(8,128)(2,1)S(1)} %get-tuple-element.40), channel_id=1, source_target_pairs={{0,8},{1,17},{2,10},{3,19},{4,12},{5,21},{6,14},{7,23},{8,0},{9,25... | collective-permute-start | bytes 2408456 | tf_op jit(solution)/shard_map/ppermute | solution.py:355
  75.3 17.1 %collective-permute-start.11 = (bf16[224,768]{1,0:T(8,128)(2,1)S(1)}, bf16[224,768]{1,0:T(8,128)(2,1)S(1)}, u32[]{:S(2)}, u32[]{:S(2)}) collective-permute-start(bf16[224,768]{1,0:T(8,128)(2,1)S(1)} %err.14.refs_1_), channel_id=1, source_target_pairs={{0,8},{1,17},{2,10},{3,19},{4,12},{5,21},{6,14},{7,23},{8,0},{9,25... | collective-permute-start | bytes 1032200 | tf_op jit(solution)/shard_map/ppermute | solution.py:355
  76.9 16.2 %collective-permute-start.15 = (bf16[448,2048]{1,0:T(8,128)(2,1)}, bf16[448,2048]{1,0:T(8,128)(2,1)S(1)}, u32[]{:S(2)}, u32[]{:S(2)}) collective-permute-start(bf16[448,2048]{1,0:T(8,128)(2,1)} %gate.4.refs_2_.refs_4_), channel_id=1, source_target_pairs={{0,1},{1,0},{2,3},{3,2},{4,5},{5,4},{6,7},{7,6},{8,9},{9,8},{10,11... | collective-permute-start | bytes 5505032 | tf_op jit(solution)/shard_map/ppermute | solution.py:359
  79.5 25.1 %collective-permute-start.17 = (bf16[448,2048]{1,0:T(8,128)(2,1)}, bf16[448,2048]{1,0:T(8,128)(2,1)}, u32[]{:S(2)}, u32[]{:S(2)}) collective-permute-start(bf16[448,2048]{1,0:T(8,128)(2,1)} %gate.4.refs_2_.refs_4_), channel_id=1, source_target_pairs={{3,1},{4,6},{11,9},{12,14},{19,17},{20,22},{27,25},{28,30}} | collective-permute-start | bytes 5505032 | tf_op jit(solution)/shard_map/ppermute | solution.py:369
  85.3 16.3 %collective-permute-start.14 = (bf16[224,1792]{1,0:T(8,128)(2,1)S(1)}, bf16[224,1792]{1,0:T(8,128)(2,1)S(1)}, u32[]{:S(2)}, u32[]{:S(2)}) collective-permute-start(bf16[224,1792]{1,0:T(8,128)(2,1)S(1)} %pair.15.refs_3_.refs_0_), channel_id=1, source_target_pairs={{0,16},{1,9},{2,18},{3,11},{4,20},{5,13},{6,22},{7,15},{8,24},{9,1... | collective-permute-start | bytes 2408456 | tf_op jit(solution)/shard_map/ppermute | solution.py:355
  101.3 15.5 %collective-permute-start.19 = (bf16[224,1792]{1,0:T(8,128)(2,1)S(1)}, bf16[224,1792]{1,0:T(8,128)(2,1)S(1)}, u32[]{:S(2)}, u32[]{:S(2)}) collective-permute-start(bf16[224,1792]{1,0:T(8,128)(2,1)S(1)} %get-tuple-element.42), channel_id=1, source_target_pairs={{0,8},{1,17},{2,10},{3,19},{4,12},{5,21},{6,14},{7,23},{8,0},{9,25... | collective-permute-start | bytes 2408456 | tf_op jit(solution)/shard_map/ppermute | solution.py:355
  102.8 28.1 %collective-permute-start.16 = (bf16[224,1792]{1,0:T(8,128)(2,1)}, bf16[224,1792]{1,0:T(8,128)(2,1)}, u32[]{:S(2)}, u32[]{:S(2)}) collective-permute-start(bf16[224,1792]{1,0:T(8,128)(2,1)} %err.15.refs_1_), channel_id=1, source_target_pairs={{0,8},{1,17},{2,10},{3,19},{4,12},{5,21},{6,14},{7,23},{8,0},{9,25... | collective-permute-start | bytes 2408456 | tf_op jit(solution)/shard_map/ppermute | solution.py:355
  104.6 13.4 %collective-permute-start.18 = (bf16[448,2048]{1,0:T(8,128)(2,1)}, bf16[448,2048]{1,0:T(8,128)(2,1)S(1)}, u32[]{:S(2)}, u32[]{:S(2)}) collective-permute-start(bf16[448,2048]{1,0:T(8,128)(2,1)} %gate.5.refs_2_.refs_5_), channel_id=1, source_target_pairs={{0,1},{1,0},{2,3},{3,2},{4,5},{5,4},{6,7},{7,6},{8,9},{9,8},{10,11... | collective-permute-start | bytes 5505032 | tf_op jit(solution)/shard_map/ppermute | solution.py:359
  117.9 21.3 %collective-permute-start.20 = (bf16[224,1792]{1,0:T(8,128)(2,1)}, bf16[224,1792]{1,0:T(8,128)(2,1)}, u32[]{:S(2)}, u32[]{:S(2)}) collective-permute-start(bf16[224,1792]{1,0:T(8,128)(2,1)} %pair.16.refs_8_.refs_0_), channel_id=1, source_target_pairs={{0,16},{1,9},{2,18},{3,11},{4,20},{5,13},{6,22},{7,15},{8,24},{9,1... | collective-permute-start | bytes 2408456 | tf_op jit(solution)/shard_map/ppermute | solution.py:355
  139.1 13.8 %collective-permute-start.22 = (bf16[224,768]{1,0:T(8,128)(2,1)S(1)}, bf16[224,768]{1,0:T(8,128)(2,1)S(1)}, u32[]{:S(2)}, u32[]{:S(2)}) collective-permute-start(bf16[224,768]{1,0:T(8,128)(2,1)S(1)} %get-tuple-element.46), channel_id=1, source_target_pairs={{0,8},{1,17},{2,10},{3,19},{4,12},{5,21},{6,14},{7,23},{8,0},{9,25... | collective-permute-start | bytes 1032200 | tf_op jit(solution)/shard_map/ppermute | solution.py:355
  140.9 20.6 %collective-permute-start.21 = (bf16[224,1792]{1,0:T(8,128)(2,1)S(1)}, bf16[224,1792]{1,0:T(8,128)(2,1)S(1)}, u32[]{:S(2)}, u32[]{:S(2)}) collective-permute-start(bf16[224,1792]{1,0:T(8,128)(2,1)S(1)} %err.16.refs_2_.refs_1_), channel_id=1, source_target_pairs={{0,8},{1,17},{2,10},{3,19},{4,12},{5,21},{6,14},{7,23},{8,0},{9,25... | collective-permute-start | bytes 2408456 | tf_op jit(solution)/shard_map/ppermute | solution.py:355
  144.7 17.5 %collective-permute-start.27 = (bf16[224,512]{1,0:T(8,128)(2,1)S(1)}, bf16[224,512]{1,0:T(8,128)(2,1)S(1)}, u32[]{:S(2)}, u32[]{:S(2)}) collective-permute-start(bf16[224,512]{1,0:T(8,128)(2,1)S(1)} %pair.17.refs_2_.refs_0_), channel_id=1, source_target_pairs={{0,16},{1,9},{2,18},{3,11},{4,20},{5,13},{6,22},{7,15},{8,24},{9,1... | collective-permute-start | bytes 688136 | tf_op jit(solution)/shard_map/ppermute | solution.py:355
  149.3 13.3 %collective-permute-start.26 = (bf16[224,512]{1,0:T(8,128)(2,1)S(1)}, bf16[224,512]{1,0:T(8,128)(2,1)S(1)}, u32[]{:S(2)}, u32[]{:S(2)}) collective-permute-start(bf16[224,512]{1,0:T(8,128)(2,1)S(1)} %pair.18.refs_2_.refs_0_), channel_id=1, source_target_pairs={{0,16},{1,9},{2,18},{3,11},{4,20},{5,13},{6,22},{7,15},{8,24},{9,1... | collective-permute-start | bytes 688136 | tf_op jit(solution)/shard_map/ppermute | solution.py:355
  162.7 23.1 %collective-permute-start.29 = (bf16[224,512]{1,0:T(8,128)(2,1)S(1)}, bf16[224,512]{1,0:T(8,128)(2,1)S(1)}, u32[]{:S(2)}, u32[]{:S(2)}) collective-permute-start(bf16[224,512]{1,0:T(8,128)(2,1)S(1)} %err.18.refs_2_.refs_1_), channel_id=1, source_target_pairs={{0,8},{1,17},{2,10},{3,19},{4,12},{5,21},{6,14},{7,23},{8,0},{9,25... | collective-permute-start | bytes 688136 | tf_op jit(solution)/shard_map/ppermute | solution.py:355
  165.4 21.0 %collective-permute-start.28 = (bf16[224,768]{1,0:T(8,128)(2,1)S(1)}, bf16[224,768]{1,0:T(8,128)(2,1)S(1)}, u32[]{:S(2)}, u32[]{:S(2)}) collective-permute-start(bf16[224,768]{1,0:T(8,128)(2,1)S(1)} %err.19.refs_3_.refs_1_), channel_id=1, source_target_pairs={{0,8},{1,17},{2,10},{3,19},{4,12},{5,21},{6,14},{7,23},{8,0},{9,25... | collective-permute-start | bytes 1032200 | tf_op jit(solution)/shard_map/ppermute | solution.py:355
  185.5 20.4 %collective-permute-start.32 = (bf16[896,512]{1,0:T(8,128)(2,1)S(1)}, bf16[896,512]{1,0:T(8,128)(2,1)S(1)}, u32[]{:S(2)}, u32[]{:S(2)}) collective-permute-start(bf16[896,512]{1,0:T(8,128)(2,1)S(1)} %get-tuple-element.52), channel_id=1, source_target_pairs={{0,8},{1,17},{2,10},{3,19},{4,12},{5,21},{6,14},{7,23},{8,0},{9,25... | collective-permute-start | bytes 2752520 | tf_op jit(solution)/shard_map/ppermute | solution.py:355
  204.0 21.0 %collective-permute-start.31 = (bf16[896,512]{1,0:T(8,128)(2,1)S(1)}, bf16[896,512]{1,0:T(8,128)(2,1)S(1)}, u32[]{:S(2)}, u32[]{:S(2)}) collective-permute-start(bf16[896,512]{1,0:T(8,128)(2,1)S(1)} %get-tuple-element.51), channel_id=1, source_target_pairs={{0,8},{1,17},{2,10},{3,19},{4,12},{5,21},{6,14},{7,23},{8,0},{9,25... | collective-permute-start | bytes 2752520 | tf_op jit(solution)/shard_map/ppermute | solution.py:355
  223.5 23.4 %collective-permute-start.36 = (bf16[896,512]{1,0:T(8,128)(2,1)S(1)}, bf16[896,512]{1,0:T(8,128)(2,1)S(1)}, u32[]{:S(2)}, u32[]{:S(2)}) collective-permute-start(bf16[896,512]{1,0:T(8,128)(2,1)S(1)} %pair.20.refs_12_.refs_0_), channel_id=1, source_target_pairs={{0,16},{1,9},{2,18},{3,11},{4,20},{5,13},{6,22},{7,15},{8,24},{9,1... | collective-permute-start | bytes 2752520 | tf_op jit(solution)/shard_map/ppermute | solution.py:355
  223.6 24.0 %collective-permute-start.35 = (bf16[896,512]{1,0:T(8,128)(2,1)S(1)}, bf16[896,512]{1,0:T(8,128)(2,1)S(1)}, u32[]{:S(2)}, u32[]{:S(2)}) collective-permute-start(bf16[896,512]{1,0:T(8,128)(2,1)S(1)} %get-tuple-element.56), channel_id=1, source_target_pairs={{0,8},{1,17},{2,10},{3,19},{4,12},{5,21},{6,14},{7,23},{8,0},{9,25... | collective-permute-start | bytes 2752520 | tf_op jit(solution)/shard_map/ppermute | solution.py:355
  236.0 30.0 %collective-permute-start.34 = (bf16[896,512]{1,0:T(8,128)(2,1)S(1)}, bf16[896,512]{1,0:T(8,128)(2,1)S(1)}, u32[]{:S(2)}, u32[]{:S(2)}) collective-permute-start(bf16[896,512]{1,0:T(8,128)(2,1)S(1)} %pair.21.refs_12_.refs_0_), channel_id=1, source_target_pairs={{0,16},{1,9},{2,18},{3,11},{4,20},{5,13},{6,22},{7,15},{8,24},{9,1... | collective-permute-start | bytes 2752520 | tf_op jit(solution)/shard_map/ppermute | solution.py:355
  236.9 30.6 %collective-permute-start.33 = (bf16[896,256]{1,0:T(8,128)(2,1)S(1)}, bf16[896,256]{1,0:T(8,128)(2,1)S(1)}, u32[]{:S(2)}, u32[]{:S(2)}) collective-permute-start(bf16[896,256]{1,0:T(8,128)(2,1)S(1)} %get-tuple-element.55), channel_id=1, source_target_pairs={{0,8},{1,17},{2,10},{3,19},{4,12},{5,21},{6,14},{7,23},{8,0},{9,25... | collective-permute-start | bytes 1376264 | tf_op jit(solution)/shard_map/ppermute | solution.py:355
  247.3 29.1 %collective-permute-start.40 = (bf16[896,512]{1,0:T(8,128)(2,1)S(1)}, bf16[896,512]{1,0:T(8,128)(2,1)S(1)}, u32[]{:S(2)}, u32[]{:S(2)}) collective-permute-start(bf16[896,512]{1,0:T(8,128)(2,1)S(1)} %err.20.refs_2_.refs_1_), channel_id=1, source_target_pairs={{0,8},{1,17},{2,10},{3,19},{4,12},{5,21},{6,14},{7,23},{8,0},{9,25... | collective-permute-start | bytes 2752520 | tf_op jit(solution)/shard_map/ppermute | solution.py:355
  248.9 38.6 %collective-permute-start.39 = (bf16[896,512]{1,0:T(8,128)(2,1)}, bf16[896,512]{1,0:T(8,128)(2,1)}, u32[]{:S(2)}, u32[]{:S(2)}) collective-permute-start(bf16[896,512]{1,0:T(8,128)(2,1)} %pair.22.refs_2_.refs_0_), channel_id=1, source_target_pairs={{0,16},{1,9},{2,18},{3,11},{4,20},{5,13},{6,22},{7,15},{8,24},{9,1... | collective-permute-start | bytes 2752520 | tf_op jit(solution)/shard_map/ppermute | solution.py:355
  267.4 23.5 %collective-permute-start.38 = (bf16[896,512]{1,0:T(8,128)(2,1)}, bf16[896,512]{1,0:T(8,128)(2,1)}, u32[]{:S(2)}, u32[]{:S(2)}) collective-permute-start(bf16[896,512]{1,0:T(8,128)(2,1)} %err.21.refs_2_.refs_1_), channel_id=1, source_target_pairs={{0,8},{1,17},{2,10},{3,19},{4,12},{5,21},{6,14},{7,23},{8,0},{9,25... | collective-permute-start | bytes 2752520 | tf_op jit(solution)/shard_map/ppermute | solution.py:355
  268.5 34.4 %collective-permute-start.37 = (bf16[896,256]{1,0:T(8,128)(2,1)}, bf16[896,256]{1,0:T(8,128)(2,1)}, u32[]{:S(2)}, u32[]{:S(2)}) collective-permute-start(bf16[896,256]{1,0:T(8,128)(2,1)} %pair.23.refs_3_.refs_0_), channel_id=1, source_target_pairs={{0,16},{1,9},{2,18},{3,11},{4,20},{5,13},{6,22},{7,15},{8,24},{9,1... | collective-permute-start | bytes 1376264 | tf_op jit(solution)/shard_map/ppermute | solution.py:355
  289.4 15.9 %collective-permute-start.42 = (bf16[896,512]{1,0:T(8,128)(2,1)S(1)}, bf16[896,512]{1,0:T(8,128)(2,1)S(1)}, u32[]{:S(2)}, u32[]{:S(2)}) collective-permute-start(bf16[896,512]{1,0:T(8,128)(2,1)S(1)} %err.22.refs_3_.refs_1_), channel_id=1, source_target_pairs={{0,8},{1,17},{2,10},{3,19},{4,12},{5,21},{6,14},{7,23},{8,0},{9,25... | collective-permute-start | bytes 2752520 | tf_op jit(solution)/shard_map/ppermute | solution.py:355
  304.3 12.4 %collective-permute-start.41 = (bf16[896,256]{1,0:T(8,128)(2,1)S(1)}, bf16[896,256]{1,0:T(8,128)(2,1)S(1)}, u32[]{:S(2)}, u32[]{:S(2)}) collective-permute-start(bf16[896,256]{1,0:T(8,128)(2,1)S(1)} %err.23.refs_3_.refs_1_), channel_id=1, source_target_pairs={{0,8},{1,17},{2,10},{3,19},{4,12},{5,21},{6,14},{7,23},{8,0},{9,25... | collective-permute-start | bytes 1376264 | tf_op jit(solution)/shard_map/ppermute | solution.py:355
  (49 other events, 298.1 us)

commit v2 on v1

--- a/solution.py
+++ b/solution.py
@@ -10,7 +10,7 @@
 TILE = 256
 STRIP = 16
 ROWS = 512
-VMEM_LIMIT = 24 * 1024 * 1024
+MIB = 1024 * 1024
 
 
 step_rate = 20.0
@@ -58,7 +58,7 @@
     return rounding
 
 
-KERNEL_FLOPS = 40_000_000_000
+PEAK_PER_US = 1_000_000_000
 VMEM = pl.BlockSpec(memory_space=pltpu.VMEM)
 ANY = pl.BlockSpec(memory_space=pl.ANY)
 HBM = pl.BlockSpec(memory_space=pltpu.HBM)
@@ -69,26 +69,26 @@
     def __init__(self):
         self.last = None
 
-    def call(self, kernel, name, operands, in_specs, out_specs, out_shape, flops, moved, grid=(), scratch=(), aliases=None, late_hbm=False):
+    def call(self, kernel, name, operands, in_specs, out_specs, out_shape, us, grid=(), scratch=(), aliases=None, late_hbm=False, mib=6, late=-1):
         count = len(operands)
-        late = [] if self.last is None or late_hbm else [self.last]
+        before = [] if self.last is None or late_hbm else [self.last]
 
         def wrapped(*refs):
-            return kernel(*refs[:count], *refs[count + len(late):])
+            return kernel(*refs[:count], *refs[count + len(before):])
 
         out = pl.pallas_call(
             wrapped,
             grid=grid,
-            in_specs=list(in_specs) + [ANY] * len(late),
+            in_specs=list(in_specs) + [ANY] * len(before),
             out_specs=out_specs,
             out_shape=out_shape,
             scratch_shapes=list(scratch),
             input_output_aliases=aliases or {},
-            compiler_params=pltpu.CompilerParams(vmem_limit_bytes=VMEM_LIMIT),
-            cost_estimate=pl.CostEstimate(flops=KERNEL_FLOPS, bytes_accessed=1024, transcendentals=0),
+            compiler_params=pltpu.CompilerParams(vmem_limit_bytes=mib * MIB),
+            cost_estimate=pl.CostEstimate(flops=int(us * PEAK_PER_US), bytes_accessed=1024, transcendentals=0),
             name=name,
-        )(*operands, *late)
-        self.last = pltpu.with_memory_space_constraint(out[0], pltpu.HBM) if late_hbm else out[-1]
+        )(*operands, *before)
+        self.last = pltpu.with_memory_space_constraint(out[0], pltpu.HBM) if late_hbm else out[late]
         return out
 
 
@@ -99,7 +99,7 @@
 
 def update_rows(grad, t, v, code, scales, kept):
     square = t * t
-    pull = jnp.where((code >= 0) & (code <= 14), grad * scales, 0.0)
+    pull = jnp.where((code >= 0.0) & (code <= 14.0), grad * scales, 0.0)
     descent = pull - (8.0 * reg_weight) * (t * square)
     return v - ((0.25 * step_rate) * kept) * (1.0 - square) * descent
 
@@ -110,7 +110,7 @@
             body(pl.multiple_of(i * BLOCK + j * STRIP, STRIP), i)
         return carry
 
-    lax.fori_loop(0, rows // BLOCK, block, 0)
+    lax.fori_loop(0, rows // BLOCK, block, 0, unroll=8)
 
 
 def steps_of(codes):
@@ -119,33 +119,36 @@
 
 def first_delta(chain, col, cols, weight, rounding, floors, scale_codes, zeros, kept):
     d = weight.shape[0]
-    wide = 512 if cols % 512 == 0 and col % 512 == 0 else TILE
-    rows = min(d, 512 * 512 // wide)
-    first = col // wide
-
-    def kernel(s_ref, zp_ref, m, v, fl, w, out):
-        def tile(v_t, fl_t, w_t):
-            j, i = pl.program_id(0), pl.program_id(1)
-            lanes = pl.ds(pl.multiple_of(j * wide, wide), wide)
-            there = pl.ds(pl.multiple_of((first + j) * wide, wide), wide)
-            s, zp = steps_of(s_ref[:, there]), zp_ref[:, there].astype(f32)
-
-            def strip(start, b):
-                at = pl.ds(start, STRIP)
-                t = jnp.tanh(0.5 * v_t[at, :])
-                mask = m[i * (rows // BLOCK) + b, :, there]
-                out[pl.ds(pl.multiple_of(i * rows + start, STRIP), STRIP), lanes] = delta_rows(
-                    t, fl_t[at, :].astype(f32), w_t[at, :].astype(f32), s, zp, mask)
-
-            by_rows(rows, strip)
-
-        spec = pl.BlockSpec((rows, wide), lambda j, i: (i, j + first))
-        pltpu.emit_pipeline(tile, grid=(cols // wide, d // rows), in_specs=[spec] * 3)(v, fl, w)
+    rows = 512 if cols <= 512 else 256
+    here = (slice(None), pl.ds(col, cols))
+
+    def kernel(s_ref, zp_ref, m, v, fl, w, out, codes):
+        def tile(v_t, fl_t, w_t, code_t):
+            g = pl.program_id(0)
+            for start, width in column_tiles(cols):
+                lanes, there = pl.ds(start, width), pl.ds(col + start, width)
+                s, zp = steps_of(s_ref[:, there]), zp_ref[:, there].astype(f32)
+
+                def strip(first, b):
+                    at = pl.ds(first, STRIP)
+                    t = jnp.tanh(0.5 * v_t[at, lanes])
+                    mask = m[g * (rows // BLOCK) + b, :, there]
+                    code = fl_t[at, lanes].astype(f32)
+                    code_t[at, lanes] = code.astype(bf16)
+                    out[pl.ds(pl.multiple_of(g * rows + first, STRIP), STRIP), lanes] = delta_rows(
+                        t, code, w_t[at, lanes].astype(f32), s, zp, mask)
+
+                by_rows(rows, strip)
+
+        spec = pl.BlockSpec((rows, cols), lambda g: (g, 0))
+        pltpu.emit_pipeline(tile, grid=(d // rows,), in_specs=[spec] * 3, out_specs=[spec])(
+            v.at[here], fl.at[here], w.at[here], codes)
 
     return chain.call(
         kernel, "delta", [scale_codes, zeros, kept, rounding, floors, weight],
-        [VMEM] * 3 + [HBM] * 3, [VMEM], [jax.ShapeDtypeStruct((d, cols), bf16)], 20 * d * cols, 12 * d * cols,
-    )[0]
+        [VMEM] * 3 + [HBM] * 3, [VMEM, HBM], [jax.ShapeDtypeStruct((d, cols), bf16), pltpu.HBM((d, cols), bf16)],
+        4.5 * cols / 512, mib=16, late=0,
+    )
 
 
 def split_rows(part, bit, send, keep, at, cols):
@@ -160,24 +163,22 @@
     return [(at, min(512, cols - at)) for at in range(0, cols, 512)]
 
 
-def forward(chain, place, x, first, chunks, rows, deltas):
-    d = x.shape[1]
-    total = sum(a.shape[1] for a in deltas)
+def forward(chain, place, x, first, rows, pieces):
+    total = sum(cols for _, _, cols in pieces)
 
     def kernel(place_ref, x_ref, *refs):
         ws, (send, keep) = refs[:-2], refs[-2:]
         base = 0
-        for w in ws:
-            for at, cols in column_tiles(w.shape[1]):
-                for i in range(chunks):
-                    part = jnp.dot(x_ref[first + i * rows:first + (i + 1) * rows, :], w[:, at:at + cols], preferred_element_type=f32)
-                    split_rows(part, place_ref[0], send, keep, i * (rows // 2), pl.ds(base + at, cols))
-            base += w.shape[1]
-
-    shape = jax.ShapeDtypeStruct((chunks * rows // 2, total), bf16)
-    return chain.call(
-        kernel, "forward", [place, x, *deltas], [SMEM] + [VMEM] * (1 + len(deltas)), [VMEM] * 2, [shape] * 2,
-        2 * chunks * rows * d * total, 2 * d * (chunks * rows + total) // 4,
+        for w, (_, start, width) in zip(ws, pieces):
+            for at, cols in column_tiles(width):
+                part = jnp.dot(x_ref[first:first + rows, :], w[:, start + at:start + at + cols], preferred_element_type=f32)
+                split_rows(part, place_ref[0], send, keep, 0, pl.ds(base + at, cols))
+            base += width
+
+    shape = jax.ShapeDtypeStruct((rows // 2, total), bf16)
+    return chain.call(
+        kernel, "forward", [place, x, *[w for w, _, _ in pieces]], [SMEM] + [VMEM] * (1 + len(pieces)), [VMEM] * 2, [shape] * 2,
+        0.5 + 1.15 * total / 512, mib=16,
     )
 
 
@@ -196,13 +197,13 @@
 
     return chain.call(
         kernel, "pair" if scale is None else "err", [a, b], [VMEM] * 2, [VMEM],
-        [jax.ShapeDtypeStruct(a.shape, bf16)], rows * cols, 6 * rows * cols,
+        [jax.ShapeDtypeStruct(a.shape, bf16)], 0.4,
     )[0]
 
 
 def gate(chain, a):
     return chain.call(
-        lambda a_ref, out: None, "gate", [a], [ANY], [ANY], [jax.ShapeDtypeStruct(a.shape, a.dtype)], 1, 1, aliases={0: 0}
+        lambda a_ref, out: None, "gate", [a], [ANY], [ANY], [jax.ShapeDtypeStruct(a.shape, a.dtype)], 0.1, aliases={0: 0}
     )[0]
 
 
@@ -234,7 +235,7 @@
 
     return chain.call(
         kernel, name, [place, *arrays], [SMEM] + [VMEM] * len(pieces) + [ANY] * len(candidates), [VMEM], [jax.ShapeDtypeStruct((sum(rows), width), bf16)],
-        1, 4 * sum(rows) * width, scratch=[pltpu.SemaphoreType.DMA((len(rows),))],
+        0.8, scratch=[pltpu.SemaphoreType.DMA((len(rows),))], mib=10,
     )[0]
 
 
@@ -257,11 +258,11 @@
 
     return chain.call(
         kernel, "join", [place, mine, got], [SMEM, VMEM, VMEM], [VMEM],
-        [jax.ShapeDtypeStruct((count * rows, cols), bf16)], rows * cols, 6 * rows * cols,
+        [jax.ShapeDtypeStruct((count * rows, cols), bf16)], 0.6,
     )[0]
 
 
-def backward(chain, place, errs, starts, x_full, weight, rounding, v_col, floors, scales, zeros, kept, col, cols, out_prev, last):
+def backward(chain, place, errs, starts, x_full, weight, rounding, v_col, codes, code_col, scales, zeros, kept, col, cols, out_prev, last):
     tokens, d = x_full.shape
     rows = tokens // 4
     n_err = len(errs)
@@ -297,14 +298,14 @@
 
             def strip(start, i):
                 at = pl.ds(start, STRIP)
-                code = fl_t[at, :]
-                old = v_t[at, :]
+                code = fl_t[at, :].astype(f32)
+                old = v_t[at, :].astype(f32)
                 mask = m[g * (ROWS // BLOCK) + i, :, lanes]
                 new = update_rows(grad[at, :], jnp.tanh(0.5 * old), old, code, scales, mask)
-                out_t[at, :] = new
+                out_t[at, :] = new.astype(out_t.dtype)
                 if not last:
                     to = pl.ds(pl.multiple_of(g * ROWS + start, STRIP), STRIP)
-                    delta[to, :] = delta_rows(jnp.tanh(0.5 * new), code.astype(f32), tiles[2][at, :].astype(f32), scales, zero, mask)
+                    delta[to, :] = delta_rows(jnp.tanh(0.5 * new), code, tiles[2][at, :].astype(f32), scales, zero, mask)
 
             by_rows(ROWS, strip)
 
@@ -313,7 +314,7 @@
 
         pltpu.emit_pipeline(
             tile, grid=(d // ROWS,),
-            in_specs=[spec(v_col // cols)] + [spec(here)] * (len(streams) - 1),
+            in_specs=[spec(v_col // cols), spec(code_col // cols)] + [spec(here)] * (len(streams) - 2),
             out_specs=[spec(here if last else 0)],
         )(*streams, out)
 
@@ -327,7 +328,7 @@
 
             lax.fori_loop(0, 2, two, 0)
 
-    operands = [place, *errs, x_full, scales, zeros, kept, rounding, floors]
+    operands = [place, *errs, x_full, scales, zeros, kept, rounding, codes]
     in_specs = [SMEM] + [VMEM] * (n_err + 4) + [HBM] * 2
     scratch = [pltpu.VMEM((tokens, cols), bf16), pltpu.VMEM((ROWS, cols), f32)]
     aliases = {}
@@ -337,16 +338,16 @@
             operands.append(out_prev)
             in_specs.append(HBM)
         out_specs = [HBM]
-        out_shape = [pltpu.HBM(floors.shape, f32)]
+        out_shape = [pltpu.HBM(weight.shape, f32)]
     else:
         operands.append(weight)
         in_specs.append(HBM)
         out_specs = [HBM, VMEM, VMEM]
-        out_shape = [pltpu.HBM((d, cols), f32)] + [jax.ShapeDtypeStruct((tokens // 2, cols), bf16)] * 2
+        out_shape = [pltpu.HBM((d, cols), bf16)] + [jax.ShapeDtypeStruct((tokens // 2, cols), bf16)] * 2
         scratch.append(pltpu.VMEM((d, cols), bf16))
     return chain.call(
         kernel, "backward_last" if last else "backward_forward", operands, in_specs, out_specs, out_shape,
-        (2 if last else 4) * tokens * d * cols, 16 * d * cols, scratch=scratch, aliases=aliases, late_hbm=last,
+        (7.0 if last else 14.5) * cols / 512, scratch=scratch, aliases=aliases, late_hbm=last, mib=14 if last else 22,
     )
 
 
@@ -369,11 +370,18 @@
     return lax.ppermute(a, "dp", pairs)
 
 
+DELTAS = [512, 1280]
+OWN = [512, 1280]
+NEAR = [512, 1280]
+MID = [512, 512, 768]
+FAR = [512, 512, 768]
+GROUPS = [512, 512, 512, 256]
 ORDER = [
-    "D0", "D1", "K0", "Fo0", "Fo1", "D2", "Po0", "Po1", "Fo2", "Eo0", "G1", "Eo1", "Po2", "Ro0", "K1", "Fn",
-    "Ro1", "Eo2", "G2", "Pn", "Ro2", "K2", "Fm", "En", "G3", "Pm", "K3", "Ff0", "Rn", "Ff1", "Ff2", "Em",
-    "Pf0", "Pf1", "Pf2", "Rm", "Ef0", "Ef1", "Ef2", "Rf0", "B0", "Rf1", "Rf2", "B1", "Ps0", "B2", "Ps1", "B3",
-    "Es0", "Ps2", "Es1", "Ps3", "Rs0", "L0", "Es2", "Rs1", "L1", "Es3", "Rs2", "L2", "Rs3", "L3",
+    "D0", "K0", "Fo0", "D1", "Po0", "Fo1", "Eo0", "G1", "Po1", "K1", "Fn0", "Fn1", "Ro0", "Eo1", "Pn0", "G2",
+    "Pn1", "Ro1", "K2", "En0", "Fm0", "Fm1", "En1", "Fm2", "Rn0", "G3", "Pm0", "Pm1", "Rn1", "K3", "Ff0", "Pm2",
+    "Em0", "Ff1", "Em1", "Pf0", "Ff2", "Em2", "Rm0", "Pf1", "Rm1", "Ef0", "Pf2", "Rm2", "Ef1", "Rf0", "B0", "Ef2",
+    "Rf1", "B1", "Ps0", "Rf2", "B2", "Ps1", "B3", "Es0", "Ps2", "Es1", "Ps3", "Rs0", "L0", "Es2", "Rs1", "L1",
+    "Es3", "Rs2", "L2", "Rs3", "L3",
 ]
 
 
@@ -390,10 +398,16 @@
     kept = jnp.repeat(block_mask.astype(f32), BLOCK, axis=1)[:, None, :]
     chain = Chain()
 
-    blocks = [(0, 512), (512, 512), (1024, width - 1024)]
-    groups = [(0, 512), (512, 512), (1024, 512), (1536, width - 1536)]
+    def ranges(widths):
+        starts = [sum(widths[:i]) for i in range(len(widths))]
+        return list(zip(starts, widths[:-1] + [width - starts[-1]]))
+
+    blocks = ranges(DELTAS)
+    parts = {"o": ranges(OWN), "n": ranges(NEAR), "m": ranges(MID), "f": ranges(FAR)}
+    groups = ranges(GROUPS)
     other = swap_core(tokens, n)
     came, passed = {}, {}
+    codes = {}
     chunk, deltas, sent, kept_part, pairs, errs, second, out = {}, {}, {}, {}, {}, {}, {}, [None]
 
     def above(step):
@@ -406,9 +420,17 @@
     mid_of = [above(2), below(1), above(1), below(2)]
     far_of = [above(3), above(2), below(2), below(3)]
 
-    def home(col):
-        i = max(i for i, (start, _) in enumerate(blocks) if start <= col)
-        return i, col - blocks[i][0]
+    def home(table, col):
+        i = max(i for i, (start, _) in enumerate(table) if start <= col)
+        return i, col - table[i][0]
+
+    def pieces_of(col, cols):
+        out = []
+        for i, (start, count) in enumerate(blocks):
+            low, high = max(start, col), min(start + count, col + cols)
+            if low < high:
+                out.append((deltas[i], low - start, high - low))
+        return out
 
     for step in ORDER:
         kind, arg = step[0], step[1:]
@@ -433,11 +455,10 @@
                 came[i + 1] = spread(came[i], i, n)
         elif kind == "D":
             i = int(arg)
-            deltas[i] = first_delta(chain, *blocks[i], weight, rounding, floor_codes, scales, zeros, kept)
+            deltas[i], codes[i] = first_delta(chain, *blocks[i], weight, rounding, floor_codes, scales, zeros, kept)
         elif kind == "F":
-            ws = [deltas[int(arg[1])]] if len(arg) > 1 else [deltas[i] for i in range(len(blocks))]
-            first, count = (3 * rows, 1) if arg[0] == "f" else (0, 1)
-            sent[arg], kept_part[arg] = forward(chain, place, chunk[arg[0]], first, count, rows, ws)
+            x, first = (chunk["f"], 3 * rows) if arg[0] == "f" else (chunk[arg[0]], 0)
+            sent[arg], kept_part[arg] = forward(chain, place, x, first, rows, pieces_of(*parts[arg[0]][int(arg[1])]))
         elif kind == "P":
             pairs[arg] = add(chain, kept_part[arg], swap_loop(sent[arg], 1, 2, n))
         elif kind == "E":
@@ -447,15 +468,17 @@
             errs[arg] = join(chain, place, *errs[arg], rows)
         elif kind == "B":
             col, cols = groups[int(arg)]
-            i, inner = home(col)
+            i, inner = home(blocks, col)
+            found = [(c, *home(parts[c], col)) for c in "onmf"]
             second[arg], sent["s" + arg], kept_part["s" + arg] = backward(
-                chain, place, [errs["o%d" % i], errs["n"], errs["m"], errs["f%d" % i]], [inner, col, col, inner],
-                chunk["f"], weight, rounding, col, floor_codes, scales, zeros, kept, col, cols, None, False)
+                chain, place, [errs["%s%d" % (c, k)] for c, k, _ in found], [at for _, _, at in found],
+                chunk["f"], weight, rounding, col, codes[i], inner, scales, zeros, kept, col, cols, None, False)
         elif kind == "L":
             col, cols = groups[int(arg)]
+            i, inner = home(blocks, col)
             (out[0],) = backward(
                 chain, place, [errs["s" + arg]], [0],
-                chunk["f"], weight, second[arg], 0, floor_codes, scales, zeros, kept, col, cols, out[0], True)
+                chunk["f"], weight, second[arg], 0, codes[i], inner, scales, zeros, kept, col, cols, out[0], True)
     return out[0]
 
 

time: 326 us -> 295 us (0.905)
  Pallas kernels: 173 us -> 146 us
  starting transfers between devices: 43.6 us -> 59.1 us
  local copies, waits for them, and re-layouts: 14.6 us -> 3.11 us
  waiting for transfers between devices: 92.1 us -> 83.8 us
    pallas_call x62 -> x69, Pallas kernels: 173 us -> 146 us  [call(): pl.pallas_call(wrapped, grid=grid, in_specs=list(in_specs) + [ANY] * len(...]
    ppermute x36 -> x42, starting transfers between devices: 31 us -> 51.2 us  [swap_loop(): return lax.ppermute(a, ('loop', 'dp'), pairs)]
    unnamed x76 -> x16, local copies, waits for them, and re-layouts: 12.7 us -> 1.24 us
    ppermute x36 -> x42, waiting for transfers between devices: 92 us -> 83.7 us  [swap_loop(): return lax.ppermute(a, ('loop', 'dp'), pairs)]
    ppermute x3, starting transfers between devices: 9.49 us -> 6.14 us  [spread(): return lax.ppermute(a, 'dp', pairs)]
  transfers between devices with their start and end apart: 43 -> 49, of which waited for: 16 -> 19; matrix products, arithmetic and copies ran while one was open for 1% -> 1% of each run, Pallas kernels for 49% -> 47%
where the time goes in v2:
time: 295 us; the launch traced here: 293 us
  Pallas kernels  146 us (49%)
  waiting for transfers between devices  83.8 us (28%)
  starting transfers between devices  59.1 us (20%)
  local copies, waits for them, and re-layouts  3.11 us (1%)
    pallas_call x69, Pallas kernels, call(): pl.pallas_call(wrapped, grid=grid, in_specs=list(in_specs) + [ANY] * len(...  146 us
    ppermute x42, waiting for transfers between devices, swap_loop(): return lax.ppermute(a, ('loop', 'dp'), pairs)  83.7 us
    ppermute x42, starting transfers between devices, swap_loop(): return lax.ppermute(a, ('loop', 'dp'), pairs)  51.2 us
    ppermute x3, starting transfers between devices, spread(): return lax.ppermute(a, 'dp', pairs)  6.14 us
  transfers between devices with their start and end apart: 49, of which 19 were waited for; matrix products, arithmetic and copies ran while one was open for 1% of the time, Pallas kernels for 47%

profile of v2, /device:TPU:0, one launch (start us, length us, event | category | flops | bytes accessed | tf_op | source)
XLA Modules:
  0.0 293.1 jit_solution(9789832024317550666)
XLA Ops:
  3.1 6.7 %delta.2 = (bf16[2048,512]{1,0:T(8,128)(2,1)S(1)}, bf16[2048,512]{1,0:T(8,128)(2,1)}) custom-call(s32[1,1792]{1,0:T(1,128)S(1)} %broadcast_in_dim.9.refs_0_.refs_6_.refs_3_, s32[1,1792]{1,0:T(1,128)S(1)} %broadcast_in_dim.10.refs_1_.refs_7_.refs_4_, f32[32,1,1792]{2,1,0:T(1,128)S(1)} %broadcast_in_dim_reshape.4.refs_2_.refs_8_.refs_5_, ...), custom_call_target="tpu_custom_call" | custom-call | flops 4499999744 | bytes 1024 | tf_op jit(solution)/shard_map/delta/pallas_call | solution.py:79
  10.8 4.6 %collective-permute-start.3 = (bf16[448,2048]{1,0:T(8,128)(2,1)S(1)}, bf16[448,2048]{1,0:T(8,128)(2,1)S(1)}, u32[]{:S(2)}, u32[]{:S(2)}) collective-permute-start(bf16[448,2048]{1,0:T(8,128)(2,1)S(1)} %own.1.refs_1_.refs_3_), channel_id=1, source_target_pairs={{0,2},{2,4},{3,1},{4,6},{5,3},{7,5},{8,10},{10,12},{11,9},{12,14},... | collective-permute-start | bytes 5505032 | tf_op jit(solution)/shard_map/ppermute | solution.py:370
  18.6 14.2 %delta.3 = (bf16[2048,1280]{1,0:T(8,128)(2,1)S(1)}, bf16[2048,1280]{1,0:T(8,128)(2,1)}) custom-call(s32[1,1792]{1,0:T(1,128)S(1)} %broadcast_in_dim.9.refs_0_.refs_6_.refs_3_, s32[1,1792]{1,0:T(1,128)S(1)} %broadcast_in_dim.10.refs_1_.refs_7_.refs_4_, f32[32,1,1792]{2,1,0:T(1,128)S(1)} %broadcast_in_dim_reshape.4.refs_2_.refs_8_.refs_5_, ...), custom_call_target="tpu_custom_call" | custom-call | flops 11249999872 | bytes 1024 | tf_op jit(solution)/shard_map/delta/pallas_call | solution.py:79
  34.5 3.1 %forward.11 = (bf16[224,1280]{1,0:T(8,128)(2,1)S(1)}, bf16[224,1280]{1,0:T(8,128)(2,1)S(1)}) custom-call(s32[3]{0:T(128)S(1)} %pad_add_fusion.refs_0_, bf16[448,2048]{1,0:T(8,128)(2,1)S(1)} %own.1.refs_1_.refs_3_, bf16[2048,1280]{1,0:T(8,128)(2,1)S(1)} %get-tuple-element.43.refs_2_, bf16[224,512]{1,0:T(8,128)(2,1)S(1)} %pair.14.refs_3_.refs_0_), custom_call_target="tpu_custom_call" | custom-call | flops 3375000064 | bytes 1024 | tf_op jit(solution)/shard_map/forward/pallas_call | solution.py:79
  42.1 7.7 %collective-permute-done.2.refs_1_ = bf16[224,1280]{1,0:T(8,128)(2,1)S(1)} collective-permute-done((bf16[224,1280]{1,0:T(8,128)(2,1)S(1)}, bf16[224,1280]{1,0:T(8,128)(2,1)S(1)}, u32[]{:S(2)}, u32[]{:S(2)}) %collective-permute-start.2) | collective-permute-done | bytes 573472 | tf_op jit(solution)/shard_map/ppermute | solution.py:356
  54.5 3.1 %forward.13 = (bf16[224,1280]{1,0:T(8,128)(2,1)S(1)}, bf16[224,1280]{1,0:T(8,128)(2,1)S(1)}) custom-call(s32[3]{0:T(128)S(1)} %pad_add_fusion.refs_0_, bf16[448,2048]{1,0:T(8,128)(2,1)S(1)} %near.1.refs_1_.refs_3_.refs_2_, bf16[2048,1280]{1,0:T(8,128)(2,1)S(1)} %get-tuple-element.43.refs_2_, bf16[224,512]{1,0:T(8,128)(2,1)S(1)} %get-tuple-element.47.refs_3_.refs_0_), custom_call_target="tpu_custom_call" | custom-call | flops 3375000064 | bytes 1024 | tf_op jit(solution)/shard_map/forward/pallas_call | solution.py:79
  58.3 3.9 %collective-permute-done.5.refs_1_ = bf16[224,1280]{1,0:T(8,128)(2,1)S(1)} collective-permute-done((bf16[224,1280]{1,0:T(8,128)(2,1)S(1)}, bf16[224,1280]{1,0:T(8,128)(2,1)S(1)}, u32[]{:S(2)}, u32[]{:S(2)}) %collective-permute-start.5) | collective-permute-done | bytes 573472 | tf_op jit(solution)/shard_map/ppermute | solution.py:356
  68.1 8.6 %collective-permute-done.9.refs_1_ = bf16[224,1280]{1,0:T(8,128)(2,1)S(1)} collective-permute-done((bf16[224,1280]{1,0:T(8,128)(2,1)S(1)}, bf16[224,1280]{1,0:T(8,128)(2,1)S(1)}, u32[]{:S(2)}, u32[]{:S(2)}) %collective-permute-start.9) | collective-permute-done | bytes 573472 | tf_op jit(solution)/shard_map/ppermute | solution.py:356
  78.4 8.0 %collective-permute-done.8.refs_2_ = bf16[224,1280]{1,0:T(8,128)(2,1)S(1)} collective-permute-done((bf16[224,1280]{1,0:T(8,128)(2,1)S(1)}, bf16[224,1280]{1,0:T(8,128)(2,1)S(1)}, u32[]{:S(2)}, u32[]{:S(2)}) %collective-permute-start.8) | collective-permute-done | bytes 573472 | tf_op jit(solution)/shard_map/ppermute | solution.py:356
  90.4 1.7 forward.15
  92.3 2.2 forward.16
  99.3 8.1 %collective-permute-done.17.refs_1_ = bf16[224,512]{1,0:T(8,128)(2,1)S(1)} collective-permute-done((bf16[224,512]{1,0:T(8,128)(2,1)S(1)}, bf16[224,512]{1,0:T(8,128)(2,1)S(1)}, u32[]{:S(2)}, u32[]{:S(2)}) %collective-permute-start.17) | collective-permute-done | bytes 229408 | tf_op jit(solution)/shard_map/ppermute | solution.py:356
  125.2 2.1 forward.19
  133.7 2.0 collective-permute-done.29.refs_2_
  136.4 2.0 collective-permute-start.33
  138.4 2.2 collective-permute-done.27.refs_1_
  142.3 3.1 %collective-permute-done.26.refs_2_ = bf16[224,768]{1,0:T(8,128)(2,1)S(1)} collective-permute-done((bf16[224,768]{1,0:T(8,128)(2,1)S(1)}, bf16[224,768]{1,0:T(8,128)(2,1)S(1)}, u32[]{:S(2)}, u32[]{:S(2)}) %collective-permute-start.26) | collective-permute-done | bytes 344096 | tf_op jit(solution)/shard_map/ppermute | solution.py:356
  146.2 2.1 collective-permute-start.37
  148.3 2.0 collective-permute-done.33.refs_2_
  151.0 15.2 %backward_forward.4 = (bf16[2048,512]{1,0:T(8,128)(2,1)}, bf16[896,512]{1,0:T(8,128)(2,1)S(1)}, bf16[896,512]{1,0:T(8,128)(2,1)S(1)}) custom-call(s32[3]{0:T(128)S(1)} %pad_add_fusion.refs_0_, bf16[448,512]{1,0:T(8,128)(2,1)S(1)} %join.14.refs_2_.refs_1_, bf16[448,512]{1,0:T(8,128)(2,1)S(1)} %join.16.refs_1_.refs_2_, ...), custom_call_target="tpu_custom_call" | custom-call | flops 14499999744 | bytes 1024 | tf_op jit(solution)/shard_map/backward_forward/pallas_call | solution.py:79
  169.1 15.2 %backward_forward.5 = (bf16[2048,512]{1,0:T(8,128)(2,1)}, bf16[896,512]{1,0:T(8,128)(2,1)S(1)}, bf16[896,512]{1,0:T(8,128)(2,1)S(1)}) custom-call(s32[3]{0:T(128)S(1)} %pad_add_fusion.refs_0_, bf16[448,1280]{1,0:T(8,128)(2,1)S(1)} %join.15.refs_5_.refs_1_, bf16[448,1280]{1,0:T(8,128)(2,1)S(1)} %join.17.refs_8_.refs_2_, ...), custom_call_target="tpu_custom_call" | custom-call | flops 14499999744 | bytes 1024 | tf_op jit(solution)/shard_map/backward_forward/pallas_call | solution.py:79
  188.6 15.2 %backward_forward.6 = (bf16[2048,512]{1,0:T(8,128)(2,1)}, bf16[896,512]{1,0:T(8,128)(2,1)S(1)}, bf16[896,512]{1,0:T(8,128)(2,1)S(1)}) custom-call(s32[3]{0:T(128)S(1)} %pad_add_fusion.refs_0_, bf16[448,1280]{1,0:T(8,128)(2,1)S(1)} %join.15.refs_5_.refs_1_, bf16[448,1280]{1,0:T(8,128)(2,1)S(1)} %join.17.refs_8_.refs_2_, ...), custom_call_target="tpu_custom_call" | custom-call | flops 14499999744 | bytes 1024 | tf_op jit(solution)/shard_map/backward_forward/pallas_call | solution.py:79
  204.3 3.4 %collective-permute-done.38.refs_1_ = bf16[896,512]{1,0:T(8,128)(2,1)S(1)} collective-permute-done((bf16[896,512]{1,0:T(8,128)(2,1)S(1)}, bf16[896,512]{1,0:T(8,128)(2,1)S(1)}, u32[]{:S(2)}, u32[]{:S(2)}) %collective-permute-start.38) | collective-permute-done | bytes 917536 | tf_op jit(solution)/shard_map/ppermute | solution.py:356
  208.8 9.3 %backward_forward.7 = (bf16[2048,256]{1,0:T(8,128)(2,1)}, bf16[896,256]{1,0:T(8,128)(2,1)S(1)}, bf16[896,256]{1,0:T(8,128)(2,1)S(1)}) custom-call(s32[3]{0:T(128)S(1)} %pad_add_fusion.refs_0_, bf16[448,1280]{1,0:T(8,128)(2,1)S(1)} %join.15.refs_5_.refs_1_, bf16[448,1280]{1,0:T(8,128)(2,1)S(1)} %join.17.refs_8_.refs_2_, ...), custom_call_target="tpu_custom_call" | custom-call | flops 7249999872 | bytes 1024 | tf_op jit(solution)/shard_map/backward_forward/pallas_call | solution.py:79
  220.6 6.7 %collective-permute-done.41.refs_1_ = bf16[896,512]{1,0:T(8,128)(2,1)S(1)} collective-permute-done((bf16[896,512]{1,0:T(8,128)(2,1)S(1)}, bf16[896,512]{1,0:T(8,128)(2,1)S(1)}, u32[]{:S(2)}, u32[]{:S(2)}) %collective-permute-start.41) | collective-permute-done | bytes 917536 | tf_op jit(solution)/shard_map/ppermute | solution.py:356
  228.4 2.9 collective-permute-done.40.refs_1_
  233.2 17.3 %collective-permute-done.39.refs_1_ = bf16[896,256]{1,0:T(8,128)(2,1)S(1)} collective-permute-done((bf16[896,256]{1,0:T(8,128)(2,1)S(1)}, bf16[896,256]{1,0:T(8,128)(2,1)S(1)}, u32[]{:S(2)}, u32[]{:S(2)}) %collective-permute-start.39) | collective-permute-done | bytes 458784 | tf_op jit(solution)/shard_map/ppermute | solution.py:356
  252.4 8.5 %backward_last.4.refs_2_.refs_8_ = f32[2048,1792]{1,0:T(8,128)} custom-call(s32[3]{0:T(128)S(1)} %pad_add_fusion.refs_0_, bf16[1792,512]{1,0:T(8,128)(2,1)S(1)} %join.24.refs_1_, bf16[1792,2048]{1,0:T(8,128)(2,1)S(1)} %all_tokens.1.refs_1_.refs_3_.refs_5_.refs_2_, s32[1,1792]{1,0:T(1,128)S(1)} %broadcast_in_dim.9.refs_0_.refs_6_.refs_3_, ...), custom_call_target="tpu_custom_call" | custom-call | flops 7000000000 | bytes 1024 | tf_op jit(solution)/shard_map/backward_last/pallas_call | solution.py:79
  263.6 8.6 %backward_last.5.refs_2_.refs_8_ = f32[2048,1792]{1,0:T(8,128)} custom-call(s32[3]{0:T(128)S(1)} %pad_add_fusion.refs_0_, bf16[1792,512]{1,0:T(8,128)(2,1)S(1)} %join.25.refs_1_, bf16[1792,2048]{1,0:T(8,128)(2,1)S(1)} %all_tokens.1.refs_1_.refs_3_.refs_5_.refs_2_, ...), custom_call_target="tpu_custom_call", output_to_operand_aliasing={{}: (8, {})} | custom-call | flops 7000000000 | bytes 1024 | tf_op jit(solution)/shard_map/backward_last/pallas_call | solution.py:79
  272.2 3.3 %collective-permute-done.43.refs_1_ = bf16[896,256]{1,0:T(8,128)(2,1)S(1)} collective-permute-done((bf16[896,256]{1,0:T(8,128)(2,1)S(1)}, bf16[896,256]{1,0:T(8,128)(2,1)S(1)}, u32[]{:S(2)}, u32[]{:S(2)}) %collective-permute-start.43) | collective-permute-done | bytes 458784 | tf_op jit(solution)/shard_map/ppermute | solution.py:356
  278.0 8.6 %backward_last.6.refs_3_.refs_8_ = f32[2048,1792]{1,0:T(8,128)} custom-call(s32[3]{0:T(128)S(1)} %pad_add_fusion.refs_0_, bf16[1792,512]{1,0:T(8,128)(2,1)S(1)} %join.26.refs_1_, bf16[1792,2048]{1,0:T(8,128)(2,1)S(1)} %all_tokens.1.refs_1_.refs_3_.refs_5_.refs_2_, ...), custom_call_target="tpu_custom_call", output_to_operand_aliasing={{}: (8, {})} | custom-call | flops 7000000000 | bytes 1024 | tf_op jit(solution)/shard_map/backward_last/pallas_call | solution.py:79
  287.8 5.3 %backward_last.7 = f32[2048,1792]{1,0:T(8,128)} custom-call(s32[3]{0:T(128)S(1)} %pad_add_fusion.refs_0_, bf16[1792,256]{1,0:T(8,128)(2,1)S(1)} %join.27.refs_1_, bf16[1792,2048]{1,0:T(8,128)(2,1)S(1)} %all_tokens.1.refs_1_.refs_3_.refs_5_.refs_2_, s32[1,1792]{1,0:T(1,128)S(1)} %broadcast_in_dim.9.refs_0_.refs_6_.refs_3_, ...), custom_call_target="tpu_custom_call", output_to_operand_aliasing={{}: (8, {})} | custom-call | flops 3500000000 | bytes 1024 | tf_op jit(solution)/shard_map/backward_last/pallas_call | solution.py:79
  (158 shorter events, 85.5 us)
Async XLA Ops:
  10.8 28.3 %collective-permute-start.3 = (bf16[448,2048]{1,0:T(8,128)(2,1)S(1)}, bf16[448,2048]{1,0:T(8,128)(2,1)S(1)}, u32[]{:S(2)}, u32[]{:S(2)}) collective-permute-start(bf16[448,2048]{1,0:T(8,128)(2,1)S(1)} %own.1.refs_1_.refs_3_), channel_id=1, source_target_pairs={{0,2},{2,4},{3,1},{4,6},{5,3},{7,5},{8,10},{10,12},{11,9},{12,14},... | collective-permute-start | bytes 5505032 | tf_op jit(solution)/shard_map/ppermute | solution.py:370
  17.1 15.7 %collective-permute-start.1 = (bf16[224,512]{1,0:T(8,128)(2,1)S(1)}, bf16[224,512]{1,0:T(8,128)(2,1)S(1)}, u32[]{:S(2)}, u32[]{:S(2)}) collective-permute-start(bf16[224,512]{1,0:T(8,128)(2,1)S(1)} %get-tuple-element.44), channel_id=1, source_target_pairs={{0,8},{1,17},{2,10},{3,19},{4,12},{5,21},{6,14},{7,23},{8,0},{9,25... | collective-permute-start | bytes 688136 | tf_op jit(solution)/shard_map/ppermute | solution.py:356
  39.2 23.3 %collective-permute-start.10 = (bf16[448,2048]{1,0:T(8,128)(2,1)S(1)}, bf16[448,2048]{1,0:T(8,128)(2,1)S(1)}, u32[]{:S(2)}, u32[]{:S(2)}) collective-permute-start(bf16[448,2048]{1,0:T(8,128)(2,1)S(1)} %gate.3.refs_2_.refs_1_), channel_id=1, source_target_pairs={{2,4},{3,1},{4,6},{5,3},{10,12},{11,9},{12,14},{13,11},{18,20},{19... | collective-permute-start | bytes 5505032 | tf_op jit(solution)/shard_map/ppermute | solution.py:370
  40.6 17.1 %collective-permute-start.6 = (bf16[224,512]{1,0:T(8,128)(2,1)S(1)}, bf16[224,512]{1,0:T(8,128)(2,1)S(1)}, u32[]{:S(2)}, u32[]{:S(2)}) collective-permute-start(bf16[224,512]{1,0:T(8,128)(2,1)S(1)} %err.14.refs_1_), channel_id=1, source_target_pairs={{0,8},{1,17},{2,10},{3,19},{4,12},{5,21},{6,14},{7,23},{8,0},{9,25... | collective-permute-start | bytes 688136 | tf_op jit(solution)/shard_map/ppermute | solution.py:356
  62.5 24.6 %collective-permute-start.13 = (bf16[448,2048]{1,0:T(8,128)(2,1)S(1)}, bf16[448,2048]{1,0:T(8,128)(2,1)S(1)}, u32[]{:S(2)}, u32[]{:S(2)}) collective-permute-start(bf16[448,2048]{1,0:T(8,128)(2,1)S(1)} %gate.4.refs_2_.refs_4_), channel_id=1, source_target_pairs={{0,1},{1,0},{2,3},{3,2},{4,5},{5,4},{6,7},{7,6},{8,9},{9,8},{10,11... | collective-permute-start | bytes 5505032 | tf_op jit(solution)/shard_map/ppermute | solution.py:360
  63.7 31.4 %collective-permute-start.18 = (bf16[448,2048]{1,0:T(8,128)(2,1)S(1)}, bf16[448,2048]{1,0:T(8,128)(2,1)S(1)}, u32[]{:S(2)}, u32[]{:S(2)}) collective-permute-start(bf16[448,2048]{1,0:T(8,128)(2,1)S(1)} %gate.4.refs_2_.refs_4_), channel_id=1, source_target_pairs={{3,1},{4,6},{11,9},{12,14},{19,17},{20,22},{27,25},{28,30}} | collective-permute-start | bytes 5505032 | tf_op jit(solution)/shard_map/ppermute | solution.py:370
  65.0 21.4 %collective-permute-start.8 = (bf16[224,1280]{1,0:T(8,128)(2,1)S(1)}, bf16[224,1280]{1,0:T(8,128)(2,1)S(1)}, u32[]{:S(2)}, u32[]{:S(2)}) collective-permute-start(bf16[224,1280]{1,0:T(8,128)(2,1)S(1)} %err.15.refs_2_.refs_1_), channel_id=1, source_target_pairs={{0,8},{1,17},{2,10},{3,19},{4,12},{5,21},{6,14},{7,23},{8,0},{9,25... | collective-permute-start | bytes 1720328 | tf_op jit(solution)/shard_map/ppermute | solution.py:356
  66.5 21.5 %collective-permute-start.14 = (bf16[224,512]{1,0:T(8,128)(2,1)S(1)}, bf16[224,512]{1,0:T(8,128)(2,1)S(1)}, u32[]{:S(2)}, u32[]{:S(2)}) collective-permute-start(bf16[224,512]{1,0:T(8,128)(2,1)S(1)} %pair.16.refs_1_.refs_0_), channel_id=1, source_target_pairs={{0,16},{1,9},{2,18},{3,11},{4,20},{5,13},{6,22},{7,15},{8,24},{9,1... | collective-permute-start | bytes 688136 | tf_op jit(solution)/shard_map/ppermute | solution.py:356
  76.8 15.2 %collective-permute-start.12 = (bf16[224,1280]{1,0:T(8,128)(2,1)S(1)}, bf16[224,1280]{1,0:T(8,128)(2,1)S(1)}, u32[]{:S(2)}, u32[]{:S(2)}) collective-permute-start(bf16[224,1280]{1,0:T(8,128)(2,1)S(1)} %pair.17.refs_3_.refs_0_), channel_id=1, source_target_pairs={{0,16},{1,9},{2,18},{3,11},{4,20},{5,13},{6,22},{7,15},{8,24},{9,1... | collective-permute-start | bytes 1720328 | tf_op jit(solution)/shard_map/ppermute | solution.py:356
  95.1 17.2 %collective-permute-start.21 = (bf16[448,2048]{1,0:T(8,128)(2,1)S(1)}, bf16[448,2048]{1,0:T(8,128)(2,1)S(1)}, u32[]{:S(2)}, u32[]{:S(2)}) collective-permute-start(bf16[448,2048]{1,0:T(8,128)(2,1)S(1)} %gate.5.refs_2_.refs_5_), channel_id=1, source_target_pairs={{0,1},{1,0},{2,3},{3,2},{4,5},{5,4},{6,7},{7,6},{8,9},{9,8},{10,11... | collective-permute-start | bytes 5505032 | tf_op jit(solution)/shard_map/ppermute | solution.py:360
  95.2 16.4 %collective-permute-start.15 = (bf16[224,1280]{1,0:T(8,128)(2,1)S(1)}, bf16[224,1280]{1,0:T(8,128)(2,1)S(1)}, u32[]{:S(2)}, u32[]{:S(2)}) collective-permute-start(bf16[224,1280]{1,0:T(8,128)(2,1)S(1)} %err.17.refs_3_.refs_1_), channel_id=1, source_target_pairs={{0,8},{1,17},{2,10},{3,19},{4,12},{5,21},{6,14},{7,23},{8,0},{9,25... | collective-permute-start | bytes 1720328 | tf_op jit(solution)/shard_map/ppermute | solution.py:356
  97.3 12.7 %collective-permute-start.16 = (bf16[224,512]{1,0:T(8,128)(2,1)S(1)}, bf16[224,512]{1,0:T(8,128)(2,1)S(1)}, u32[]{:S(2)}, u32[]{:S(2)}) collective-permute-start(bf16[224,512]{1,0:T(8,128)(2,1)S(1)} %get-tuple-element.53), channel_id=1, source_target_pairs={{0,8},{1,17},{2,10},{3,19},{4,12},{5,21},{6,14},{7,23},{8,0},{9,25... | collective-permute-start | bytes 688136 | tf_op jit(solution)/shard_map/ppermute | solution.py:356
  98.8 18.5 %collective-permute-start.20 = (bf16[224,768]{1,0:T(8,128)(2,1)S(1)}, bf16[224,768]{1,0:T(8,128)(2,1)S(1)}, u32[]{:S(2)}, u32[]{:S(2)}) collective-permute-start(bf16[224,768]{1,0:T(8,128)(2,1)S(1)} %get-tuple-element.56), channel_id=1, source_target_pairs={{0,8},{1,17},{2,10},{3,19},{4,12},{5,21},{6,14},{7,23},{8,0},{9,25... | collective-permute-start | bytes 1032200 | tf_op jit(solution)/shard_map/ppermute | solution.py:356
  110.0 12.9 %collective-permute-start.24 = (bf16[224,512]{1,0:T(8,128)(2,1)S(1)}, bf16[224,512]{1,0:T(8,128)(2,1)S(1)}, u32[]{:S(2)}, u32[]{:S(2)}) collective-permute-start(bf16[224,512]{1,0:T(8,128)(2,1)S(1)} %pair.19.refs_3_.refs_0_), channel_id=1, source_target_pairs={{0,16},{1,9},{2,18},{3,11},{4,20},{5,13},{6,22},{7,15},{8,24},{9,1... | collective-permute-start | bytes 688136 | tf_op jit(solution)/shard_map/ppermute | solution.py:356
  123.0 12.6 %collective-permute-start.29 = (bf16[224,512]{1,0:T(8,128)(2,1)S(1)}, bf16[224,512]{1,0:T(8,128)(2,1)S(1)}, u32[]{:S(2)}, u32[]{:S(2)}) collective-permute-start(bf16[224,512]{1,0:T(8,128)(2,1)S(1)} %err.19.refs_2_.refs_1_), channel_id=1, source_target_pairs={{0,8},{1,17},{2,10},{3,19},{4,12},{5,21},{6,14},{7,23},{8,0},{9,25... | collective-permute-start | bytes 688136 | tf_op jit(solution)/shard_map/ppermute | solution.py:356
  130.0 15.4 %collective-permute-start.26 = (bf16[224,768]{1,0:T(8,128)(2,1)S(1)}, bf16[224,768]{1,0:T(8,128)(2,1)S(1)}, u32[]{:S(2)}, u32[]{:S(2)}) collective-permute-start(bf16[224,768]{1,0:T(8,128)(2,1)S(1)} %err.20.refs_3_.refs_1_), channel_id=1, source_target_pairs={{0,8},{1,17},{2,10},{3,19},{4,12},{5,21},{6,14},{7,23},{8,0},{9,25... | collective-permute-start | bytes 1032200 | tf_op jit(solution)/shard_map/ppermute | solution.py:356
  132.1 14.0 %collective-permute-start.34 = (bf16[224,512]{1,0:T(8,128)(2,1)S(1)}, bf16[224,512]{1,0:T(8,128)(2,1)S(1)}, u32[]{:S(2)}, u32[]{:S(2)}) collective-permute-start(bf16[224,512]{1,0:T(8,128)(2,1)S(1)} %pair.22.refs_3_.refs_0_), channel_id=1, source_target_pairs={{0,16},{1,9},{2,18},{3,11},{4,20},{5,13},{6,22},{7,15},{8,24},{9,1... | collective-permute-start | bytes 688136 | tf_op jit(solution)/shard_map/ppermute | solution.py:356
  136.4 13.9 %collective-permute-start.33 = (bf16[224,512]{1,0:T(8,128)(2,1)S(1)}, bf16[224,512]{1,0:T(8,128)(2,1)S(1)}, u32[]{:S(2)}, u32[]{:S(2)}) collective-permute-start(bf16[224,512]{1,0:T(8,128)(2,1)S(1)} %err.21.refs_2_.refs_1_), channel_id=1, source_target_pairs={{0,8},{1,17},{2,10},{3,19},{4,12},{5,21},{6,14},{7,23},{8,0},{9,25... | collective-permute-start | bytes 688136 | tf_op jit(solution)/shard_map/ppermute | solution.py:356
  140.7 27.1 %collective-permute-start.32 = (bf16[224,768]{1,0:T(8,128)(2,1)S(1)}, bf16[224,768]{1,0:T(8,128)(2,1)S(1)}, u32[]{:S(2)}, u32[]{:S(2)}) collective-permute-start(bf16[224,768]{1,0:T(8,128)(2,1)S(1)} %pair.23.refs_3_.refs_0_), channel_id=1, source_target_pairs={{0,16},{1,9},{2,18},{3,11},{4,20},{5,13},{6,22},{7,15},{8,24},{9,1... | collective-permute-start | bytes 1032200 | tf_op jit(solution)/shard_map/ppermute | solution.py:356
  146.2 22.3 %collective-permute-start.37 = (bf16[224,512]{1,0:T(8,128)(2,1)S(1)}, bf16[224,512]{1,0:T(8,128)(2,1)S(1)}, u32[]{:S(2)}, u32[]{:S(2)}) collective-permute-start(bf16[224,512]{1,0:T(8,128)(2,1)S(1)} %err.22.refs_3_.refs_1_), channel_id=1, source_target_pairs={{0,8},{1,17},{2,10},{3,19},{4,12},{5,21},{6,14},{7,23},{8,0},{9,25... | collective-permute-start | bytes 688136 | tf_op jit(solution)/shard_map/ppermute | solution.py:356
  166.1 19.8 %collective-permute-start.36 = (bf16[896,512]{1,0:T(8,128)(2,1)S(1)}, bf16[896,512]{1,0:T(8,128)(2,1)S(1)}, u32[]{:S(2)}, u32[]{:S(2)}) collective-permute-start(bf16[896,512]{1,0:T(8,128)(2,1)S(1)} %get-tuple-element.65), channel_id=1, source_target_pairs={{0,8},{1,17},{2,10},{3,19},{4,12},{5,21},{6,14},{7,23},{8,0},{9,25... | collective-permute-start | bytes 2752520 | tf_op jit(solution)/shard_map/ppermute | solution.py:356
  167.9 20.0 %collective-permute-start.35 = (bf16[224,768]{1,0:T(8,128)(2,1)S(1)}, bf16[224,768]{1,0:T(8,128)(2,1)S(1)}, u32[]{:S(2)}, u32[]{:S(2)}) collective-permute-start(bf16[224,768]{1,0:T(8,128)(2,1)S(1)} %err.23.refs_3_.refs_1_), channel_id=1, source_target_pairs={{0,8},{1,17},{2,10},{3,19},{4,12},{5,21},{6,14},{7,23},{8,0},{9,25... | collective-permute-start | bytes 1032200 | tf_op jit(solution)/shard_map/ppermute | solution.py:356
  184.3 23.3 %collective-permute-start.38 = (bf16[896,512]{1,0:T(8,128)(2,1)S(1)}, bf16[896,512]{1,0:T(8,128)(2,1)S(1)}, u32[]{:S(2)}, u32[]{:S(2)}) collective-permute-start(bf16[896,512]{1,0:T(8,128)(2,1)S(1)} %get-tuple-element.68), channel_id=1, source_target_pairs={{0,8},{1,17},{2,10},{3,19},{4,12},{5,21},{6,14},{7,23},{8,0},{9,25... | collective-permute-start | bytes 2752520 | tf_op jit(solution)/shard_map/ppermute | solution.py:356
  186.3 31.8 %collective-permute-start.42 = (bf16[896,512]{1,0:T(8,128)(2,1)S(1)}, bf16[896,512]{1,0:T(8,128)(2,1)S(1)}, u32[]{:S(2)}, u32[]{:S(2)}) collective-permute-start(bf16[896,512]{1,0:T(8,128)(2,1)S(1)} %pair.24.refs_3_.refs_0_), channel_id=1, source_target_pairs={{0,16},{1,9},{2,18},{3,11},{4,20},{5,13},{6,22},{7,15},{8,24},{9,1... | collective-permute-start | bytes 2752520 | tf_op jit(solution)/shard_map/ppermute | solution.py:356
  203.8 23.5 %collective-permute-start.41 = (bf16[896,512]{1,0:T(8,128)(2,1)S(1)}, bf16[896,512]{1,0:T(8,128)(2,1)S(1)}, u32[]{:S(2)}, u32[]{:S(2)}) collective-permute-start(bf16[896,512]{1,0:T(8,128)(2,1)S(1)} %get-tuple-element.72), channel_id=1, source_target_pairs={{0,8},{1,17},{2,10},{3,19},{4,12},{5,21},{6,14},{7,23},{8,0},{9,25... | collective-permute-start | bytes 2752520 | tf_op jit(solution)/shard_map/ppermute | solution.py:356
  208.0 23.4 %collective-permute-start.40 = (bf16[896,512]{1,0:T(8,128)(2,1)S(1)}, bf16[896,512]{1,0:T(8,128)(2,1)S(1)}, u32[]{:S(2)}, u32[]{:S(2)}) collective-permute-start(bf16[896,512]{1,0:T(8,128)(2,1)S(1)} %pair.25.refs_12_.refs_0_), channel_id=1, source_target_pairs={{0,16},{1,9},{2,18},{3,11},{4,20},{5,13},{6,22},{7,15},{8,24},{9,1... | collective-permute-start | bytes 2752520 | tf_op jit(solution)/shard_map/ppermute | solution.py:356
  218.5 32.2 %collective-permute-start.46 = (bf16[896,512]{1,0:T(8,128)(2,1)S(1)}, bf16[896,512]{1,0:T(8,128)(2,1)S(1)}, u32[]{:S(2)}, u32[]{:S(2)}) collective-permute-start(bf16[896,512]{1,0:T(8,128)(2,1)S(1)} %err.24.refs_2_.refs_1_), channel_id=1, source_target_pairs={{0,8},{1,17},{2,10},{3,19},{4,12},{5,21},{6,14},{7,23},{8,0},{9,25... | collective-permute-start | bytes 2752520 | tf_op jit(solution)/shard_map/ppermute | solution.py:356
  219.3 31.3 %collective-permute-start.39 = (bf16[896,256]{1,0:T(8,128)(2,1)S(1)}, bf16[896,256]{1,0:T(8,128)(2,1)S(1)}, u32[]{:S(2)}, u32[]{:S(2)}) collective-permute-start(bf16[896,256]{1,0:T(8,128)(2,1)S(1)} %get-tuple-element.71), channel_id=1, source_target_pairs={{0,8},{1,17},{2,10},{3,19},{4,12},{5,21},{6,14},{7,23},{8,0},{9,25... | collective-permute-start | bytes 1376264 | tf_op jit(solution)/shard_map/ppermute | solution.py:356
  227.7 33.2 %collective-permute-start.45 = (bf16[896,512]{1,0:T(8,128)(2,1)S(1)}, bf16[896,512]{1,0:T(8,128)(2,1)S(1)}, u32[]{:S(2)}, u32[]{:S(2)}) collective-permute-start(bf16[896,512]{1,0:T(8,128)(2,1)S(1)} %pair.26.refs_2_.refs_0_), channel_id=1, source_target_pairs={{0,16},{1,9},{2,18},{3,11},{4,20},{5,13},{6,22},{7,15},{8,24},{9,1... | collective-permute-start | bytes 2752520 | tf_op jit(solution)/shard_map/ppermute | solution.py:356
  231.8 31.0 %collective-permute-start.44 = (bf16[896,512]{1,0:T(8,128)(2,1)S(1)}, bf16[896,512]{1,0:T(8,128)(2,1)S(1)}, u32[]{:S(2)}, u32[]{:S(2)}) collective-permute-start(bf16[896,512]{1,0:T(8,128)(2,1)S(1)} %err.25.refs_2_.refs_1_), channel_id=1, source_target_pairs={{0,8},{1,17},{2,10},{3,19},{4,12},{5,21},{6,14},{7,23},{8,0},{9,25... | collective-permute-start | bytes 2752520 | tf_op jit(solution)/shard_map/ppermute | solution.py:356
  261.3 15.9 %collective-permute-start.48 = (bf16[896,512]{1,0:T(8,128)(2,1)S(1)}, bf16[896,512]{1,0:T(8,128)(2,1)S(1)}, u32[]{:S(2)}, u32[]{:S(2)}) collective-permute-start(bf16[896,512]{1,0:T(8,128)(2,1)S(1)} %err.26.refs_3_.refs_1_), channel_id=1, source_target_pairs={{0,8},{1,17},{2,10},{3,19},{4,12},{5,21},{6,14},{7,23},{8,0},{9,25... | collective-permute-start | bytes 2752520 | tf_op jit(solution)/shard_map/ppermute | solution.py:356
  262.1 13.5 %collective-permute-start.43 = (bf16[896,256]{1,0:T(8,128)(2,1)S(1)}, bf16[896,256]{1,0:T(8,128)(2,1)S(1)}, u32[]{:S(2)}, u32[]{:S(2)}) collective-permute-start(bf16[896,256]{1,0:T(8,128)(2,1)S(1)} %pair.27.refs_3_.refs_0_), channel_id=1, source_target_pairs={{0,16},{1,9},{2,18},{3,11},{4,20},{5,13},{6,22},{7,15},{8,24},{9,1... | collective-permute-start | bytes 1376264 | tf_op jit(solution)/shard_map/ppermute | solution.py:356
  (25 other events, 233.4 us)

commit v3 on v2

--- a/solution.py
+++ b/solution.py
@@ -377,10 +377,10 @@
 FAR = [512, 512, 768]
 GROUPS = [512, 512, 512, 256]
 ORDER = [
-    "D0", "K0", "Fo0", "D1", "Po0", "Fo1", "Eo0", "G1", "Po1", "K1", "Fn0", "Fn1", "Ro0", "Eo1", "Pn0", "G2",
-    "Pn1", "Ro1", "K2", "En0", "Fm0", "Fm1", "En1", "Fm2", "Rn0", "G3", "Pm0", "Pm1", "Rn1", "K3", "Ff0", "Pm2",
-    "Em0", "Ff1", "Em1", "Pf0", "Ff2", "Em2", "Rm0", "Pf1", "Rm1", "Ef0", "Pf2", "Rm2", "Ef1", "Rf0", "B0", "Ef2",
-    "Rf1", "B1", "Ps0", "Rf2", "B2", "Ps1", "B3", "Es0", "Ps2", "Es1", "Ps3", "Rs0", "L0", "Es2", "Rs1", "L1",
+    "D0", "K0", "Fo0", "D1", "Po0", "Fo1", "Eo0", "G1", "K1", "Po1", "Fn0", "Fn1", "Ro0", "Eo1", "Pn0", "G2",
+    "K2", "Pn1", "Fm0", "Ro1", "En0", "Fm1", "En1", "G3", "Fm2", "Rn0", "K3", "Ff0", "Pm0", "Pm1", "Ff1", "Pf0",
+    "Rn1", "Em0", "Pf1", "Ff2", "Ef0", "Em1", "Ef1", "Pm2", "Rm0", "Pf2", "Rf0", "B0", "Em2", "Rf1", "Rm1", "Ef2",
+    "B1", "Ps0", "Rm2", "Rf2", "B2", "Ps1", "Es0", "B3", "Ps2", "Es1", "Ps3", "Rs0", "L0", "Es2", "Rs1", "L1",
     "Es3", "Rs2", "L2", "Rs3", "L3",
 ]
 

time: 295 us -> 281 us (0.953)
  waiting for transfers between devices: 83.8 us -> 73.9 us
    ppermute x42, waiting for transfers between devices: 83.7 us -> 70.6 us  [swap_loop(): return lax.ppermute(a, ('loop', 'dp'), pairs)]
    ppermute x4, waiting for transfers between devices: 0.01 us -> 3.28 us  [swap_core(): return lax.ppermute(a, 'dp', [(i, i ^ 1) for i in range(n)])]
  transfers between devices with their start and end apart: 49 -> 49, of which waited for: 19 -> 17; matrix products, arithmetic and copies ran while one was open for 1% -> 1% of each run, Pallas kernels for 47% -> 49%
where the time goes in v3:
time: 281 us
  Pallas kernels  146 us (52%)
  waiting for transfers between devices  73.9 us (26%)
  starting transfers between devices  56.6 us (20%)
  local copies, waits for them, and re-layouts  3.34 us (1%)
    pallas_call x69, Pallas kernels, call(): pl.pallas_call(wrapped, grid=grid, in_specs=list(in_specs) + [ANY] * len(...  146 us
    ppermute x42, waiting for transfers between devices, swap_loop(): return lax.ppermute(a, ('loop', 'dp'), pairs)  70.6 us
    ppermute x42, starting transfers between devices, swap_loop(): return lax.ppermute(a, ('loop', 'dp'), pairs)  49.7 us
    ppermute x3, starting transfers between devices, spread(): return lax.ppermute(a, 'dp', pairs)  6.15 us
  transfers between devices with their start and end apart: 49, of which 17 were waited for; matrix products, arithmetic and copies ran while one was open for 1% of the time, Pallas kernels for 49%

profile of v3, /device:TPU:0, one launch (start us, length us, event | category | flops | bytes accessed | tf_op | source)
XLA Modules:
  0.0 281.0 jit_solution(13619862163232467453)
XLA Ops:
  3.1 6.7 %delta.2 = (bf16[2048,512]{1,0:T(8,128)(2,1)S(1)}, bf16[2048,512]{1,0:T(8,128)(2,1)}) custom-call(s32[1,1792]{1,0:T(1,128)S(1)} %broadcast_in_dim.9.refs_0_.refs_6_.refs_3_, s32[1,1792]{1,0:T(1,128)S(1)} %broadcast_in_dim.10.refs_1_.refs_7_.refs_4_, f32[32,1,1792]{2,1,0:T(1,128)S(1)} %broadcast_in_dim_reshape.4.refs_2_.refs_8_.refs_5_, ...), custom_call_target="tpu_custom_call" | custom-call | flops 4499999744 | bytes 1024 | tf_op jit(solution)/shard_map/delta/pallas_call | solution.py:79
  10.8 4.6 %collective-permute-start.3 = (bf16[448,2048]{1,0:T(8,128)(2,1)S(1)}, bf16[448,2048]{1,0:T(8,128)(2,1)S(1)}, u32[]{:S(2)}, u32[]{:S(2)}) collective-permute-start(bf16[448,2048]{1,0:T(8,128)(2,1)S(1)} %own.1.refs_1_.refs_3_), channel_id=1, source_target_pairs={{0,2},{2,4},{3,1},{4,6},{5,3},{7,5},{8,10},{10,12},{11,9},{12,14},... | collective-permute-start | bytes 5505032 | tf_op jit(solution)/shard_map/ppermute | solution.py:370
  18.6 14.2 %delta.3 = (bf16[2048,1280]{1,0:T(8,128)(2,1)S(1)}, bf16[2048,1280]{1,0:T(8,128)(2,1)}) custom-call(s32[1,1792]{1,0:T(1,128)S(1)} %broadcast_in_dim.9.refs_0_.refs_6_.refs_3_, s32[1,1792]{1,0:T(1,128)S(1)} %broadcast_in_dim.10.refs_1_.refs_7_.refs_4_, f32[32,1,1792]{2,1,0:T(1,128)S(1)} %broadcast_in_dim_reshape.4.refs_2_.refs_8_.refs_5_, ...), custom_call_target="tpu_custom_call" | custom-call | flops 11249999872 | bytes 1024 | tf_op jit(solution)/shard_map/delta/pallas_call | solution.py:79
  34.5 3.1 %forward.11 = (bf16[224,1280]{1,0:T(8,128)(2,1)S(1)}, bf16[224,1280]{1,0:T(8,128)(2,1)S(1)}) custom-call(s32[3]{0:T(128)S(1)} %pad_add_fusion.refs_0_, bf16[448,2048]{1,0:T(8,128)(2,1)S(1)} %own.1.refs_1_.refs_3_, bf16[2048,1280]{1,0:T(8,128)(2,1)S(1)} %get-tuple-element.43.refs_2_, bf16[224,512]{1,0:T(8,128)(2,1)S(1)} %pair.14.refs_3_.refs_0_), custom_call_target="tpu_custom_call" | custom-call | flops 3375000064 | bytes 1024 | tf_op jit(solution)/shard_map/forward/pallas_call | solution.py:79
  40.6 2.4 collective-permute-done.5.refs_2_.refs_3_
  43.7 6.0 %collective-permute-done.2.refs_1_ = bf16[224,1280]{1,0:T(8,128)(2,1)S(1)} collective-permute-done((bf16[224,1280]{1,0:T(8,128)(2,1)S(1)}, bf16[224,1280]{1,0:T(8,128)(2,1)S(1)}, u32[]{:S(2)}, u32[]{:S(2)}) %collective-permute-start.2) | collective-permute-done | bytes 573472 | tf_op jit(solution)/shard_map/ppermute | solution.py:356
  55.3 3.1 %forward.13 = (bf16[224,1280]{1,0:T(8,128)(2,1)S(1)}, bf16[224,1280]{1,0:T(8,128)(2,1)S(1)}) custom-call(s32[3]{0:T(128)S(1)} %pad_add_fusion.refs_0_, bf16[448,2048]{1,0:T(8,128)(2,1)S(1)} %near.1.refs_2_.refs_1_, bf16[2048,1280]{1,0:T(8,128)(2,1)S(1)} %get-tuple-element.43.refs_2_, bf16[224,512]{1,0:T(8,128)(2,1)S(1)} %get-tuple-element.47.refs_3_.refs_0_), custom_call_target="tpu_custom_call" | custom-call | flops 3375000064 | bytes 1024 | tf_op jit(solution)/shard_map/forward/pallas_call | solution.py:79
  58.4 1.7 collective-permute-done.7.refs_2_
  60.7 3.3 %collective-permute-done.6.refs_1_ = bf16[224,1280]{1,0:T(8,128)(2,1)S(1)} collective-permute-done((bf16[224,1280]{1,0:T(8,128)(2,1)S(1)}, bf16[224,1280]{1,0:T(8,128)(2,1)S(1)}, u32[]{:S(2)}, u32[]{:S(2)}) %collective-permute-start.6) | collective-permute-done | bytes 573472 | tf_op jit(solution)/shard_map/ppermute | solution.py:356
  69.2 5.9 %collective-permute-done.12.refs_1_ = bf16[224,1280]{1,0:T(8,128)(2,1)S(1)} collective-permute-done((bf16[224,1280]{1,0:T(8,128)(2,1)S(1)}, bf16[224,1280]{1,0:T(8,128)(2,1)S(1)}, u32[]{:S(2)}, u32[]{:S(2)}) %collective-permute-start.12) | collective-permute-done | bytes 573472 | tf_op jit(solution)/shard_map/ppermute | solution.py:356
  78.9 5.3 %collective-permute-done.8.refs_2_ = bf16[224,1280]{1,0:T(8,128)(2,1)S(1)} collective-permute-done((bf16[224,1280]{1,0:T(8,128)(2,1)S(1)}, bf16[224,1280]{1,0:T(8,128)(2,1)S(1)}, u32[]{:S(2)}, u32[]{:S(2)}) %collective-permute-start.8) | collective-permute-done | bytes 573472 | tf_op jit(solution)/shard_map/ppermute | solution.py:356
  84.9 4.9 %collective-permute-done.14.refs_1_ = bf16[224,512]{1,0:T(8,128)(2,1)S(1)} collective-permute-done((bf16[224,512]{1,0:T(8,128)(2,1)S(1)}, bf16[224,512]{1,0:T(8,128)(2,1)S(1)}, u32[]{:S(2)}, u32[]{:S(2)}) %collective-permute-start.14) | collective-permute-done | bytes 229408 | tf_op jit(solution)/shard_map/ppermute | solution.py:356
  89.9 1.7 forward.15
  96.0 2.1 forward.16
  100.0 1.7 forward.17
  104.6 1.7 forward.18
  108.3 5.6 %collective-permute-done.19.refs_1_ = bf16[224,512]{1,0:T(8,128)(2,1)S(1)} collective-permute-done((bf16[224,512]{1,0:T(8,128)(2,1)S(1)}, bf16[224,512]{1,0:T(8,128)(2,1)S(1)}, u32[]{:S(2)}, u32[]{:S(2)}) %collective-permute-start.19) | collective-permute-done | bytes 229408 | tf_op jit(solution)/shard_map/ppermute | solution.py:356
  118.6 2.1 forward.19
  122.0 5.1 %collective-permute-done.27.refs_1_ = bf16[224,512]{1,0:T(8,128)(2,1)S(1)} collective-permute-done((bf16[224,512]{1,0:T(8,128)(2,1)S(1)}, bf16[224,512]{1,0:T(8,128)(2,1)S(1)}, u32[]{:S(2)}, u32[]{:S(2)}) %collective-permute-start.27) | collective-permute-done | bytes 229408 | tf_op jit(solution)/shard_map/ppermute | solution.py:356
  129.4 2.6 collective-permute-done.25.refs_1_
  138.1 15.2 %backward_forward.4 = (bf16[2048,512]{1,0:T(8,128)(2,1)}, bf16[896,512]{1,0:T(8,128)(2,1)S(1)}, bf16[896,512]{1,0:T(8,128)(2,1)S(1)}) custom-call(s32[3]{0:T(128)S(1)} %pad_add_fusion.refs_0_, bf16[448,512]{1,0:T(8,128)(2,1)S(1)} %join.14.refs_2_.refs_1_, bf16[448,512]{1,0:T(8,128)(2,1)S(1)} %join.16.refs_8_.refs_2_, ...), custom_call_target="tpu_custom_call" | custom-call | flops 14499999744 | bytes 1024 | tf_op jit(solution)/shard_map/backward_forward/pallas_call | solution.py:79
  158.5 15.2 %backward_forward.5 = (bf16[2048,512]{1,0:T(8,128)(2,1)}, bf16[896,512]{1,0:T(8,128)(2,1)S(1)}, bf16[896,512]{1,0:T(8,128)(2,1)S(1)}) custom-call(s32[3]{0:T(128)S(1)} %pad_add_fusion.refs_0_, bf16[448,1280]{1,0:T(8,128)(2,1)S(1)} %join.15.refs_2_.refs_1_, bf16[448,1280]{1,0:T(8,128)(2,1)S(1)} %join.17.refs_2_, bf16[448,512]{1,0:T(8,128)(2,1)S(1)} %join.21.refs_2_.refs_3_, ...), custom_call_target="tpu_custom_call" | custom-call | flops 14499999744 | bytes 1024 | tf_op jit(solution)/shard_map/backward_forward/pallas_call | solution.py:79
  177.4 15.2 %backward_forward.6 = (bf16[2048,512]{1,0:T(8,128)(2,1)}, bf16[896,512]{1,0:T(8,128)(2,1)S(1)}, bf16[896,512]{1,0:T(8,128)(2,1)S(1)}) custom-call(s32[3]{0:T(128)S(1)} %pad_add_fusion.refs_0_, bf16[448,1280]{1,0:T(8,128)(2,1)S(1)} %join.15.refs_2_.refs_1_, bf16[448,1280]{1,0:T(8,128)(2,1)S(1)} %join.17.refs_2_, bf16[448,768]{1,0:T(8,128)(2,1)S(1)} %join.22.refs_3_, ...), custom_call_target="tpu_custom_call" | custom-call | flops 14499999744 | bytes 1024 | tf_op jit(solution)/shard_map/backward_forward/pallas_call | solution.py:79
  195.0 2.6 collective-permute-start.41
  199.5 9.3 %backward_forward.7 = (bf16[2048,256]{1,0:T(8,128)(2,1)}, bf16[896,256]{1,0:T(8,128)(2,1)S(1)}, bf16[896,256]{1,0:T(8,128)(2,1)S(1)}) custom-call(s32[3]{0:T(128)S(1)} %pad_add_fusion.refs_0_, bf16[448,1280]{1,0:T(8,128)(2,1)S(1)} %join.15.refs_2_.refs_1_, bf16[448,1280]{1,0:T(8,128)(2,1)S(1)} %join.17.refs_2_, bf16[448,768]{1,0:T(8,128)(2,1)S(1)} %join.22.refs_3_, ...), custom_call_target="tpu_custom_call" | custom-call | flops 7249999872 | bytes 1024 | tf_op jit(solution)/shard_map/backward_forward/pallas_call | solution.py:79
  209.5 6.5 %collective-permute-done.42.refs_1_ = bf16[896,512]{1,0:T(8,128)(2,1)S(1)} collective-permute-done((bf16[896,512]{1,0:T(8,128)(2,1)S(1)}, bf16[896,512]{1,0:T(8,128)(2,1)S(1)}, u32[]{:S(2)}, u32[]{:S(2)}) %collective-permute-start.42) | collective-permute-done | bytes 917536 | tf_op jit(solution)/shard_map/ppermute | solution.py:356
  220.7 17.6 %collective-permute-done.40.refs_1_ = bf16[896,256]{1,0:T(8,128)(2,1)S(1)} collective-permute-done((bf16[896,256]{1,0:T(8,128)(2,1)S(1)}, bf16[896,256]{1,0:T(8,128)(2,1)S(1)}, u32[]{:S(2)}, u32[]{:S(2)}) %collective-permute-start.40) | collective-permute-done | bytes 458784 | tf_op jit(solution)/shard_map/ppermute | solution.py:356
  240.2 8.5 %backward_last.4.refs_2_.refs_8_ = f32[2048,1792]{1,0:T(8,128)} custom-call(s32[3]{0:T(128)S(1)} %pad_add_fusion.refs_0_, bf16[1792,512]{1,0:T(8,128)(2,1)S(1)} %join.24.refs_1_, bf16[1792,2048]{1,0:T(8,128)(2,1)S(1)} %all_tokens.1.refs_1_.refs_3_.refs_5_.refs_2_, s32[1,1792]{1,0:T(1,128)S(1)} %broadcast_in_dim.9.refs_0_.refs_6_.refs_3_, ...), custom_call_target="tpu_custom_call" | custom-call | flops 7000000000 | bytes 1024 | tf_op jit(solution)/shard_map/backward_last/pallas_call | solution.py:79
  252.7 8.6 %backward_last.5.refs_2_.refs_8_ = f32[2048,1792]{1,0:T(8,128)} custom-call(s32[3]{0:T(128)S(1)} %pad_add_fusion.refs_0_, bf16[1792,512]{1,0:T(8,128)(2,1)S(1)} %join.25.refs_1_, bf16[1792,2048]{1,0:T(8,128)(2,1)S(1)} %all_tokens.1.refs_1_.refs_3_.refs_5_.refs_2_, ...), custom_call_target="tpu_custom_call", output_to_operand_aliasing={{}: (8, {})} | custom-call | flops 7000000000 | bytes 1024 | tf_op jit(solution)/shard_map/backward_last/pallas_call | solution.py:79
  261.3 2.5 collective-permute-done.43.refs_1_
  265.8 8.6 %backward_last.6.refs_3_.refs_8_ = f32[2048,1792]{1,0:T(8,128)} custom-call(s32[3]{0:T(128)S(1)} %pad_add_fusion.refs_0_, bf16[1792,512]{1,0:T(8,128)(2,1)S(1)} %join.26.refs_1_, bf16[1792,2048]{1,0:T(8,128)(2,1)S(1)} %all_tokens.1.refs_1_.refs_3_.refs_5_.refs_2_, ...), custom_call_target="tpu_custom_call", output_to_operand_aliasing={{}: (8, {})} | custom-call | flops 7000000000 | bytes 1024 | tf_op jit(solution)/shard_map/backward_last/pallas_call | solution.py:79
  275.6 5.3 %backward_last.7 = f32[2048,1792]{1,0:T(8,128)} custom-call(s32[3]{0:T(128)S(1)} %pad_add_fusion.refs_0_, bf16[1792,256]{1,0:T(8,128)(2,1)S(1)} %join.27.refs_1_, bf16[1792,2048]{1,0:T(8,128)(2,1)S(1)} %all_tokens.1.refs_1_.refs_3_.refs_5_.refs_2_, s32[1,1792]{1,0:T(1,128)S(1)} %broadcast_in_dim.9.refs_0_.refs_6_.refs_3_, ...), custom_call_target="tpu_custom_call", output_to_operand_aliasing={{}: (8, {})} | custom-call | flops 3500000000 | bytes 1024 | tf_op jit(solution)/shard_map/backward_last/pallas_call | solution.py:79
  (158 shorter events, 81.3 us)
Async XLA Ops:
  10.8 28.3 %collective-permute-start.3 = (bf16[448,2048]{1,0:T(8,128)(2,1)S(1)}, bf16[448,2048]{1,0:T(8,128)(2,1)S(1)}, u32[]{:S(2)}, u32[]{:S(2)}) collective-permute-start(bf16[448,2048]{1,0:T(8,128)(2,1)S(1)} %own.1.refs_1_.refs_3_), channel_id=1, source_target_pairs={{0,2},{2,4},{3,1},{4,6},{5,3},{7,5},{8,10},{10,12},{11,9},{12,14},... | collective-permute-start | bytes 5505032 | tf_op jit(solution)/shard_map/ppermute | solution.py:370
  17.1 15.7 %collective-permute-start.1 = (bf16[224,512]{1,0:T(8,128)(2,1)S(1)}, bf16[224,512]{1,0:T(8,128)(2,1)S(1)}, u32[]{:S(2)}, u32[]{:S(2)}) collective-permute-start(bf16[224,512]{1,0:T(8,128)(2,1)S(1)} %get-tuple-element.44), channel_id=1, source_target_pairs={{0,8},{1,17},{2,10},{3,19},{4,12},{5,21},{6,14},{7,23},{8,0},{9,25... | collective-permute-start | bytes 688136 | tf_op jit(solution)/shard_map/ppermute | solution.py:356
  39.2 25.1 %collective-permute-start.9 = (bf16[448,2048]{1,0:T(8,128)(2,1)S(1)}, bf16[448,2048]{1,0:T(8,128)(2,1)S(1)}, u32[]{:S(2)}, u32[]{:S(2)}) collective-permute-start(bf16[448,2048]{1,0:T(8,128)(2,1)S(1)} %gate.3.refs_1_.refs_3_), channel_id=1, source_target_pairs={{2,4},{3,1},{4,6},{5,3},{10,12},{11,9},{12,14},{13,11},{18,20},{19... | collective-permute-start | bytes 5505032 | tf_op jit(solution)/shard_map/ppermute | solution.py:370
  49.9 14.1 %collective-permute-start.6 = (bf16[224,1280]{1,0:T(8,128)(2,1)S(1)}, bf16[224,1280]{1,0:T(8,128)(2,1)S(1)}, u32[]{:S(2)}, u32[]{:S(2)}) collective-permute-start(bf16[224,1280]{1,0:T(8,128)(2,1)S(1)} %pair.15.refs_3_.refs_0_), channel_id=1, source_target_pairs={{0,16},{1,9},{2,18},{3,11},{4,20},{5,13},{6,22},{7,15},{8,24},{9,1... | collective-permute-start | bytes 1720328 | tf_op jit(solution)/shard_map/ppermute | solution.py:356
  64.5 27.3 %collective-permute-start.16 = (bf16[448,2048]{1,0:T(8,128)(2,1)S(1)}, bf16[448,2048]{1,0:T(8,128)(2,1)S(1)}, u32[]{:S(2)}, u32[]{:S(2)}) collective-permute-start(bf16[448,2048]{1,0:T(8,128)(2,1)S(1)} %gate.4.refs_2_.refs_5_.refs_4_), channel_id=1, source_target_pairs={{3,1},{4,6},{11,9},{12,14},{19,17},{20,22},{27,25},{28,30}} | collective-permute-start | bytes 5505032 | tf_op jit(solution)/shard_map/ppermute | solution.py:370
  66.4 17.8 %collective-permute-start.8 = (bf16[224,1280]{1,0:T(8,128)(2,1)S(1)}, bf16[224,1280]{1,0:T(8,128)(2,1)S(1)}, u32[]{:S(2)}, u32[]{:S(2)}) collective-permute-start(bf16[224,1280]{1,0:T(8,128)(2,1)S(1)} %err.15.refs_2_.refs_1_), channel_id=1, source_target_pairs={{0,8},{1,17},{2,10},{3,19},{4,12},{5,21},{6,14},{7,23},{8,0},{9,25... | collective-permute-start | bytes 1720328 | tf_op jit(solution)/shard_map/ppermute | solution.py:356
  75.2 16.4 %collective-permute-start.13 = (bf16[224,1280]{1,0:T(8,128)(2,1)S(1)}, bf16[224,1280]{1,0:T(8,128)(2,1)S(1)}, u32[]{:S(2)}, u32[]{:S(2)}) collective-permute-start(bf16[224,1280]{1,0:T(8,128)(2,1)S(1)} %pair.17.refs_3_.refs_0_), channel_id=1, source_target_pairs={{0,16},{1,9},{2,18},{3,11},{4,20},{5,13},{6,22},{7,15},{8,24},{9,1... | collective-permute-start | bytes 1720328 | tf_op jit(solution)/shard_map/ppermute | solution.py:356
  76.8 13.0 %collective-permute-start.14 = (bf16[224,512]{1,0:T(8,128)(2,1)S(1)}, bf16[224,512]{1,0:T(8,128)(2,1)S(1)}, u32[]{:S(2)}, u32[]{:S(2)}) collective-permute-start(bf16[224,512]{1,0:T(8,128)(2,1)S(1)} %pair.16.refs_1_.refs_0_), channel_id=1, source_target_pairs={{0,16},{1,9},{2,18},{3,11},{4,20},{5,13},{6,22},{7,15},{8,24},{9,1... | collective-permute-start | bytes 688136 | tf_op jit(solution)/shard_map/ppermute | solution.py:356
  95.1 20.4 %collective-permute-start.15 = (bf16[224,1280]{1,0:T(8,128)(2,1)S(1)}, bf16[224,1280]{1,0:T(8,128)(2,1)S(1)}, u32[]{:S(2)}, u32[]{:S(2)}) collective-permute-start(bf16[224,1280]{1,0:T(8,128)(2,1)S(1)} %err.17.refs_1_), channel_id=1, source_target_pairs={{0,8},{1,17},{2,10},{3,19},{4,12},{5,21},{6,14},{7,23},{8,0},{9,25... | collective-permute-start | bytes 1720328 | tf_op jit(solution)/shard_map/ppermute | solution.py:356
  101.6 12.3 %collective-permute-start.19 = (bf16[224,512]{1,0:T(8,128)(2,1)S(1)}, bf16[224,512]{1,0:T(8,128)(2,1)S(1)}, u32[]{:S(2)}, u32[]{:S(2)}) collective-permute-start(bf16[224,512]{1,0:T(8,128)(2,1)S(1)} %get-tuple-element.55), channel_id=1, source_target_pairs={{0,8},{1,17},{2,10},{3,19},{4,12},{5,21},{6,14},{7,23},{8,0},{9,25... | collective-permute-start | bytes 688136 | tf_op jit(solution)/shard_map/ppermute | solution.py:356
  102.9 13.9 %collective-permute-start.24 = (bf16[224,512]{1,0:T(8,128)(2,1)S(1)}, bf16[224,512]{1,0:T(8,128)(2,1)S(1)}, u32[]{:S(2)}, u32[]{:S(2)}) collective-permute-start(bf16[224,512]{1,0:T(8,128)(2,1)S(1)} %pair.18.refs_2_.refs_0_), channel_id=1, source_target_pairs={{0,16},{1,9},{2,18},{3,11},{4,20},{5,13},{6,22},{7,15},{8,24},{9,1... | collective-permute-start | bytes 688136 | tf_op jit(solution)/shard_map/ppermute | solution.py:356
  107.2 26.3 %collective-permute-start.22 = (bf16[224,768]{1,0:T(8,128)(2,1)S(1)}, bf16[224,768]{1,0:T(8,128)(2,1)S(1)}, u32[]{:S(2)}, u32[]{:S(2)}) collective-permute-start(bf16[224,768]{1,0:T(8,128)(2,1)S(1)} %get-tuple-element.59), channel_id=1, source_target_pairs={{0,8},{1,17},{2,10},{3,19},{4,12},{5,21},{6,14},{7,23},{8,0},{9,25... | collective-permute-start | bytes 1032200 | tf_op jit(solution)/shard_map/ppermute | solution.py:356
  114.0 14.6 %collective-permute-start.26 = (bf16[224,512]{1,0:T(8,128)(2,1)S(1)}, bf16[224,512]{1,0:T(8,128)(2,1)S(1)}, u32[]{:S(2)}, u32[]{:S(2)}) collective-permute-start(bf16[224,512]{1,0:T(8,128)(2,1)S(1)} %pair.19.refs_3_.refs_0_), channel_id=1, source_target_pairs={{0,16},{1,9},{2,18},{3,11},{4,20},{5,13},{6,22},{7,15},{8,24},{9,1... | collective-permute-start | bytes 688136 | tf_op jit(solution)/shard_map/ppermute | solution.py:356
  117.1 14.9 %collective-permute-start.25 = (bf16[224,512]{1,0:T(8,128)(2,1)S(1)}, bf16[224,512]{1,0:T(8,128)(2,1)S(1)}, u32[]{:S(2)}, u32[]{:S(2)}) collective-permute-start(bf16[224,512]{1,0:T(8,128)(2,1)S(1)} %pair.21.refs_3_.refs_0_), channel_id=1, source_target_pairs={{0,16},{1,9},{2,18},{3,11},{4,20},{5,13},{6,22},{7,15},{8,24},{9,1... | collective-permute-start | bytes 688136 | tf_op jit(solution)/shard_map/ppermute | solution.py:356
  120.8 15.7 %collective-permute-start.31 = (bf16[224,768]{1,0:T(8,128)(2,1)S(1)}, bf16[224,768]{1,0:T(8,128)(2,1)S(1)}, u32[]{:S(2)}, u32[]{:S(2)}) collective-permute-start(bf16[224,768]{1,0:T(8,128)(2,1)S(1)} %get-tuple-element.62), channel_id=1, source_target_pairs={{0,8},{1,17},{2,10},{3,19},{4,12},{5,21},{6,14},{7,23},{8,0},{9,25... | collective-permute-start | bytes 1032200 | tf_op jit(solution)/shard_map/ppermute | solution.py:356
  132.0 24.3 %collective-permute-start.34 = (bf16[224,512]{1,0:T(8,128)(2,1)S(1)}, bf16[224,512]{1,0:T(8,128)(2,1)S(1)}, u32[]{:S(2)}, u32[]{:S(2)}) collective-permute-start(bf16[224,512]{1,0:T(8,128)(2,1)S(1)} %err.20.refs_2_.refs_1_), channel_id=1, source_target_pairs={{0,8},{1,17},{2,10},{3,19},{4,12},{5,21},{6,14},{7,23},{8,0},{9,25... | collective-permute-start | bytes 688136 | tf_op jit(solution)/shard_map/ppermute | solution.py:356
  133.5 22.1 %collective-permute-start.35 = (bf16[224,512]{1,0:T(8,128)(2,1)S(1)}, bf16[224,512]{1,0:T(8,128)(2,1)S(1)}, u32[]{:S(2)}, u32[]{:S(2)}) collective-permute-start(bf16[224,512]{1,0:T(8,128)(2,1)S(1)} %err.21.refs_2_.refs_1_), channel_id=1, source_target_pairs={{0,8},{1,17},{2,10},{3,19},{4,12},{5,21},{6,14},{7,23},{8,0},{9,25... | collective-permute-start | bytes 688136 | tf_op jit(solution)/shard_map/ppermute | solution.py:356
  134.3 20.4 %collective-permute-start.28 = (bf16[224,768]{1,0:T(8,128)(2,1)S(1)}, bf16[224,768]{1,0:T(8,128)(2,1)S(1)}, u32[]{:S(2)}, u32[]{:S(2)}) collective-permute-start(bf16[224,768]{1,0:T(8,128)(2,1)S(1)} %pair.22.refs_3_.refs_0_), channel_id=1, source_target_pairs={{0,16},{1,9},{2,18},{3,11},{4,20},{5,13},{6,22},{7,15},{8,24},{9,1... | collective-permute-start | bytes 1032200 | tf_op jit(solution)/shard_map/ppermute | solution.py:356
  136.7 20.2 %collective-permute-start.36 = (bf16[224,768]{1,0:T(8,128)(2,1)S(1)}, bf16[224,768]{1,0:T(8,128)(2,1)S(1)}, u32[]{:S(2)}, u32[]{:S(2)}) collective-permute-start(bf16[224,768]{1,0:T(8,128)(2,1)S(1)} %pair.23.refs_3_.refs_0_), channel_id=1, source_target_pairs={{0,16},{1,9},{2,18},{3,11},{4,20},{5,13},{6,22},{7,15},{8,24},{9,1... | collective-permute-start | bytes 1032200 | tf_op jit(solution)/shard_map/ppermute | solution.py:356
  153.3 21.1 %collective-permute-start.33 = (bf16[896,512]{1,0:T(8,128)(2,1)S(1)}, bf16[896,512]{1,0:T(8,128)(2,1)S(1)}, u32[]{:S(2)}, u32[]{:S(2)}) collective-permute-start(bf16[896,512]{1,0:T(8,128)(2,1)S(1)} %get-tuple-element.65), channel_id=1, source_target_pairs={{0,8},{1,17},{2,10},{3,19},{4,12},{5,21},{6,14},{7,23},{8,0},{9,25... | collective-permute-start | bytes 2752520 | tf_op jit(solution)/shard_map/ppermute | solution.py:356
  154.9 21.2 %collective-permute-start.32 = (bf16[224,768]{1,0:T(8,128)(2,1)S(1)}, bf16[224,768]{1,0:T(8,128)(2,1)S(1)}, u32[]{:S(2)}, u32[]{:S(2)}) collective-permute-start(bf16[224,768]{1,0:T(8,128)(2,1)S(1)} %err.22.refs_3_.refs_1_), channel_id=1, source_target_pairs={{0,8},{1,17},{2,10},{3,19},{4,12},{5,21},{6,14},{7,23},{8,0},{9,25... | collective-permute-start | bytes 1032200 | tf_op jit(solution)/shard_map/ppermute | solution.py:356
  157.0 19.7 %collective-permute-start.37 = (bf16[224,768]{1,0:T(8,128)(2,1)S(1)}, bf16[224,768]{1,0:T(8,128)(2,1)S(1)}, u32[]{:S(2)}, u32[]{:S(2)}) collective-permute-start(bf16[224,768]{1,0:T(8,128)(2,1)S(1)} %err.23.refs_12_.refs_1_), channel_id=1, source_target_pairs={{0,8},{1,17},{2,10},{3,19},{4,12},{5,21},{6,14},{7,23},{8,0},{9,25... | collective-permute-start | bytes 1032200 | tf_op jit(solution)/shard_map/ppermute | solution.py:356
  173.7 20.9 %collective-permute-start.39 = (bf16[896,512]{1,0:T(8,128)(2,1)S(1)}, bf16[896,512]{1,0:T(8,128)(2,1)S(1)}, u32[]{:S(2)}, u32[]{:S(2)}) collective-permute-start(bf16[896,512]{1,0:T(8,128)(2,1)S(1)} %get-tuple-element.68), channel_id=1, source_target_pairs={{0,8},{1,17},{2,10},{3,19},{4,12},{5,21},{6,14},{7,23},{8,0},{9,25... | collective-permute-start | bytes 2752520 | tf_op jit(solution)/shard_map/ppermute | solution.py:356
  174.8 22.8 %collective-permute-start.38 = (bf16[896,512]{1,0:T(8,128)(2,1)S(1)}, bf16[896,512]{1,0:T(8,128)(2,1)S(1)}, u32[]{:S(2)}, u32[]{:S(2)}) collective-permute-start(bf16[896,512]{1,0:T(8,128)(2,1)S(1)} %pair.24.refs_3_.refs_0_), channel_id=1, source_target_pairs={{0,16},{1,9},{2,18},{3,11},{4,20},{5,13},{6,22},{7,15},{8,24},{9,1... | collective-permute-start | bytes 2752520 | tf_op jit(solution)/shard_map/ppermute | solution.py:356
  192.7 23.4 %collective-permute-start.42 = (bf16[896,512]{1,0:T(8,128)(2,1)S(1)}, bf16[896,512]{1,0:T(8,128)(2,1)S(1)}, u32[]{:S(2)}, u32[]{:S(2)}) collective-permute-start(bf16[896,512]{1,0:T(8,128)(2,1)S(1)} %get-tuple-element.72), channel_id=1, source_target_pairs={{0,8},{1,17},{2,10},{3,19},{4,12},{5,21},{6,14},{7,23},{8,0},{9,25... | collective-permute-start | bytes 2752520 | tf_op jit(solution)/shard_map/ppermute | solution.py:356
  195.0 23.9 %collective-permute-start.41 = (bf16[896,512]{1,0:T(8,128)(2,1)S(1)}, bf16[896,512]{1,0:T(8,128)(2,1)S(1)}, u32[]{:S(2)}, u32[]{:S(2)}) collective-permute-start(bf16[896,512]{1,0:T(8,128)(2,1)S(1)} %pair.25.refs_2_.refs_0_), channel_id=1, source_target_pairs={{0,16},{1,9},{2,18},{3,11},{4,20},{5,13},{6,22},{7,15},{8,24},{9,1... | collective-permute-start | bytes 2752520 | tf_op jit(solution)/shard_map/ppermute | solution.py:356
  198.0 40.6 %collective-permute-start.46 = (bf16[896,512]{1,0:T(8,128)(2,1)S(1)}, bf16[896,512]{1,0:T(8,128)(2,1)S(1)}, u32[]{:S(2)}, u32[]{:S(2)}) collective-permute-start(bf16[896,512]{1,0:T(8,128)(2,1)S(1)} %err.24.refs_12_.refs_1_), channel_id=1, source_target_pairs={{0,8},{1,17},{2,10},{3,19},{4,12},{5,21},{6,14},{7,23},{8,0},{9,25... | collective-permute-start | bytes 2752520 | tf_op jit(solution)/shard_map/ppermute | solution.py:356
  208.8 29.6 %collective-permute-start.40 = (bf16[896,256]{1,0:T(8,128)(2,1)S(1)}, bf16[896,256]{1,0:T(8,128)(2,1)S(1)}, u32[]{:S(2)}, u32[]{:S(2)}) collective-permute-start(bf16[896,256]{1,0:T(8,128)(2,1)S(1)} %get-tuple-element.71), channel_id=1, source_target_pairs={{0,8},{1,17},{2,10},{3,19},{4,12},{5,21},{6,14},{7,23},{8,0},{9,25... | collective-permute-start | bytes 1376264 | tf_op jit(solution)/shard_map/ppermute | solution.py:356
  216.4 32.3 %collective-permute-start.45 = (bf16[896,512]{1,0:T(8,128)(2,1)S(1)}, bf16[896,512]{1,0:T(8,128)(2,1)S(1)}, u32[]{:S(2)}, u32[]{:S(2)}) collective-permute-start(bf16[896,512]{1,0:T(8,128)(2,1)S(1)} %pair.26.refs_2_.refs_0_), channel_id=1, source_target_pairs={{0,16},{1,9},{2,18},{3,11},{4,20},{5,13},{6,22},{7,15},{8,24},{9,1... | collective-permute-start | bytes 2752520 | tf_op jit(solution)/shard_map/ppermute | solution.py:356
  219.3 32.6 %collective-permute-start.44 = (bf16[896,512]{1,0:T(8,128)(2,1)S(1)}, bf16[896,512]{1,0:T(8,128)(2,1)S(1)}, u32[]{:S(2)}, u32[]{:S(2)}) collective-permute-start(bf16[896,512]{1,0:T(8,128)(2,1)S(1)} %err.25.refs_2_.refs_1_), channel_id=1, source_target_pairs={{0,8},{1,17},{2,10},{3,19},{4,12},{5,21},{6,14},{7,23},{8,0},{9,25... | collective-permute-start | bytes 2752520 | tf_op jit(solution)/shard_map/ppermute | solution.py:356
  249.1 15.9 %collective-permute-start.48 = (bf16[896,512]{1,0:T(8,128)(2,1)S(1)}, bf16[896,512]{1,0:T(8,128)(2,1)S(1)}, u32[]{:S(2)}, u32[]{:S(2)}) collective-permute-start(bf16[896,512]{1,0:T(8,128)(2,1)S(1)} %err.26.refs_3_.refs_1_), channel_id=1, source_target_pairs={{0,8},{1,17},{2,10},{3,19},{4,12},{5,21},{6,14},{7,23},{8,0},{9,25... | collective-permute-start | bytes 2752520 | tf_op jit(solution)/shard_map/ppermute | solution.py:356
  250.3 13.5 %collective-permute-start.43 = (bf16[896,256]{1,0:T(8,128)(2,1)S(1)}, bf16[896,256]{1,0:T(8,128)(2,1)S(1)}, u32[]{:S(2)}, u32[]{:S(2)}) collective-permute-start(bf16[896,256]{1,0:T(8,128)(2,1)S(1)} %pair.27.refs_3_.refs_0_), channel_id=1, source_target_pairs={{0,16},{1,9},{2,18},{3,11},{4,20},{5,13},{6,22},{7,15},{8,24},{9,1... | collective-permute-start | bytes 1376264 | tf_op jit(solution)/shard_map/ppermute | solution.py:356
  (25 other events, 202.8 us)

commit v4 on v3

--- a/solution.py
+++ b/solution.py
@@ -378,7 +378,7 @@
 GROUPS = [512, 512, 512, 256]
 ORDER = [
     "D0", "K0", "Fo0", "D1", "Po0", "Fo1", "Eo0", "G1", "K1", "Po1", "Fn0", "Fn1", "Ro0", "Eo1", "Pn0", "G2",
-    "K2", "Pn1", "Fm0", "Ro1", "En0", "Fm1", "En1", "G3", "Fm2", "Rn0", "K3", "Ff0", "Pm0", "Pm1", "Ff1", "Pf0",
+    "K2", "Pn1", "Fm0", "Fm1", "Ro1", "En0", "En1", "G3", "Fm2", "Rn0", "K3", "Ff0", "Pm0", "Pm1", "Ff1", "Pf0",
     "Rn1", "Em0", "Pf1", "Ff2", "Ef0", "Em1", "Ef1", "Pm2", "Rm0", "Pf2", "Rf0", "B0", "Em2", "Rf1", "Rm1", "Ef2",
     "B1", "Ps0", "Rm2", "Rf2", "B2", "Ps1", "Es0", "B3", "Ps2", "Es1", "Ps3", "Rs0", "L0", "Es2", "Rs1", "L1",
     "Es3", "Rs2", "L2", "Rs3", "L3",

time: 281 us -> 280 us (level)
  transfers between devices with their start and end apart: 49 -> 49, of which waited for: 17 -> 17; matrix products, arithmetic and copies ran while one was open for 1% -> 1% of each run, Pallas kernels for 49% -> 50%
where the time goes in v4:
time: 280 us; the launch traced here: 279 us
  Pallas kernels  146 us (52%)
  waiting for transfers between devices  72.3 us (26%)
  starting transfers between devices  56.6 us (20%)
  local copies, waits for them, and re-layouts  3.34 us (1%)
    pallas_call x69, Pallas kernels, call(): pl.pallas_call(wrapped, grid=grid, in_specs=list(in_specs) + [ANY] * len(...  146 us
    ppermute x42, waiting for transfers between devices, swap_loop(): return lax.ppermute(a, ('loop', 'dp'), pairs)  69 us
    ppermute x42, starting transfers between devices, swap_loop(): return lax.ppermute(a, ('loop', 'dp'), pairs)  49.7 us
    ppermute x3, starting transfers between devices, spread(): return lax.ppermute(a, 'dp', pairs)  6.15 us
  transfers between devices with their start and end apart: 49, of which 17 were waited for; matrix products, arithmetic and copies ran while one was open for 1% of the time, Pallas kernels for 50%

profile of v4, /device:TPU:0, one launch (start us, length us, event | category | flops | bytes accessed | tf_op | source)
XLA Modules:
  0.0 279.3 jit_solution(7888909543594291831)
XLA Ops:
  3.1 6.7 %delta.2 = (bf16[2048,512]{1,0:T(8,128)(2,1)S(1)}, bf16[2048,512]{1,0:T(8,128)(2,1)}) custom-call(s32[1,1792]{1,0:T(1,128)S(1)} %broadcast_in_dim.9.refs_0_.refs_6_.refs_3_, s32[1,1792]{1,0:T(1,128)S(1)} %broadcast_in_dim.10.refs_1_.refs_7_.refs_4_, f32[32,1,1792]{2,1,0:T(1,128)S(1)} %broadcast_in_dim_reshape.4.refs_2_.refs_8_.refs_5_, ...), custom_call_target="tpu_custom_call" | custom-call | flops 4499999744 | bytes 1024 | tf_op jit(solution)/shard_map/delta/pallas_call | solution.py:79
  10.8 4.6 %collective-permute-start.3 = (bf16[448,2048]{1,0:T(8,128)(2,1)S(1)}, bf16[448,2048]{1,0:T(8,128)(2,1)S(1)}, u32[]{:S(2)}, u32[]{:S(2)}) collective-permute-start(bf16[448,2048]{1,0:T(8,128)(2,1)S(1)} %own.1.refs_1_.refs_3_), channel_id=1, source_target_pairs={{0,2},{2,4},{3,1},{4,6},{5,3},{7,5},{8,10},{10,12},{11,9},{12,14},... | collective-permute-start | bytes 5505032 | tf_op jit(solution)/shard_map/ppermute | solution.py:370
  15.4 1.7 forward.10
  18.6 14.2 %delta.3 = (bf16[2048,1280]{1,0:T(8,128)(2,1)S(1)}, bf16[2048,1280]{1,0:T(8,128)(2,1)}) custom-call(s32[1,1792]{1,0:T(1,128)S(1)} %broadcast_in_dim.9.refs_0_.refs_6_.refs_3_, s32[1,1792]{1,0:T(1,128)S(1)} %broadcast_in_dim.10.refs_1_.refs_7_.refs_4_, f32[32,1,1792]{2,1,0:T(1,128)S(1)} %broadcast_in_dim_reshape.4.refs_2_.refs_8_.refs_5_, ...), custom_call_target="tpu_custom_call" | custom-call | flops 11249999872 | bytes 1024 | tf_op jit(solution)/shard_map/delta/pallas_call | solution.py:79
  34.5 3.1 %forward.11 = (bf16[224,1280]{1,0:T(8,128)(2,1)S(1)}, bf16[224,1280]{1,0:T(8,128)(2,1)S(1)}) custom-call(s32[3]{0:T(128)S(1)} %pad_add_fusion.refs_0_, bf16[448,2048]{1,0:T(8,128)(2,1)S(1)} %own.1.refs_1_.refs_3_, bf16[2048,1280]{1,0:T(8,128)(2,1)S(1)} %get-tuple-element.43.refs_2_, bf16[224,512]{1,0:T(8,128)(2,1)S(1)} %pair.14.refs_3_.refs_0_), custom_call_target="tpu_custom_call" | custom-call | flops 3375000064 | bytes 1024 | tf_op jit(solution)/shard_map/forward/pallas_call | solution.py:79
  40.6 2.4 collective-permute-done.5.refs_2_.refs_3_
  43.7 6.0 %collective-permute-done.2.refs_1_ = bf16[224,1280]{1,0:T(8,128)(2,1)S(1)} collective-permute-done((bf16[224,1280]{1,0:T(8,128)(2,1)S(1)}, bf16[224,1280]{1,0:T(8,128)(2,1)S(1)}, u32[]{:S(2)}, u32[]{:S(2)}) %collective-permute-start.2) | collective-permute-done | bytes 573472 | tf_op jit(solution)/shard_map/ppermute | solution.py:356
  55.3 3.1 %forward.13 = (bf16[224,1280]{1,0:T(8,128)(2,1)S(1)}, bf16[224,1280]{1,0:T(8,128)(2,1)S(1)}) custom-call(s32[3]{0:T(128)S(1)} %pad_add_fusion.refs_0_, bf16[448,2048]{1,0:T(8,128)(2,1)S(1)} %near.1.refs_2_.refs_1_, bf16[2048,1280]{1,0:T(8,128)(2,1)S(1)} %get-tuple-element.43.refs_2_, bf16[224,512]{1,0:T(8,128)(2,1)S(1)} %get-tuple-element.47.refs_3_.refs_0_), custom_call_target="tpu_custom_call" | custom-call | flops 3375000064 | bytes 1024 | tf_op jit(solution)/shard_map/forward/pallas_call | solution.py:79
  58.4 1.7 collective-permute-done.7.refs_2_
  60.7 3.3 %collective-permute-done.6.refs_1_ = bf16[224,1280]{1,0:T(8,128)(2,1)S(1)} collective-permute-done((bf16[224,1280]{1,0:T(8,128)(2,1)S(1)}, bf16[224,1280]{1,0:T(8,128)(2,1)S(1)}, u32[]{:S(2)}, u32[]{:S(2)}) %collective-permute-start.6) | collective-permute-done | bytes 573472 | tf_op jit(solution)/shard_map/ppermute | solution.py:356
  69.2 5.9 %collective-permute-done.12.refs_1_ = bf16[224,1280]{1,0:T(8,128)(2,1)S(1)} collective-permute-done((bf16[224,1280]{1,0:T(8,128)(2,1)S(1)}, bf16[224,1280]{1,0:T(8,128)(2,1)S(1)}, u32[]{:S(2)}, u32[]{:S(2)}) %collective-permute-start.12) | collective-permute-done | bytes 573472 | tf_op jit(solution)/shard_map/ppermute | solution.py:356
  78.9 1.7 forward.15
  80.6 3.7 %collective-permute-done.8.refs_2_ = bf16[224,1280]{1,0:T(8,128)(2,1)S(1)} collective-permute-done((bf16[224,1280]{1,0:T(8,128)(2,1)S(1)}, bf16[224,1280]{1,0:T(8,128)(2,1)S(1)}, u32[]{:S(2)}, u32[]{:S(2)}) %collective-permute-start.8) | collective-permute-done | bytes 573472 | tf_op jit(solution)/shard_map/ppermute | solution.py:356
  84.9 4.9 %collective-permute-done.14.refs_1_ = bf16[224,512]{1,0:T(8,128)(2,1)S(1)} collective-permute-done((bf16[224,512]{1,0:T(8,128)(2,1)S(1)}, bf16[224,512]{1,0:T(8,128)(2,1)S(1)}, u32[]{:S(2)}, u32[]{:S(2)}) %collective-permute-start.14) | collective-permute-done | bytes 229408 | tf_op jit(solution)/shard_map/ppermute | solution.py:356
  94.4 2.1 forward.16
  102.9 1.7 forward.18
  106.7 5.6 %collective-permute-done.19.refs_1_ = bf16[224,512]{1,0:T(8,128)(2,1)S(1)} collective-permute-done((bf16[224,512]{1,0:T(8,128)(2,1)S(1)}, bf16[224,512]{1,0:T(8,128)(2,1)S(1)}, u32[]{:S(2)}, u32[]{:S(2)}) %collective-permute-start.19) | collective-permute-done | bytes 229408 | tf_op jit(solution)/shard_map/ppermute | solution.py:356
  117.0 2.1 forward.19
  120.3 5.1 %collective-permute-done.27.refs_1_ = bf16[224,512]{1,0:T(8,128)(2,1)S(1)} collective-permute-done((bf16[224,512]{1,0:T(8,128)(2,1)S(1)}, bf16[224,512]{1,0:T(8,128)(2,1)S(1)}, u32[]{:S(2)}, u32[]{:S(2)}) %collective-permute-start.27) | collective-permute-done | bytes 229408 | tf_op jit(solution)/shard_map/ppermute | solution.py:356
  127.7 2.6 collective-permute-done.25.refs_1_
  136.5 15.2 %backward_forward.4 = (bf16[2048,512]{1,0:T(8,128)(2,1)}, bf16[896,512]{1,0:T(8,128)(2,1)S(1)}, bf16[896,512]{1,0:T(8,128)(2,1)S(1)}) custom-call(s32[3]{0:T(128)S(1)} %pad_add_fusion.refs_0_, bf16[448,512]{1,0:T(8,128)(2,1)S(1)} %join.14.refs_2_.refs_1_, bf16[448,512]{1,0:T(8,128)(2,1)S(1)} %join.16.refs_8_.refs_2_, ...), custom_call_target="tpu_custom_call" | custom-call | flops 14499999744 | bytes 1024 | tf_op jit(solution)/shard_map/backward_forward/pallas_call | solution.py:79
  156.8 15.2 %backward_forward.5 = (bf16[2048,512]{1,0:T(8,128)(2,1)}, bf16[896,512]{1,0:T(8,128)(2,1)S(1)}, bf16[896,512]{1,0:T(8,128)(2,1)S(1)}) custom-call(s32[3]{0:T(128)S(1)} %pad_add_fusion.refs_0_, bf16[448,1280]{1,0:T(8,128)(2,1)S(1)} %join.15.refs_2_.refs_1_, bf16[448,1280]{1,0:T(8,128)(2,1)S(1)} %join.17.refs_2_, bf16[448,512]{1,0:T(8,128)(2,1)S(1)} %join.21.refs_2_.refs_3_, ...), custom_call_target="tpu_custom_call" | custom-call | flops 14499999744 | bytes 1024 | tf_op jit(solution)/shard_map/backward_forward/pallas_call | solution.py:79
  175.8 15.2 %backward_forward.6 = (bf16[2048,512]{1,0:T(8,128)(2,1)}, bf16[896,512]{1,0:T(8,128)(2,1)S(1)}, bf16[896,512]{1,0:T(8,128)(2,1)S(1)}) custom-call(s32[3]{0:T(128)S(1)} %pad_add_fusion.refs_0_, bf16[448,1280]{1,0:T(8,128)(2,1)S(1)} %join.15.refs_2_.refs_1_, bf16[448,1280]{1,0:T(8,128)(2,1)S(1)} %join.17.refs_2_, bf16[448,768]{1,0:T(8,128)(2,1)S(1)} %join.22.refs_3_, ...), custom_call_target="tpu_custom_call" | custom-call | flops 14499999744 | bytes 1024 | tf_op jit(solution)/shard_map/backward_forward/pallas_call | solution.py:79
  193.3 2.6 collective-permute-start.41
  197.8 9.3 %backward_forward.7 = (bf16[2048,256]{1,0:T(8,128)(2,1)}, bf16[896,256]{1,0:T(8,128)(2,1)S(1)}, bf16[896,256]{1,0:T(8,128)(2,1)S(1)}) custom-call(s32[3]{0:T(128)S(1)} %pad_add_fusion.refs_0_, bf16[448,1280]{1,0:T(8,128)(2,1)S(1)} %join.15.refs_2_.refs_1_, bf16[448,1280]{1,0:T(8,128)(2,1)S(1)} %join.17.refs_2_, bf16[448,768]{1,0:T(8,128)(2,1)S(1)} %join.22.refs_3_, ...), custom_call_target="tpu_custom_call" | custom-call | flops 7249999872 | bytes 1024 | tf_op jit(solution)/shard_map/backward_forward/pallas_call | solution.py:79
  207.8 6.5 %collective-permute-done.42.refs_1_ = bf16[896,512]{1,0:T(8,128)(2,1)S(1)} collective-permute-done((bf16[896,512]{1,0:T(8,128)(2,1)S(1)}, bf16[896,512]{1,0:T(8,128)(2,1)S(1)}, u32[]{:S(2)}, u32[]{:S(2)}) %collective-permute-start.42) | collective-permute-done | bytes 917536 | tf_op jit(solution)/shard_map/ppermute | solution.py:356
  219.1 17.6 %collective-permute-done.40.refs_1_ = bf16[896,256]{1,0:T(8,128)(2,1)S(1)} collective-permute-done((bf16[896,256]{1,0:T(8,128)(2,1)S(1)}, bf16[896,256]{1,0:T(8,128)(2,1)S(1)}, u32[]{:S(2)}, u32[]{:S(2)}) %collective-permute-start.40) | collective-permute-done | bytes 458784 | tf_op jit(solution)/shard_map/ppermute | solution.py:356
  238.5 8.5 %backward_last.4.refs_2_.refs_8_ = f32[2048,1792]{1,0:T(8,128)} custom-call(s32[3]{0:T(128)S(1)} %pad_add_fusion.refs_0_, bf16[1792,512]{1,0:T(8,128)(2,1)S(1)} %join.24.refs_1_, bf16[1792,2048]{1,0:T(8,128)(2,1)S(1)} %all_tokens.1.refs_1_.refs_3_.refs_5_.refs_2_, s32[1,1792]{1,0:T(1,128)S(1)} %broadcast_in_dim.9.refs_0_.refs_6_.refs_3_, ...), custom_call_target="tpu_custom_call" | custom-call | flops 7000000000 | bytes 1024 | tf_op jit(solution)/shard_map/backward_last/pallas_call | solution.py:79
  251.0 8.6 %backward_last.5.refs_2_.refs_8_ = f32[2048,1792]{1,0:T(8,128)} custom-call(s32[3]{0:T(128)S(1)} %pad_add_fusion.refs_0_, bf16[1792,512]{1,0:T(8,128)(2,1)S(1)} %join.25.refs_1_, bf16[1792,2048]{1,0:T(8,128)(2,1)S(1)} %all_tokens.1.refs_1_.refs_3_.refs_5_.refs_2_, ...), custom_call_target="tpu_custom_call", output_to_operand_aliasing={{}: (8, {})} | custom-call | flops 7000000000 | bytes 1024 | tf_op jit(solution)/shard_map/backward_last/pallas_call | solution.py:79
  259.6 2.5 collective-permute-done.43.refs_1_
  264.2 8.6 %backward_last.6.refs_3_.refs_8_ = f32[2048,1792]{1,0:T(8,128)} custom-call(s32[3]{0:T(128)S(1)} %pad_add_fusion.refs_0_, bf16[1792,512]{1,0:T(8,128)(2,1)S(1)} %join.26.refs_1_, bf16[1792,2048]{1,0:T(8,128)(2,1)S(1)} %all_tokens.1.refs_1_.refs_3_.refs_5_.refs_2_, ...), custom_call_target="tpu_custom_call", output_to_operand_aliasing={{}: (8, {})} | custom-call | flops 7000000000 | bytes 1024 | tf_op jit(solution)/shard_map/backward_last/pallas_call | solution.py:79
  274.0 5.3 %backward_last.7 = f32[2048,1792]{1,0:T(8,128)} custom-call(s32[3]{0:T(128)S(1)} %pad_add_fusion.refs_0_, bf16[1792,256]{1,0:T(8,128)(2,1)S(1)} %join.27.refs_1_, bf16[1792,2048]{1,0:T(8,128)(2,1)S(1)} %all_tokens.1.refs_1_.refs_3_.refs_5_.refs_2_, s32[1,1792]{1,0:T(1,128)S(1)} %broadcast_in_dim.9.refs_0_.refs_6_.refs_3_, ...), custom_call_target="tpu_custom_call", output_to_operand_aliasing={{}: (8, {})} | custom-call | flops 3500000000 | bytes 1024 | tf_op jit(solution)/shard_map/backward_last/pallas_call | solution.py:79
  (158 shorter events, 81.3 us)
Async XLA Ops:
  10.8 28.3 %collective-permute-start.3 = (bf16[448,2048]{1,0:T(8,128)(2,1)S(1)}, bf16[448,2048]{1,0:T(8,128)(2,1)S(1)}, u32[]{:S(2)}, u32[]{:S(2)}) collective-permute-start(bf16[448,2048]{1,0:T(8,128)(2,1)S(1)} %own.1.refs_1_.refs_3_), channel_id=1, source_target_pairs={{0,2},{2,4},{3,1},{4,6},{5,3},{7,5},{8,10},{10,12},{11,9},{12,14},... | collective-permute-start | bytes 5505032 | tf_op jit(solution)/shard_map/ppermute | solution.py:370
  17.1 15.7 %collective-permute-start.1 = (bf16[224,512]{1,0:T(8,128)(2,1)S(1)}, bf16[224,512]{1,0:T(8,128)(2,1)S(1)}, u32[]{:S(2)}, u32[]{:S(2)}) collective-permute-start(bf16[224,512]{1,0:T(8,128)(2,1)S(1)} %get-tuple-element.44), channel_id=1, source_target_pairs={{0,8},{1,17},{2,10},{3,19},{4,12},{5,21},{6,14},{7,23},{8,0},{9,25... | collective-permute-start | bytes 688136 | tf_op jit(solution)/shard_map/ppermute | solution.py:356
  39.2 25.1 %collective-permute-start.9 = (bf16[448,2048]{1,0:T(8,128)(2,1)S(1)}, bf16[448,2048]{1,0:T(8,128)(2,1)S(1)}, u32[]{:S(2)}, u32[]{:S(2)}) collective-permute-start(bf16[448,2048]{1,0:T(8,128)(2,1)S(1)} %gate.3.refs_1_.refs_3_), channel_id=1, source_target_pairs={{2,4},{3,1},{4,6},{5,3},{10,12},{11,9},{12,14},{13,11},{18,20},{19... | collective-permute-start | bytes 5505032 | tf_op jit(solution)/shard_map/ppermute | solution.py:370
  49.9 14.1 %collective-permute-start.6 = (bf16[224,1280]{1,0:T(8,128)(2,1)S(1)}, bf16[224,1280]{1,0:T(8,128)(2,1)S(1)}, u32[]{:S(2)}, u32[]{:S(2)}) collective-permute-start(bf16[224,1280]{1,0:T(8,128)(2,1)S(1)} %pair.15.refs_3_.refs_0_), channel_id=1, source_target_pairs={{0,16},{1,9},{2,18},{3,11},{4,20},{5,13},{6,22},{7,15},{8,24},{9,1... | collective-permute-start | bytes 1720328 | tf_op jit(solution)/shard_map/ppermute | solution.py:356
  64.5 25.7 %collective-permute-start.16 = (bf16[448,2048]{1,0:T(8,128)(2,1)S(1)}, bf16[448,2048]{1,0:T(8,128)(2,1)S(1)}, u32[]{:S(2)}, u32[]{:S(2)}) collective-permute-start(bf16[448,2048]{1,0:T(8,128)(2,1)S(1)} %gate.4.refs_2_.refs_5_.refs_4_), channel_id=1, source_target_pairs={{3,1},{4,6},{11,9},{12,14},{19,17},{20,22},{27,25},{28,30}} | collective-permute-start | bytes 5505032 | tf_op jit(solution)/shard_map/ppermute | solution.py:370
  66.4 17.8 %collective-permute-start.8 = (bf16[224,1280]{1,0:T(8,128)(2,1)S(1)}, bf16[224,1280]{1,0:T(8,128)(2,1)S(1)}, u32[]{:S(2)}, u32[]{:S(2)}) collective-permute-start(bf16[224,1280]{1,0:T(8,128)(2,1)S(1)} %err.15.refs_2_.refs_1_), channel_id=1, source_target_pairs={{0,8},{1,17},{2,10},{3,19},{4,12},{5,21},{6,14},{7,23},{8,0},{9,25... | collective-permute-start | bytes 1720328 | tf_op jit(solution)/shard_map/ppermute | solution.py:356
  75.2 14.7 %collective-permute-start.13 = (bf16[224,1280]{1,0:T(8,128)(2,1)S(1)}, bf16[224,1280]{1,0:T(8,128)(2,1)S(1)}, u32[]{:S(2)}, u32[]{:S(2)}) collective-permute-start(bf16[224,1280]{1,0:T(8,128)(2,1)S(1)} %pair.17.refs_3_.refs_0_), channel_id=1, source_target_pairs={{0,16},{1,9},{2,18},{3,11},{4,20},{5,13},{6,22},{7,15},{8,24},{9,1... | collective-permute-start | bytes 1720328 | tf_op jit(solution)/shard_map/ppermute | solution.py:356
  76.8 13.0 %collective-permute-start.14 = (bf16[224,512]{1,0:T(8,128)(2,1)S(1)}, bf16[224,512]{1,0:T(8,128)(2,1)S(1)}, u32[]{:S(2)}, u32[]{:S(2)}) collective-permute-start(bf16[224,512]{1,0:T(8,128)(2,1)S(1)} %pair.16.refs_1_.refs_0_), channel_id=1, source_target_pairs={{0,16},{1,9},{2,18},{3,11},{4,20},{5,13},{6,22},{7,15},{8,24},{9,1... | collective-permute-start | bytes 688136 | tf_op jit(solution)/shard_map/ppermute | solution.py:356
  93.5 20.4 %collective-permute-start.15 = (bf16[224,1280]{1,0:T(8,128)(2,1)S(1)}, bf16[224,1280]{1,0:T(8,128)(2,1)S(1)}, u32[]{:S(2)}, u32[]{:S(2)}) collective-permute-start(bf16[224,1280]{1,0:T(8,128)(2,1)S(1)} %err.17.refs_1_), channel_id=1, source_target_pairs={{0,8},{1,17},{2,10},{3,19},{4,12},{5,21},{6,14},{7,23},{8,0},{9,25... | collective-permute-start | bytes 1720328 | tf_op jit(solution)/shard_map/ppermute | solution.py:356
  100.0 12.3 %collective-permute-start.19 = (bf16[224,512]{1,0:T(8,128)(2,1)S(1)}, bf16[224,512]{1,0:T(8,128)(2,1)S(1)}, u32[]{:S(2)}, u32[]{:S(2)}) collective-permute-start(bf16[224,512]{1,0:T(8,128)(2,1)S(1)} %get-tuple-element.55), channel_id=1, source_target_pairs={{0,8},{1,17},{2,10},{3,19},{4,12},{5,21},{6,14},{7,23},{8,0},{9,25... | collective-permute-start | bytes 688136 | tf_op jit(solution)/shard_map/ppermute | solution.py:356
  101.3 13.9 %collective-permute-start.24 = (bf16[224,512]{1,0:T(8,128)(2,1)S(1)}, bf16[224,512]{1,0:T(8,128)(2,1)S(1)}, u32[]{:S(2)}, u32[]{:S(2)}) collective-permute-start(bf16[224,512]{1,0:T(8,128)(2,1)S(1)} %pair.18.refs_2_.refs_0_), channel_id=1, source_target_pairs={{0,16},{1,9},{2,18},{3,11},{4,20},{5,13},{6,22},{7,15},{8,24},{9,1... | collective-permute-start | bytes 688136 | tf_op jit(solution)/shard_map/ppermute | solution.py:356
  105.6 26.3 %collective-permute-start.22 = (bf16[224,768]{1,0:T(8,128)(2,1)S(1)}, bf16[224,768]{1,0:T(8,128)(2,1)S(1)}, u32[]{:S(2)}, u32[]{:S(2)}) collective-permute-start(bf16[224,768]{1,0:T(8,128)(2,1)S(1)} %get-tuple-element.59), channel_id=1, source_target_pairs={{0,8},{1,17},{2,10},{3,19},{4,12},{5,21},{6,14},{7,23},{8,0},{9,25... | collective-permute-start | bytes 1032200 | tf_op jit(solution)/shard_map/ppermute | solution.py:356
  112.3 14.6 %collective-permute-start.26 = (bf16[224,512]{1,0:T(8,128)(2,1)S(1)}, bf16[224,512]{1,0:T(8,128)(2,1)S(1)}, u32[]{:S(2)}, u32[]{:S(2)}) collective-permute-start(bf16[224,512]{1,0:T(8,128)(2,1)S(1)} %pair.19.refs_3_.refs_0_), channel_id=1, source_target_pairs={{0,16},{1,9},{2,18},{3,11},{4,20},{5,13},{6,22},{7,15},{8,24},{9,1... | collective-permute-start | bytes 688136 | tf_op jit(solution)/shard_map/ppermute | solution.py:356
  115.4 14.9 %collective-permute-start.25 = (bf16[224,512]{1,0:T(8,128)(2,1)S(1)}, bf16[224,512]{1,0:T(8,128)(2,1)S(1)}, u32[]{:S(2)}, u32[]{:S(2)}) collective-permute-start(bf16[224,512]{1,0:T(8,128)(2,1)S(1)} %pair.21.refs_3_.refs_0_), channel_id=1, source_target_pairs={{0,16},{1,9},{2,18},{3,11},{4,20},{5,13},{6,22},{7,15},{8,24},{9,1... | collective-permute-start | bytes 688136 | tf_op jit(solution)/shard_map/ppermute | solution.py:356
  119.1 15.7 %collective-permute-start.31 = (bf16[224,768]{1,0:T(8,128)(2,1)S(1)}, bf16[224,768]{1,0:T(8,128)(2,1)S(1)}, u32[]{:S(2)}, u32[]{:S(2)}) collective-permute-start(bf16[224,768]{1,0:T(8,128)(2,1)S(1)} %get-tuple-element.62), channel_id=1, source_target_pairs={{0,8},{1,17},{2,10},{3,19},{4,12},{5,21},{6,14},{7,23},{8,0},{9,25... | collective-permute-start | bytes 1032200 | tf_op jit(solution)/shard_map/ppermute | solution.py:356
  130.3 24.3 %collective-permute-start.34 = (bf16[224,512]{1,0:T(8,128)(2,1)S(1)}, bf16[224,512]{1,0:T(8,128)(2,1)S(1)}, u32[]{:S(2)}, u32[]{:S(2)}) collective-permute-start(bf16[224,512]{1,0:T(8,128)(2,1)S(1)} %err.20.refs_2_.refs_1_), channel_id=1, source_target_pairs={{0,8},{1,17},{2,10},{3,19},{4,12},{5,21},{6,14},{7,23},{8,0},{9,25... | collective-permute-start | bytes 688136 | tf_op jit(solution)/shard_map/ppermute | solution.py:356
  131.8 22.1 %collective-permute-start.35 = (bf16[224,512]{1,0:T(8,128)(2,1)S(1)}, bf16[224,512]{1,0:T(8,128)(2,1)S(1)}, u32[]{:S(2)}, u32[]{:S(2)}) collective-permute-start(bf16[224,512]{1,0:T(8,128)(2,1)S(1)} %err.21.refs_2_.refs_1_), channel_id=1, source_target_pairs={{0,8},{1,17},{2,10},{3,19},{4,12},{5,21},{6,14},{7,23},{8,0},{9,25... | collective-permute-start | bytes 688136 | tf_op jit(solution)/shard_map/ppermute | solution.py:356
  132.7 20.4 %collective-permute-start.28 = (bf16[224,768]{1,0:T(8,128)(2,1)S(1)}, bf16[224,768]{1,0:T(8,128)(2,1)S(1)}, u32[]{:S(2)}, u32[]{:S(2)}) collective-permute-start(bf16[224,768]{1,0:T(8,128)(2,1)S(1)} %pair.22.refs_3_.refs_0_), channel_id=1, source_target_pairs={{0,16},{1,9},{2,18},{3,11},{4,20},{5,13},{6,22},{7,15},{8,24},{9,1... | collective-permute-start | bytes 1032200 | tf_op jit(solution)/shard_map/ppermute | solution.py:356
  135.0 20.2 %collective-permute-start.36 = (bf16[224,768]{1,0:T(8,128)(2,1)S(1)}, bf16[224,768]{1,0:T(8,128)(2,1)S(1)}, u32[]{:S(2)}, u32[]{:S(2)}) collective-permute-start(bf16[224,768]{1,0:T(8,128)(2,1)S(1)} %pair.23.refs_3_.refs_0_), channel_id=1, source_target_pairs={{0,16},{1,9},{2,18},{3,11},{4,20},{5,13},{6,22},{7,15},{8,24},{9,1... | collective-permute-start | bytes 1032200 | tf_op jit(solution)/shard_map/ppermute | solution.py:356
  151.6 21.1 %collective-permute-start.33 = (bf16[896,512]{1,0:T(8,128)(2,1)S(1)}, bf16[896,512]{1,0:T(8,128)(2,1)S(1)}, u32[]{:S(2)}, u32[]{:S(2)}) collective-permute-start(bf16[896,512]{1,0:T(8,128)(2,1)S(1)} %get-tuple-element.65), channel_id=1, source_target_pairs={{0,8},{1,17},{2,10},{3,19},{4,12},{5,21},{6,14},{7,23},{8,0},{9,25... | collective-permute-start | bytes 2752520 | tf_op jit(solution)/shard_map/ppermute | solution.py:356
  153.2 21.2 %collective-permute-start.32 = (bf16[224,768]{1,0:T(8,128)(2,1)S(1)}, bf16[224,768]{1,0:T(8,128)(2,1)S(1)}, u32[]{:S(2)}, u32[]{:S(2)}) collective-permute-start(bf16[224,768]{1,0:T(8,128)(2,1)S(1)} %err.22.refs_3_.refs_1_), channel_id=1, source_target_pairs={{0,8},{1,17},{2,10},{3,19},{4,12},{5,21},{6,14},{7,23},{8,0},{9,25... | collective-permute-start | bytes 1032200 | tf_op jit(solution)/shard_map/ppermute | solution.py:356
  155.4 19.7 %collective-permute-start.37 = (bf16[224,768]{1,0:T(8,128)(2,1)S(1)}, bf16[224,768]{1,0:T(8,128)(2,1)S(1)}, u32[]{:S(2)}, u32[]{:S(2)}) collective-permute-start(bf16[224,768]{1,0:T(8,128)(2,1)S(1)} %err.23.refs_12_.refs_1_), channel_id=1, source_target_pairs={{0,8},{1,17},{2,10},{3,19},{4,12},{5,21},{6,14},{7,23},{8,0},{9,25... | collective-permute-start | bytes 1032200 | tf_op jit(solution)/shard_map/ppermute | solution.py:356
  172.0 20.9 %collective-permute-start.39 = (bf16[896,512]{1,0:T(8,128)(2,1)S(1)}, bf16[896,512]{1,0:T(8,128)(2,1)S(1)}, u32[]{:S(2)}, u32[]{:S(2)}) collective-permute-start(bf16[896,512]{1,0:T(8,128)(2,1)S(1)} %get-tuple-element.68), channel_id=1, source_target_pairs={{0,8},{1,17},{2,10},{3,19},{4,12},{5,21},{6,14},{7,23},{8,0},{9,25... | collective-permute-start | bytes 2752520 | tf_op jit(solution)/shard_map/ppermute | solution.py:356
  173.1 22.8 %collective-permute-start.38 = (bf16[896,512]{1,0:T(8,128)(2,1)S(1)}, bf16[896,512]{1,0:T(8,128)(2,1)S(1)}, u32[]{:S(2)}, u32[]{:S(2)}) collective-permute-start(bf16[896,512]{1,0:T(8,128)(2,1)S(1)} %pair.24.refs_3_.refs_0_), channel_id=1, source_target_pairs={{0,16},{1,9},{2,18},{3,11},{4,20},{5,13},{6,22},{7,15},{8,24},{9,1... | collective-permute-start | bytes 2752520 | tf_op jit(solution)/shard_map/ppermute | solution.py:356
  191.0 23.4 %collective-permute-start.42 = (bf16[896,512]{1,0:T(8,128)(2,1)S(1)}, bf16[896,512]{1,0:T(8,128)(2,1)S(1)}, u32[]{:S(2)}, u32[]{:S(2)}) collective-permute-start(bf16[896,512]{1,0:T(8,128)(2,1)S(1)} %get-tuple-element.72), channel_id=1, source_target_pairs={{0,8},{1,17},{2,10},{3,19},{4,12},{5,21},{6,14},{7,23},{8,0},{9,25... | collective-permute-start | bytes 2752520 | tf_op jit(solution)/shard_map/ppermute | solution.py:356
  193.3 23.9 %collective-permute-start.41 = (bf16[896,512]{1,0:T(8,128)(2,1)S(1)}, bf16[896,512]{1,0:T(8,128)(2,1)S(1)}, u32[]{:S(2)}, u32[]{:S(2)}) collective-permute-start(bf16[896,512]{1,0:T(8,128)(2,1)S(1)} %pair.25.refs_2_.refs_0_), channel_id=1, source_target_pairs={{0,16},{1,9},{2,18},{3,11},{4,20},{5,13},{6,22},{7,15},{8,24},{9,1... | collective-permute-start | bytes 2752520 | tf_op jit(solution)/shard_map/ppermute | solution.py:356
  196.4 40.6 %collective-permute-start.46 = (bf16[896,512]{1,0:T(8,128)(2,1)S(1)}, bf16[896,512]{1,0:T(8,128)(2,1)S(1)}, u32[]{:S(2)}, u32[]{:S(2)}) collective-permute-start(bf16[896,512]{1,0:T(8,128)(2,1)S(1)} %err.24.refs_12_.refs_1_), channel_id=1, source_target_pairs={{0,8},{1,17},{2,10},{3,19},{4,12},{5,21},{6,14},{7,23},{8,0},{9,25... | collective-permute-start | bytes 2752520 | tf_op jit(solution)/shard_map/ppermute | solution.py:356
  207.1 29.6 %collective-permute-start.40 = (bf16[896,256]{1,0:T(8,128)(2,1)S(1)}, bf16[896,256]{1,0:T(8,128)(2,1)S(1)}, u32[]{:S(2)}, u32[]{:S(2)}) collective-permute-start(bf16[896,256]{1,0:T(8,128)(2,1)S(1)} %get-tuple-element.71), channel_id=1, source_target_pairs={{0,8},{1,17},{2,10},{3,19},{4,12},{5,21},{6,14},{7,23},{8,0},{9,25... | collective-permute-start | bytes 1376264 | tf_op jit(solution)/shard_map/ppermute | solution.py:356
  214.7 32.3 %collective-permute-start.45 = (bf16[896,512]{1,0:T(8,128)(2,1)S(1)}, bf16[896,512]{1,0:T(8,128)(2,1)S(1)}, u32[]{:S(2)}, u32[]{:S(2)}) collective-permute-start(bf16[896,512]{1,0:T(8,128)(2,1)S(1)} %pair.26.refs_2_.refs_0_), channel_id=1, source_target_pairs={{0,16},{1,9},{2,18},{3,11},{4,20},{5,13},{6,22},{7,15},{8,24},{9,1... | collective-permute-start | bytes 2752520 | tf_op jit(solution)/shard_map/ppermute | solution.py:356
  217.6 32.6 %collective-permute-start.44 = (bf16[896,512]{1,0:T(8,128)(2,1)S(1)}, bf16[896,512]{1,0:T(8,128)(2,1)S(1)}, u32[]{:S(2)}, u32[]{:S(2)}) collective-permute-start(bf16[896,512]{1,0:T(8,128)(2,1)S(1)} %err.25.refs_2_.refs_1_), channel_id=1, source_target_pairs={{0,8},{1,17},{2,10},{3,19},{4,12},{5,21},{6,14},{7,23},{8,0},{9,25... | collective-permute-start | bytes 2752520 | tf_op jit(solution)/shard_map/ppermute | solution.py:356
  247.5 15.9 %collective-permute-start.48 = (bf16[896,512]{1,0:T(8,128)(2,1)S(1)}, bf16[896,512]{1,0:T(8,128)(2,1)S(1)}, u32[]{:S(2)}, u32[]{:S(2)}) collective-permute-start(bf16[896,512]{1,0:T(8,128)(2,1)S(1)} %err.26.refs_3_.refs_1_), channel_id=1, source_target_pairs={{0,8},{1,17},{2,10},{3,19},{4,12},{5,21},{6,14},{7,23},{8,0},{9,25... | collective-permute-start | bytes 2752520 | tf_op jit(solution)/shard_map/ppermute | solution.py:356
  248.7 13.5 %collective-permute-start.43 = (bf16[896,256]{1,0:T(8,128)(2,1)S(1)}, bf16[896,256]{1,0:T(8,128)(2,1)S(1)}, u32[]{:S(2)}, u32[]{:S(2)}) collective-permute-start(bf16[896,256]{1,0:T(8,128)(2,1)S(1)} %pair.27.refs_3_.refs_0_), channel_id=1, source_target_pairs={{0,16},{1,9},{2,18},{3,11},{4,20},{5,13},{6,22},{7,15},{8,24},{9,1... | collective-permute-start | bytes 1376264 | tf_op jit(solution)/shard_map/ppermute | solution.py:356
  (25 other events, 202.8 us)
